TPU v7x, 128 devices: a whole 4x4x4 slice. The times are simulated.
128 devices in a mesh: island: 16 (over z_lo, x, core), fsdp: 8 (over y, z_hi).
Axes of the slice: x: 4, y: 4, z: 4 (z_hi: 2, z_lo: 2; z = z_hi * 2 + z_lo), core: 2. Of those that a mesh axis runs over, the one named last changes fastest.
Arguments:
- inner: float32 [16, 4, 256, 10240], P('island', None, 'fsdp'), may hold values from -24 to 24, as said below
- anchor: float32 [4, 256, 10240], P(None, 'fsdp'), may hold values from -100 to 100, as said below
- momentum: float32 [4, 256, 10240], P(None, 'fsdp'), may hold values from -3 to 3
Outputs:
- new_anchor: float32 [4, 256, 10240], P(None, 'fsdp')
- new_momentum: float32 [4, 256, 10240], P(None, 'fsdp')
Inputs may be any that keep to these rules, and one draw needn't show every extreme that they name: `anchor`: finite values. `inner`: finite values.
All inputs are finite; a program needn't handle non-finite values.
Results may differ from a plain program's by a relative error of at most 0.00014.
Values sent between devices are 32-bit elements; how exact they have to be, the bound alone decides.
No kernel may reach another device: no remote copies, remote signals or barrier semaphores. Data moves between devices by JAX's collectives and lax.ppermute only.
A program may use at most 128 MiB of HBM per device.

v0:
```python
import jax
import jax.numpy as jnp
from jax import lax
from jax.sharding import PartitionSpec as P

EPS = 1e-06
RMS_MAX = 0.5
MU = 0.9
LR = 0.7


def apply_update(average, anchor, momentum, total_sq, entries):
    rms_value = jnp.sqrt(total_sq / entries + EPS)
    factor = jnp.minimum(1.0, RMS_MAX / rms_value)
    clipped = average * factor[:, None, None]
    new_momentum = MU * momentum + clipped
    new_anchor = anchor - LR * (clipped + MU * new_momentum)
    return (new_anchor, new_momentum)


def on_device(inner, anchor, momentum):
    islands = lax.axis_size("island")
    entries = anchor.shape[1] * lax.axis_size("fsdp") * anchor.shape[2]
    delta = anchor - inner[0]
    average = lax.psum(delta, "island") / islands
    local_sq = jnp.sum(average * average, axis=(1, 2))
    total_sq = lax.psum(local_sq, "fsdp")
    return apply_update(average, anchor, momentum, total_sq, entries)


def solution(mesh):
    placed = (P("island", None, "fsdp", None), P(None, "fsdp", None), P(None, "fsdp", None))
    return jax.shard_map(
        on_device,
        mesh=mesh,
        in_specs=placed,
        out_specs=(P(None, "fsdp", None), P(None, "fsdp", None)),
        check_vma=False,
    )
```

profile of v0, /device:TPU:0, one launch (start us, length us, event | category | flops | bytes accessed | tf_op | source)
XLA Modules:
  0.0 195.7 jit_solution(15872219506433498855)
XLA Ops:
  7.2 0.0 all-reduce.2.cloned.1.call-start
  7.2 7.1 %bitcast_subtract_fusion = f32[4,32,10240]{2,1,0:T(8,128)} fusion(f32[4,32,10240]{2,1,0:T(8,128)} %param.4, f32[1,4,32,10240]{3,2,1,0:T(8,128)} %param.3), kind=kLoop, calls=%fused_computation | loop fusion | flops 1310720 | bytes 15728640 | tf_op jit(solution)/shard_map/sub | solution.py:24
  14.3 0.0 all-reduce.2.cloned.1.call-update
  14.3 135.4 %all-reduce.2.cloned.1.call-done = f32[4,32,10240]{2,1,0:T(8,128)} async-done(((f32[4,32,10240]{2,1,0:T(8,128)}), f32[4,32,10240]{2,1,0:T(8,128)}) %all-reduce.2.cloned.1.call-update) | async-done | bytes 5242896 | tf_op jit(solution)/shard_map/psum | solution.py:25
  149.7 3.3 %multiply_reduce_fusion = f32[4]{0:T(128)S(1)} fusion(f32[4,32,10240]{2,1,0:T(8,128)} %all-reduce.2.cloned.1.call-done), kind=kLoop, calls=%fused_computation.3 | loop fusion | flops 3932156 | bytes 5242896 | tf_op jit(solution)/shard_map/reduce_sum | solution.py:26
  153.0 24.0 %psum.15 = f32[4]{0:T(128)S(1)} all-reduce(f32[4]{0:T(128)S(1)} %multiply_reduce_fusion), channel_id=1, replica_groups=mesh['island'=16,'fsdp'=8] {'fsdp'}, use_global_device_ids=true, to_apply=%region_2.0 | all-reduce | flops 4 | bytes 32 | tf_op jit(solution)/shard_map/psum | solution.py:27
  177.0 11.8 %multiply_subtract_fusion = (f32[4,32,10240]{2,1,0:T(8,128)}, f32[4,32,10240]{2,1,0:T(8,128)}) fusion(f32[4,32,10240]{2,1,0:T(8,128)} %param.4, f32[4,32,10240]{2,1,0:T(8,128)} %all-reduce.2.cloned.1.call-done, f32[4]{0:T(128)S(1)} %minimum_multiply_fusion, f32[4,32,10240]{2,1,0:T(8,128)} %param.5), kind=kLoop, calls=%fused_computation.1 | loop fusion | flops 9175040 | bytes 26214416 | tf_op jit(solution)/shard_map/sub | solution.py:17
  (1 shorter events, 0.0 us)
Async XLA Ops:
  7.2 142.6 %all-reduce.2.cloned.1.call-start = ((), (), s32[]{:S(2)}) async-start(), calls=%async_computation | async-start | bytes 10485760 | tf_op jit(solution)/shard_map/psum | solution.py:25
Sparse Core Ops, SparseCore 0:
  14.4 135.2 all-reduce.1
where the time goes:
time: 196 us
  waiting for transfers between devices  135 us (69%)
  blocking collectives  24 us (12%)
  other arithmetic  22.2 us (11%)
  between operations  14 us (7%)
    psum x1, waiting for transfers between devices, on_device(): average = lax.psum(delta, 'island') / islands  135 us
    psum x1, blocking collectives, on_device(): total_sq = lax.psum(local_sq, 'fsdp')  24 us
    sub x1, other arithmetic, apply_update(): new_anchor = anchor - LR * (clipped + MU * new_momentum)  11.8 us
    sub x1, other arithmetic, on_device(): delta = anchor - inner[0]  7.06 us
  transfers between devices with their start and end apart: 1, of which 1 were waited for; matrix products, arithmetic and copies ran while one was open for 0% of the time, Pallas kernels for 0%

commit v1 on v0

v1 whole, which is shorter than its diff:
```python
import jax
import jax.numpy as jnp
from jax import lax
from jax.sharding import PartitionSpec as P
from jax.experimental import pallas as pl
from jax.experimental.pallas import tpu as pltpu

EPS = 1e-06
RMS_MAX = 0.5
MU = 0.9
LR = 0.7
X, CORES = 4, 2


def island_id(z, x, core):
    return ((z % 2) * X + x % X) * CORES + core % CORES


def neighbour(x, core, parity):
    return x + 1 if (x + core + parity) % 2 == 0 else x - 1


PLACES = [(z, x, core) for z in range(2) for x in range(X) for core in range(CORES)]
CORE = [(island_id(*p), island_id(p[0], p[1], p[2] + 1)) for p in PLACES]
Z = [(island_id(*p), island_id(p[0] + 1, p[1], p[2])) for p in PLACES]
X0 = [(island_id(*p), island_id(p[0], neighbour(p[1], p[2], 0), p[2])) for p in PLACES]
X1 = [(island_id(*p), island_id(p[0], neighbour(p[1], p[2], 1), p[2])) for p in PLACES]
YZ = [(y, h) for y in range(4) for h in range(2)]
Y0 = [(y * 2 + h, (y ^ 1) * 2 + h) for y, h in YZ]
Y1 = [(y * 2 + h, ((y + (1 if y % 2 else -1)) % 4) * 2 + h) for y, h in YZ]
H = [(y * 2 + h, y * 2 + (1 - h)) for y, h in YZ]


def hop(value, pairs, axis="island"):
    return lax.ppermute(value, axis, pairs)


def update_kernel(cols, first, ids, scale, *refs):
    n = len(cols)
    sums = refs[:n]
    anchor, momentum = refs[n : n + 2]
    k = n + 2 + (0 if first else 2)
    out_a, out_m = refs[k : k + 2]
    va, vm = refs[k + 2 : k + 2 + n], refs[k + 2 + n : k + 2 + 2 * n]
    sem_in, sem_out = refs[k + 2 + 2 * n :]

    def place(ref, i):
        start, width = cols[i]
        return ref.at[ids[i], :, pl.ds(start, width)]

    loads, stores = [], []
    for i in range(n):
        loads.append(
            (
                pltpu.make_async_copy(place(anchor, i), va[i], sem_in.at[0, i]),
                pltpu.make_async_copy(place(momentum, i), vm[i], sem_in.at[1, i]),
            )
        )
        for copy in loads[-1]:
            copy.start()
    for i in range(n):
        for copy in loads[i]:
            copy.wait()
        factor = scale[ids[i]]
        clipped = sums[i][...] * factor
        new_m = MU * vm[i][...] + clipped
        va[i][...] = va[i][...] - LR * (clipped + MU * new_m)
        vm[i][...] = new_m
        out = (
            pltpu.make_async_copy(va[i], place(out_a, i), sem_out.at[0, i]),
            pltpu.make_async_copy(vm[i], place(out_m, i), sem_out.at[1, i]),
        )
        for copy in out:
            copy.start()
        stores.extend(out)
    for copy in stores:
        copy.wait()


def update(pieces, cols, ids, scale, anchor, momentum, outs=None):
    n = len(pieces)
    first = outs is None
    shape = jax.ShapeDtypeStruct(anchor.shape, anchor.dtype)
    any_spec = pl.BlockSpec(memory_space=pl.ANY)
    smem = pl.BlockSpec(memory_space=pltpu.SMEM)
    scratch = [pltpu.VMEM((32, w), jnp.float32) for _, w in cols] * 2
    total = sum(w for _, w in cols) * 32 * 4
    return pl.pallas_call(
        lambda *refs: update_kernel(cols, first, *refs),
        out_shape=(shape, shape),
        in_specs=[smem, smem]
        + [pl.BlockSpec(memory_space=pltpu.VMEM)] * n
        + [any_spec] * (2 if first else 4),
        out_specs=(any_spec, any_spec),
        scratch_shapes=scratch
        + [pltpu.SemaphoreType.DMA((2, n)), pltpu.SemaphoreType.DMA((2, n))],
        input_output_aliases={} if first else {n + 4: 0, n + 5: 1},
        compiler_params=pltpu.CompilerParams(vmem_limit_bytes=5 * total + (4 << 20)),
        cost_estimate=pl.CostEstimate(
            flops=2 * total, bytes_accessed=5 * total, transcendentals=0
        ),
    )(ids, scale, *pieces, anchor, momentum, *(() if first else outs))


WA, WB = 3456, 3456


def on_device(inner, anchor, momentum):
    inner = inner[0]
    rows, width = anchor.shape[1:]
    islands = lax.axis_size("island")
    entries = rows * lax.axis_size("fsdp") * width
    me = lax.axis_index("island")
    core, x, z = me % 2, (me // 2) % X, me // 8
    bit = ((x + 1 - core) // 2) % 2
    peer_bit = ((x + core) // 2) % 2
    a_cols, b_cols, c_cols = (0, WA), (WA, WB), (WA + WB, width - WA - WB)
    bc_cols = (WA, width - WA)

    def cut(array, frag, cols):
        return lax.dynamic_slice(array, (frag, 0, cols[0]), (1, rows, cols[1]))[0]

    own, other = 2 * core, 2 * (1 - core)
    got_a_out = hop(cut(inner, other + 1 - z, a_cols), CORE)
    got_bc_out = hop(cut(inner, other + 1 - peer_bit, bc_cols), CORE)
    got_a_in = hop(cut(inner, other + z, a_cols), CORE)
    got_bc_in = hop(cut(inner, other + peer_bit, bc_cols), CORE)

    def delta(got, frag, cols):
        base = cut(anchor, frag, cols)
        return (base - cut(inner, frag, cols)) + (base - got)

    a_r = hop(delta(got_a_out, own + 1 - z, a_cols), Z)
    bc_r = hop(delta(got_bc_out, own + 1 - bit, bc_cols), X0)
    a = delta(got_a_in, own + z, a_cols) + a_r
    bc = delta(got_bc_in, own + bit, bc_cols) + bc_r
    b, c = bc[:, :WB], bc[:, WB:]
    a_r, b_r, c_r = hop(a, X1), hop(b, X1), hop(c, Z)
    a, b, c = a + a_r, b + b_r, c + c_r
    a_r, b_r, c_r = hop(a, X0), hop(b, Z), hop(c, X1)
    a, bc = a + a_r, jnp.concatenate([b + b_r, c + c_r], axis=1)
    a_far, bc_far = hop(a, Z), hop(bc, X0)
    a_peer, bc_peer = hop(a, CORE), hop(bc, CORE)
    a_peer_far, bc_peer_far = hop(a_far, CORE), hop(bc_far, CORE)
    frag = jnp.arange(4)
    sq = jnp.where(frag == own + z, jnp.sum(a * a), 0.0)
    sq = sq + jnp.where(frag == own + bit, jnp.sum(bc * bc), 0.0)
    sq = jnp.broadcast_to(jnp.pad(sq, (0, 4))[:, None], (8, 128))
    for pairs, axis in ((X0, "island"), (Z, "island"), (CORE, "island"), (Y0, "fsdp"), (Y1, "fsdp"), (H, "fsdp")):
        sq = sq + hop(sq, pairs, axis)
    mean_sq = sq[:4, 0] * (0.5 / (islands * islands)) / entries
    factor = jnp.minimum(1.0, RMS_MAX / jnp.sqrt(mean_sq + EPS)) / islands
    cols = [a_cols, bc_cols, a_cols, bc_cols]
    near = jnp.stack([own + z, own + bit, other + z, other + peer_bit])
    far = jnp.stack([own + 1 - z, own + 1 - bit, other + 1 - z, other + 1 - peer_bit])
    outs = update([a, bc, a_peer, bc_peer], cols, near, factor, anchor, momentum)
    return tuple(
        update([a_far, bc_far, a_peer_far, bc_peer_far], cols, far, factor, anchor, momentum, outs)
    )


def solution(mesh):
    spec = P(None, "fsdp", None)
    return jax.shard_map(
        on_device,
        mesh=mesh,
        in_specs=(P("island", None, "fsdp", None), spec, spec),
        out_specs=(spec, spec),
        check_vma=False,
    )
```

time: 196 us -> 115 us (0.59)
  waiting for transfers between devices: 135 us -> 58.9 us
  starting transfers between devices: 0.04 us -> 33 us
  blocking collectives: 24 us -> 0 us
  between operations: 14 us -> 0.9 us
  other arithmetic: 22.2 us -> 10.3 us
  Pallas kernels: 0 us -> 7.58 us
  local copies, waits for them, and re-layouts: 0 us -> 3.85 us
    psum x1 -> x0, waiting for transfers between devices: 135 us -> none  [on_device(): average = lax.psum(delta, 'island') / islands]
    ppermute x0 -> x24, waiting for transfers between devices: none -> 58.9 us  [hop(): return lax.ppermute(value, axis, pairs)]
    ppermute x0 -> x24, starting transfers between devices: none -> 33 us  [hop(): return lax.ppermute(value, axis, pairs)]
    psum x1 -> x0, blocking collectives: 24 us -> none  [on_device(): total_sq = lax.psum(local_sq, 'fsdp')]
    sub x2 -> x0, other arithmetic: 18.9 us -> none  [the longest x1 11.8 us: apply_update(): new_anchor = anchor - LR * (clipped + MU * new_momentum)]
    add x0 -> x15, other arithmetic: none -> 8.56 us  [the longest x2 4.06 us: delta(): return base - cut(inner, frag, cols) + (base - got)]
    pallas_call x0 -> x2, Pallas kernels: none -> 7.58 us  [update(): pl.pallas_call(lambda *refs: update_kernel(cols, first, *refs), out_shape...]
    squeeze x0 -> x2, local copies, waits for them, and re-layouts: none -> 3.76 us  [cut(): return lax.dynamic_slice(array, (frag, 0, cols[0]), (1, rows, cols[1]))[0]]
  transfers between devices with their start and end apart: 1 -> 24, of which waited for: 1 -> 13; matrix products, arithmetic and copies ran while one was open for 0% -> 11% of each run, Pallas kernels for 0% -> 3%
where the time goes in v1:
time: 115 us; the launch traced here: 114 us
  waiting for transfers between devices  58.9 us (51%)
  starting transfers between devices  33 us (29%)
  other arithmetic  10.3 us (9%)
  Pallas kernels  7.58 us (7%)
  local copies, waits for them, and re-layouts  3.85 us (3%)
    ppermute x24, waiting for transfers between devices, hop(): return lax.ppermute(value, axis, pairs)  58.9 us
    ppermute x24, starting transfers between devices, hop(): return lax.ppermute(value, axis, pairs)  33 us
    pallas_call x2, Pallas kernels, update(): pl.pallas_call(lambda *refs: update_kernel(cols, first, *refs), out_shape...  7.58 us
    add x2, other arithmetic, delta(): return base - cut(inner, frag, cols) + (base - got)  4.06 us
    squeeze x2, local copies, waits for them, and re-layouts, cut(): return lax.dynamic_slice(array, (frag, 0, cols[0]), (1, rows, cols[1]))[0]  3.76 us
  transfers between devices with their start and end apart: 24, of which 13 were waited for; matrix products, arithmetic and copies ran while one was open for 11% of the time, Pallas kernels for 3%

profile of v1, /device:TPU:0, one launch (start us, length us, event | category | flops | bytes accessed | tf_op | source)
XLA Modules:
  0.0 114.5 jit_solution(12622558446185988652)
XLA Ops:
  0.7 1.5 %dynamic-slice_bitcast_fusion.1 = (f32[32,6784]{1,0:T(8,128)S(1)}, f32[32,6784]{1,0:T(8,128)S(1)}) fusion(f32[1,4,32,10240]{3,2,1,0:T(8,128)} %param.3, s32[]{:T(128)S(6)} %select_n.81, s32[]{:T(128)S(6)} %select_n.83), kind=kLoop, calls=%fused_computation.10 | loop fusion | bytes 3473416 | tf_op jit(solution)/shard_map/squeeze | solution.py:121
  2.9 2.3 %collective-permute-done.6 = f32[32,6784]{1,0:T(8,128)} collective-permute-done((f32[32,6784]{1,0:T(8,128)S(1)}, f32[32,6784]{1,0:T(8,128)}, u32[]{:S(2)}, u32[]{:S(2)}) %collective-permute-start.6) | collective-permute-done | bytes 868384 | tf_op jit(solution)/shard_map/ppermute | solution.py:35
  5.2 2.7 %fusion = f32[32,6784]{1,0:T(8,128)} fusion(f32[32,6784]{1,0:T(8,128)} %collective-permute-done.6, f32[1,4,32,10240]{3,2,1,0:T(8,128)} %param.3, s32[]{:T(128)S(6)} %select_n.82, f32[4,32,10240]{2,1,0:T(8,128)} %refs_6_.3), kind=kLoop, calls=%fused_computation.2 | loop fusion | flops 651264 | bytes 3473412 | tf_op jit(solution)/shard_map/add | solution.py:131
  7.9 1.6 %collective-permute-start.7 = (f32[32,6784]{1,0:T(8,128)}, f32[32,6784]{1,0:T(8,128)}, u32[]{:S(2)}, u32[]{:S(2)}) collective-permute-start(f32[32,6784]{1,0:T(8,128)} %fusion), channel_id=1, source_target_pairs={{0,16},{8,56},{16,0},{24,40},{32,48},{40,24},{48,32},{56,8},{64,80... | collective-permute-start | bytes 2605064 | tf_op jit(solution)/shard_map/ppermute | solution.py:35
  9.5 2.2 %dynamic-slice_bitcast_fusion.3 = (f32[32,3456]{1,0:T(8,128)}, f32[32,3456]{1,0:T(8,128)}) fusion(f32[1,4,32,10240]{3,2,1,0:T(8,128)} %param.3, s32[]{:T(128)S(6)} %select_n.76, s32[]{:T(128)S(6)} %select_n.78), kind=kLoop, calls=%fused_computation.20 | loop fusion | bytes 1769480 | tf_op jit(solution)/shard_map/squeeze | solution.py:121
  11.7 1.1 collective-permute-start
  12.8 8.2 %collective-permute-done.7 = f32[32,6784]{1,0:T(8,128)} collective-permute-done((f32[32,6784]{1,0:T(8,128)}, f32[32,6784]{1,0:T(8,128)}, u32[]{:S(2)}, u32[]{:S(2)}) %collective-permute-start.7) | collective-permute-done | bytes 868384 | tf_op jit(solution)/shard_map/ppermute | solution.py:35
  21.1 1.8 %fusion.2 = f32[32,6784]{1,0:T(8,128)S(1)} fusion(f32[32,6784]{1,0:T(8,128)} %collective-permute-done.7, f32[32,6784]{1,0:T(8,128)S(1)} %collective-permute-done.5, f32[1,4,32,10240]{3,2,1,0:T(8,128)} %param.3, s32[]{:T(128)S(6)} %select_n.80, f32[4,32,10240]{2,1,0:T(8,128)} %refs_6_.3), kind=kLoop, calls=%fused_computation.6 | loop fusion | flops 868352 | bytes 4341764 | tf_op jit(solution)/shard_map/add | solution.py:136
  23.0 2.1 %collective-permute-start.10 = (f32[32,3328]{1,0:T(8,128)S(1)}, f32[32,3328]{1,0:T(8,128)S(1)}, u32[]{:S(2)}, u32[]{:S(2)}) collective-permute-start(f32[32,3328]{1,0:T(8,128)S(1)} %slice.13), channel_id=1, source_target_pairs={{0,64},{8,72},{16,80},{24,88},{32,96},{40,104},{48,112},{56,120},{... | collective-permute-start | bytes 1277960 | tf_op jit(solution)/shard_map/ppermute | solution.py:35
  25.0 1.3 %fusion.3 = f32[32,3456]{1,0:T(8,128)S(1)} fusion(f32[32,3456]{1,0:T(8,128)} %collective-permute-done.1, f32[1,4,32,10240]{3,2,1,0:T(8,128)} %param.3, s32[]{:T(128)S(6)} %select_n.77, f32[4,32,10240]{2,1,0:T(8,128)} %refs_6_.3), kind=kLoop, calls=%fused_computation.12 | loop fusion | flops 331776 | bytes 1769476 | tf_op jit(solution)/shard_map/add | solution.py:131
  26.5 2.9 %collective-permute-start.8 = (f32[32,3456]{1,0:T(8,128)S(1)}, f32[32,3456]{1,0:T(8,128)S(1)}, u32[]{:S(2)}, u32[]{:S(2)}) collective-permute-start(f32[32,3456]{1,0:T(8,128)S(1)} %slice.12), channel_id=1, source_target_pairs={{0,48},{8,24},{16,32},{24,8},{32,16},{40,56},{48,0},{56,40},{64,11... | collective-permute-start | bytes 1327112 | tf_op jit(solution)/shard_map/ppermute | solution.py:35
  29.4 6.2 %collective-permute-done.10 = f32[32,3328]{1,0:T(8,128)S(1)} collective-permute-done((f32[32,3328]{1,0:T(8,128)S(1)}, f32[32,3328]{1,0:T(8,128)S(1)}, u32[]{:S(2)}, u32[]{:S(2)}) %collective-permute-start.10) | collective-permute-done | bytes 426016 | tf_op jit(solution)/shard_map/ppermute | solution.py:35
  35.7 2.9 %collective-permute-start.11 = (f32[32,3328]{1,0:T(8,128)S(1)}, f32[32,3328]{1,0:T(8,128)S(1)}, u32[]{:S(2)}, u32[]{:S(2)}) collective-permute-start(f32[32,3328]{1,0:T(8,128)S(1)} %slice_add_fusion.1), channel_id=1, source_target_pairs={{0,48},{8,24},{16,32},{24,8},{32,16},{40,56},{48,0},{56,40},{64,11... | collective-permute-start | bytes 1277960 | tf_op jit(solution)/shard_map/ppermute | solution.py:35
  38.7 2.0 %collective-permute-start.9 = (f32[32,3456]{1,0:T(8,128)S(1)}, f32[32,3456]{1,0:T(8,128)S(1)}, u32[]{:S(2)}, u32[]{:S(2)}) collective-permute-start(f32[32,3456]{1,0:T(8,128)S(1)} %slice_add_fusion.2), channel_id=1, source_target_pairs={{0,64},{8,72},{16,80},{24,88},{32,96},{40,104},{48,112},{56,120},{... | collective-permute-start | bytes 1327112 | tf_op jit(solution)/shard_map/ppermute | solution.py:35
  40.7 4.4 %collective-permute-done.2 = f32[32,3456]{1,0:T(8,128)S(1)} collective-permute-done((f32[32,3456]{1,0:T(8,128)S(1)}, f32[32,3456]{1,0:T(8,128)S(1)}, u32[]{:S(2)}, u32[]{:S(2)}) %collective-permute-start.2) | collective-permute-done | bytes 442400 | tf_op jit(solution)/shard_map/ppermute | solution.py:35
  45.1 1.1 fusion.5
  46.2 2.9 %collective-permute-start.3 = (f32[32,3456]{1,0:T(8,128)S(1)}, f32[32,3456]{1,0:T(8,128)S(1)}, u32[]{:S(2)}, u32[]{:S(2)}) collective-permute-start(f32[32,3456]{1,0:T(8,128)S(1)} %fusion.5), channel_id=1, source_target_pairs={{0,48},{8,24},{16,32},{24,8},{32,16},{40,56},{48,0},{56,40},{64,11... | collective-permute-start | bytes 1327112 | tf_op jit(solution)/shard_map/ppermute | solution.py:35
  49.2 4.9 %collective-permute-done.9 = f32[32,3456]{1,0:T(8,128)S(1)} collective-permute-done((f32[32,3456]{1,0:T(8,128)S(1)}, f32[32,3456]{1,0:T(8,128)S(1)}, u32[]{:S(2)}, u32[]{:S(2)}) %collective-permute-start.9) | collective-permute-done | bytes 442400 | tf_op jit(solution)/shard_map/ppermute | solution.py:35
  55.9 1.3 %collective-permute-start.4 = (f32[32,3456]{1,0:T(8,128)S(1)}, f32[32,3456]{1,0:T(8,128)S(1)}, u32[]{:S(2)}, u32[]{:S(2)}) collective-permute-start(f32[32,3456]{1,0:T(8,128)S(1)} %add.161), channel_id=1, source_target_pairs={{0,16},{8,56},{16,0},{24,40},{32,48},{40,24},{48,32},{56,8},{64,80... | collective-permute-start | bytes 1327112 | tf_op jit(solution)/shard_map/ppermute | solution.py:35
  57.2 15.4 %collective-permute-done.4 = f32[32,3456]{1,0:T(8,128)S(1)} collective-permute-done((f32[32,3456]{1,0:T(8,128)S(1)}, f32[32,3456]{1,0:T(8,128)S(1)}, u32[]{:S(2)}, u32[]{:S(2)}) %collective-permute-start.4) | collective-permute-done | bytes 442400 | tf_op jit(solution)/shard_map/ppermute | solution.py:35
  73.4 1.3 %fusion.6 = f32[4]{0:T(128)S(1)} fusion(f32[]{:T(128)} %get-tuple-element.13, s32[]{:T(128)} %add.163, f32[]{:T(128)} %get-tuple-element.6, s32[]{:T(128)} %add.152), kind=kLoop, calls=%fused_computation.24 | loop fusion | flops 20 | bytes 32 | tf_op jit(solution)/shard_map/add | solution.py:147
  75.4 1.7 %collective-permute-start.18 = (f32[32,3456]{1,0:T(8,128)S(1)}, f32[32,3456]{1,0:T(8,128)S(1)}, u32[]{:S(2)}, u32[]{:S(2)}) collective-permute-start(f32[32,3456]{1,0:T(8,128)S(1)} %get-tuple-element.7.refs_2_), channel_id=1, source_target_pairs={{0,64},{8,72},{16,80},{24,88},{32,96},{40,104},{48,112},{56,120},{... | collective-permute-start | bytes 1327112 | tf_op jit(solution)/shard_map/ppermute | solution.py:35
  79.1 1.8 %collective-permute-start.13 = (f32[8,128]{0,1:T(8,128)S(1)}, f32[8,128]{0,1:T(8,128)S(1)}, u32[]{:S(2)}, u32[]{:S(2)}) collective-permute-start(f32[8,128]{0,1:T(8,128)S(1)} %broadcast_add_fusion), channel_id=1, source_target_pairs={{0,64},{8,72},{16,80},{24,88},{32,96},{40,104},{48,112},{56,120},{... | collective-permute-start | bytes 12296 | tf_op jit(solution)/shard_map/ppermute | solution.py:35
  80.9 8.4 %collective-permute-done.13 = f32[8,128]{0,1:T(8,128)S(1)} collective-permute-done((f32[8,128]{0,1:T(8,128)S(1)}, f32[8,128]{0,1:T(8,128)S(1)}, u32[]{:S(2)}, u32[]{:S(2)}) %collective-permute-start.13) | collective-permute-done | bytes 4128 | tf_op jit(solution)/shard_map/ppermute | solution.py:35
  90.6 1.7 %collective-permute-start.15 = (f32[8,128]{0,1:T(8,128)S(1)}, f32[8,128]{0,1:T(8,128)S(1)}, u32[]{:S(2)}, u32[]{:S(2)}) collective-permute-start(f32[8,128]{0,1:T(8,128)S(1)} %add.179), channel_id=1, source_target_pairs={{0,2},{1,3},{2,0},{3,1},{4,6},{5,7},{6,4},{7,5},{8,10},{9,11},{10,... | collective-permute-start | bytes 12296 | tf_op jit(solution)/shard_map/ppermute | solution.py:35
  92.8 2.2 %collective-permute-done.15 = f32[8,128]{0,1:T(8,128)S(1)} collective-permute-done((f32[8,128]{0,1:T(8,128)S(1)}, f32[8,128]{0,1:T(8,128)S(1)}, u32[]{:S(2)}, u32[]{:S(2)}) %collective-permute-start.15) | collective-permute-done | bytes 4128 | tf_op jit(solution)/shard_map/ppermute | solution.py:35
  95.1 3.1 %collective-permute-start.16 = (f32[8,128]{0,1:T(8,128)S(1)}, f32[8,128]{0,1:T(8,128)S(1)}, u32[]{:S(2)}, u32[]{:S(2)}) collective-permute-start(f32[8,128]{0,1:T(8,128)S(1)} %add.180), channel_id=1, source_target_pairs={{0,6},{1,7},{2,4},{3,5},{4,2},{5,3},{6,0},{7,1},{8,14},{9,15},{10,... | collective-permute-start | bytes 12296 | tf_op jit(solution)/shard_map/ppermute | solution.py:35
  98.2 2.4 %collective-permute-done.16 = f32[8,128]{0,1:T(8,128)S(1)} collective-permute-done((f32[8,128]{0,1:T(8,128)S(1)}, f32[8,128]{0,1:T(8,128)S(1)}, u32[]{:S(2)}, u32[]{:S(2)}) %collective-permute-start.16) | collective-permute-done | bytes 4128 | tf_op jit(solution)/shard_map/ppermute | solution.py:35
  100.6 3.9 %collective-permute-start.17 = (f32[8,128]{0,1:T(8,128)S(1)}, f32[8,128]{0,1:T(8,128)S(1)}, u32[]{:S(2)}, u32[]{:S(2)}) collective-permute-start(f32[8,128]{0,1:T(8,128)S(1)} %add.181), channel_id=1, source_target_pairs={{0,1},{1,0},{2,3},{3,2},{4,5},{5,4},{6,7},{7,6},{8,9},{9,8},{10,11... | collective-permute-start | bytes 12296 | tf_op jit(solution)/shard_map/ppermute | solution.py:35
  104.7 2.2 %collective-permute-done.17 = f32[8,128]{0,1:T(8,128)S(1)} collective-permute-done((f32[8,128]{0,1:T(8,128)S(1)}, f32[8,128]{0,1:T(8,128)S(1)}, u32[]{:S(2)}, u32[]{:S(2)}) %collective-permute-start.17) | collective-permute-done | bytes 4128 | tf_op jit(solution)/shard_map/ppermute | solution.py:35
  106.9 3.8 %shard_map.50 = (f32[4,32,10240]{2,1,0:T(8,128)}, f32[4,32,10240]{2,1,0:T(8,128)}) custom-call(s32[4]{0:T(128)S(1)} %pad_add_fusion.1.refs_0_, f32[4]{0:T(128)S(1)} %multiply_bitcast_fusion.refs_1_, f32[32,3456]{1,0:T(8,128)S(1)} %get-tuple-element.7.refs_2_, f32[32,6784]{1,0:T(8,128)S(1)} %get-tuple-element.12.refs_3_, ...), custom_call_target="tpu_custom_call" | custom-call | flops 5242880 | bytes 13107200 | tf_op jit(solution)/shard_map/pallas_call | solution.py:88
  110.7 3.8 %shard_map.51 = (f32[4,32,10240]{2,1,0:T(8,128)}, f32[4,32,10240]{2,1,0:T(8,128)}) custom-call(s32[4]{0:T(128)S(1)} %pad_add_fusion.refs_0_, f32[4]{0:T(128)S(1)} %multiply_bitcast_fusion.refs_1_, f32[32,3456]{1,0:T(8,128)S(1)} %collective-permute-done.18.refs_2_, ...), custom_call_target="tpu_custom_call", output_to_operand_aliasing={{0}: (8, {}), {1}: (9, {})} | custom-call | flops 5242880 | bytes 13107200 | tf_op jit(solution)/shard_map/pallas_call | solution.py:88
  (54 shorter events, 8.0 us)
Async XLA Ops:
  2.3 2.9 %collective-permute-start.6 = (f32[32,6784]{1,0:T(8,128)S(1)}, f32[32,6784]{1,0:T(8,128)}, u32[]{:S(2)}, u32[]{:S(2)}) collective-permute-start(f32[32,6784]{1,0:T(8,128)S(1)} %get-tuple-element.11), channel_id=1, source_target_pairs={{0,8},{8,0},{16,24},{24,16},{32,40},{40,32},{48,56},{56,48},{64,72... | collective-permute-start | bytes 2605064 | tf_op jit(solution)/shard_map/ppermute | solution.py:35
  2.4 10.5 %collective-permute-start.5 = (f32[32,6784]{1,0:T(8,128)S(1)}, f32[32,6784]{1,0:T(8,128)S(1)}, u32[]{:S(2)}, u32[]{:S(2)}) collective-permute-start(f32[32,6784]{1,0:T(8,128)S(1)} %get-tuple-element.10), channel_id=1, source_target_pairs={{0,8},{8,0},{16,24},{24,16},{32,40},{40,32},{48,56},{56,48},{64,72... | collective-permute-start | bytes 2605064 | tf_op jit(solution)/shard_map/ppermute | solution.py:35
  7.9 13.2 %collective-permute-start.7 = (f32[32,6784]{1,0:T(8,128)}, f32[32,6784]{1,0:T(8,128)}, u32[]{:S(2)}, u32[]{:S(2)}) collective-permute-start(f32[32,6784]{1,0:T(8,128)} %fusion), channel_id=1, source_target_pairs={{0,16},{8,56},{16,0},{24,40},{32,48},{40,24},{48,32},{56,8},{64,80... | collective-permute-start | bytes 2605064 | tf_op jit(solution)/shard_map/ppermute | solution.py:35
  9.5 35.7 %slice-start = ((s8[5242880]{0:T(1024)(128)(4,1)}), s8[1048576]{0:T(1024)(128)(4,1)S(1)}, s32[]{:S(2)}) async-start(s8[5242880]{0:T(1024)(128)(4,1)} %bitcast.58), calls=%async_computation | async-start | bytes 2097152
  11.7 29.0 %collective-permute-start = (f32[32,3456]{1,0:T(8,128)}, f32[32,3456]{1,0:T(8,128)S(1)}, u32[]{:S(2)}, u32[]{:S(2)}) collective-permute-start(f32[32,3456]{1,0:T(8,128)} %get-tuple-element.8), channel_id=1, source_target_pairs={{0,8},{8,0},{16,24},{24,16},{32,40},{40,32},{48,56},{56,48},{64,72... | collective-permute-start | bytes 1327112 | tf_op jit(solution)/shard_map/ppermute | solution.py:35
  12.8 12.2 %collective-permute-start.1 = (f32[32,3456]{1,0:T(8,128)}, f32[32,3456]{1,0:T(8,128)}, u32[]{:S(2)}, u32[]{:S(2)}) collective-permute-start(f32[32,3456]{1,0:T(8,128)} %get-tuple-element.9), channel_id=1, source_target_pairs={{0,8},{8,0},{16,24},{24,16},{32,40},{40,32},{48,56},{56,48},{64,72... | collective-permute-start | bytes 1327112 | tf_op jit(solution)/shard_map/ppermute | solution.py:35
  12.8 32.3 %slice-start.1 = ((s8[5242880]{0:T(1024)(128)(4,1)}), s8[4194304]{0:T(1024)(128)(4,1)S(1)}, s32[]{:S(2)}) async-start(s8[5242880]{0:T(1024)(128)(4,1)} %bitcast.58), calls=%async_computation.1 | async-start | bytes 8388608
  23.0 12.7 %collective-permute-start.10 = (f32[32,3328]{1,0:T(8,128)S(1)}, f32[32,3328]{1,0:T(8,128)S(1)}, u32[]{:S(2)}, u32[]{:S(2)}) collective-permute-start(f32[32,3328]{1,0:T(8,128)S(1)} %slice.13), channel_id=1, source_target_pairs={{0,64},{8,72},{16,80},{24,88},{32,96},{40,104},{48,112},{56,120},{... | collective-permute-start | bytes 1277960 | tf_op jit(solution)/shard_map/ppermute | solution.py:35
  26.4 18.7 %collective-permute-start.2 = (f32[32,3456]{1,0:T(8,128)S(1)}, f32[32,3456]{1,0:T(8,128)S(1)}, u32[]{:S(2)}, u32[]{:S(2)}) collective-permute-start(f32[32,3456]{1,0:T(8,128)S(1)} %fusion.3), channel_id=1, source_target_pairs={{0,64},{8,72},{16,80},{24,88},{32,96},{40,104},{48,112},{56,120},{... | collective-permute-start | bytes 1327112 | tf_op jit(solution)/shard_map/ppermute | solution.py:35
  26.5 80.4 %slice-start.2 = ((s8[5242880]{0:T(1024)(128)(4,1)}), s8[4194304]{0:T(1024)(128)(4,1)S(1)}, s32[]{:S(2)}) async-start(s8[5242880]{0:T(1024)(128)(4,1)} %bitcast.60), calls=%async_computation.2 | async-start | bytes 8388608
  26.5 12.1 %collective-permute-start.8 = (f32[32,3456]{1,0:T(8,128)S(1)}, f32[32,3456]{1,0:T(8,128)S(1)}, u32[]{:S(2)}, u32[]{:S(2)}) collective-permute-start(f32[32,3456]{1,0:T(8,128)S(1)} %slice.12), channel_id=1, source_target_pairs={{0,48},{8,24},{16,32},{24,8},{32,16},{40,56},{48,0},{56,40},{64,11... | collective-permute-start | bytes 1327112 | tf_op jit(solution)/shard_map/ppermute | solution.py:35
  35.7 13.5 %collective-permute-start.11 = (f32[32,3328]{1,0:T(8,128)S(1)}, f32[32,3328]{1,0:T(8,128)S(1)}, u32[]{:S(2)}, u32[]{:S(2)}) collective-permute-start(f32[32,3328]{1,0:T(8,128)S(1)} %slice_add_fusion.1), channel_id=1, source_target_pairs={{0,48},{8,24},{16,32},{24,8},{32,16},{40,56},{48,0},{56,40},{64,11... | collective-permute-start | bytes 1277960 | tf_op jit(solution)/shard_map/ppermute | solution.py:35
  38.7 15.5 %collective-permute-start.9 = (f32[32,3456]{1,0:T(8,128)S(1)}, f32[32,3456]{1,0:T(8,128)S(1)}, u32[]{:S(2)}, u32[]{:S(2)}) collective-permute-start(f32[32,3456]{1,0:T(8,128)S(1)} %slice_add_fusion.2), channel_id=1, source_target_pairs={{0,64},{8,72},{16,80},{24,88},{32,96},{40,104},{48,112},{56,120},{... | collective-permute-start | bytes 1327112 | tf_op jit(solution)/shard_map/ppermute | solution.py:35
  46.2 60.6 %slice-start.3 = ((s8[5242880]{0:T(1024)(128)(4,1)}), s8[1048576]{0:T(1024)(128)(4,1)S(1)}, s32[]{:S(2)}) async-start(s8[5242880]{0:T(1024)(128)(4,1)} %bitcast.60), calls=%async_computation.3 | async-start | bytes 2097152
  46.2 9.6 %collective-permute-start.3 = (f32[32,3456]{1,0:T(8,128)S(1)}, f32[32,3456]{1,0:T(8,128)S(1)}, u32[]{:S(2)}, u32[]{:S(2)}) collective-permute-start(f32[32,3456]{1,0:T(8,128)S(1)} %fusion.5), channel_id=1, source_target_pairs={{0,48},{8,24},{16,32},{24,8},{32,16},{40,56},{48,0},{56,40},{64,11... | collective-permute-start | bytes 1327112 | tf_op jit(solution)/shard_map/ppermute | solution.py:35
  55.0 23.1 %collective-permute-start.19 = (f32[32,6784]{1,0:T(8,128)S(1)}, f32[32,6784]{1,0:T(8,128)S(1)}, u32[]{:S(2)}, u32[]{:S(2)}) collective-permute-start(f32[32,6784]{1,0:T(8,128)S(1)} %get-tuple-element.12.refs_3_), channel_id=1, source_target_pairs={{0,16},{8,56},{16,0},{24,40},{32,48},{40,24},{48,32},{56,8},{64,80... | collective-permute-start | bytes 2605064 | tf_op jit(solution)/shard_map/ppermute | solution.py:35
  55.9 16.8 %collective-permute-start.4 = (f32[32,3456]{1,0:T(8,128)S(1)}, f32[32,3456]{1,0:T(8,128)S(1)}, u32[]{:S(2)}, u32[]{:S(2)}) collective-permute-start(f32[32,3456]{1,0:T(8,128)S(1)} %add.161), channel_id=1, source_target_pairs={{0,16},{8,56},{16,0},{24,40},{32,48},{40,24},{48,32},{56,8},{64,80... | collective-permute-start | bytes 1327112 | tf_op jit(solution)/shard_map/ppermute | solution.py:35
  74.7 4.3 %collective-permute-start.12 = (f32[8,128]{0,1:T(8,128)S(1)}, f32[8,128]{0,1:T(8,128)S(1)}, u32[]{:S(2)}, u32[]{:S(2)}) collective-permute-start(f32[8,128]{0,1:T(8,128)S(1)} %broadcast_in_dim.21), channel_id=1, source_target_pairs={{0,16},{8,56},{16,0},{24,40},{32,48},{40,24},{48,32},{56,8},{64,80... | collective-permute-start | bytes 12296 | tf_op jit(solution)/shard_map/ppermute | solution.py:35
  75.4 17.0 %collective-permute-start.18 = (f32[32,3456]{1,0:T(8,128)S(1)}, f32[32,3456]{1,0:T(8,128)S(1)}, u32[]{:S(2)}, u32[]{:S(2)}) collective-permute-start(f32[32,3456]{1,0:T(8,128)S(1)} %get-tuple-element.7.refs_2_), channel_id=1, source_target_pairs={{0,64},{8,72},{16,80},{24,88},{32,96},{40,104},{48,112},{56,120},{... | collective-permute-start | bytes 1327112 | tf_op jit(solution)/shard_map/ppermute | solution.py:35
  77.1 29.8 %collective-permute-start.23 = (f32[32,6784]{1,0:T(8,128)S(1)}, f32[32,6784]{1,0:T(8,128)S(1)}, u32[]{:S(2)}, u32[]{:S(2)}) collective-permute-start(f32[32,6784]{1,0:T(8,128)S(1)} %get-tuple-element.12.refs_3_), channel_id=1, source_target_pairs={{0,8},{8,0},{16,24},{24,16},{32,40},{40,32},{48,56},{56,48},{64,72... | collective-permute-start | bytes 2605064 | tf_op jit(solution)/shard_map/ppermute | solution.py:35
  78.2 32.5 %collective-permute-start.21 = (f32[32,6784]{1,0:T(8,128)S(1)}, f32[32,6784]{1,0:T(8,128)S(1)}, u32[]{:S(2)}, u32[]{:S(2)}) collective-permute-start(f32[32,6784]{1,0:T(8,128)S(1)} %collective-permute-done.19.refs_3_), channel_id=1, source_target_pairs={{0,8},{8,0},{16,24},{24,16},{32,40},{40,32},{48,56},{56,48},{64,72... | collective-permute-start | bytes 2605064 | tf_op jit(solution)/shard_map/ppermute | solution.py:35
  79.1 10.2 %collective-permute-start.13 = (f32[8,128]{0,1:T(8,128)S(1)}, f32[8,128]{0,1:T(8,128)S(1)}, u32[]{:S(2)}, u32[]{:S(2)}) collective-permute-start(f32[8,128]{0,1:T(8,128)S(1)} %broadcast_add_fusion), channel_id=1, source_target_pairs={{0,64},{8,72},{16,80},{24,88},{32,96},{40,104},{48,112},{56,120},{... | collective-permute-start | bytes 12296 | tf_op jit(solution)/shard_map/ppermute | solution.py:35
  89.3 1.3 %collective-permute-start.14 = (f32[8,128]{0,1:T(8,128)S(1)}, f32[8,128]{0,1:T(8,128)S(1)}, u32[]{:S(2)}, u32[]{:S(2)}) collective-permute-start(f32[8,128]{0,1:T(8,128)S(1)} %fusion.8), channel_id=1, source_target_pairs={{0,8},{8,0},{16,24},{24,16},{32,40},{40,32},{48,56},{56,48},{64,72... | collective-permute-start | bytes 12296 | tf_op jit(solution)/shard_map/ppermute | solution.py:35
  90.6 4.4 %collective-permute-start.15 = (f32[8,128]{0,1:T(8,128)S(1)}, f32[8,128]{0,1:T(8,128)S(1)}, u32[]{:S(2)}, u32[]{:S(2)}) collective-permute-start(f32[8,128]{0,1:T(8,128)S(1)} %add.179), channel_id=1, source_target_pairs={{0,2},{1,3},{2,0},{3,1},{4,6},{5,7},{6,4},{7,5},{8,10},{9,11},{10,... | collective-permute-start | bytes 12296 | tf_op jit(solution)/shard_map/ppermute | solution.py:35
  92.3 14.5 %collective-permute-start.22 = (f32[32,3456]{1,0:T(8,128)S(1)}, f32[32,3456]{1,0:T(8,128)S(1)}, u32[]{:S(2)}, u32[]{:S(2)}) collective-permute-start(f32[32,3456]{1,0:T(8,128)S(1)} %get-tuple-element.7.refs_2_), channel_id=1, source_target_pairs={{0,8},{8,0},{16,24},{24,16},{32,40},{40,32},{48,56},{56,48},{64,72... | collective-permute-start | bytes 1327112 | tf_op jit(solution)/shard_map/ppermute | solution.py:35
  92.4 18.3 %collective-permute-start.20 = (f32[32,3456]{1,0:T(8,128)S(1)}, f32[32,3456]{1,0:T(8,128)S(1)}, u32[]{:S(2)}, u32[]{:S(2)}) collective-permute-start(f32[32,3456]{1,0:T(8,128)S(1)} %collective-permute-done.18.refs_2_), channel_id=1, source_target_pairs={{0,8},{8,0},{16,24},{24,16},{32,40},{40,32},{48,56},{56,48},{64,72... | collective-permute-start | bytes 1327112 | tf_op jit(solution)/shard_map/ppermute | solution.py:35
  95.1 5.6 %collective-permute-start.16 = (f32[8,128]{0,1:T(8,128)S(1)}, f32[8,128]{0,1:T(8,128)S(1)}, u32[]{:S(2)}, u32[]{:S(2)}) collective-permute-start(f32[8,128]{0,1:T(8,128)S(1)} %add.180), channel_id=1, source_target_pairs={{0,6},{1,7},{2,4},{3,5},{4,2},{5,3},{6,0},{7,1},{8,14},{9,15},{10,... | collective-permute-start | bytes 12296 | tf_op jit(solution)/shard_map/ppermute | solution.py:35
  100.6 6.2 %collective-permute-start.17 = (f32[8,128]{0,1:T(8,128)S(1)}, f32[8,128]{0,1:T(8,128)S(1)}, u32[]{:S(2)}, u32[]{:S(2)}) collective-permute-start(f32[8,128]{0,1:T(8,128)S(1)} %add.181), channel_id=1, source_target_pairs={{0,1},{1,0},{2,3},{3,2},{4,5},{5,4},{6,7},{7,6},{8,9},{9,8},{10,11... | collective-permute-start | bytes 12296 | tf_op jit(solution)/shard_map/ppermute | solution.py:35

commit v2 on v0

v2 whole, which is shorter than its diff:
```python
import jax
import jax.numpy as jnp
from jax import lax
from jax.sharding import PartitionSpec as P
from jax.experimental import pallas as pl
from jax.experimental.pallas import tpu as pltpu

EPS = 1e-06
RMS_MAX = 0.5
MU = 0.9
LR = 0.7
X, CORES = 4, 2


def island_id(z, x, core):
    return ((z % 2) * X + x % X) * CORES + core % CORES


def neighbour(x, core, parity):
    return x + 1 if (x + core + parity) % 2 == 0 else x - 1


PLACES = [(z, x, core) for z in range(2) for x in range(X) for core in range(CORES)]
CORE = [(island_id(*p), island_id(p[0], p[1], p[2] + 1)) for p in PLACES]
Z = [(island_id(*p), island_id(p[0] + 1, p[1], p[2])) for p in PLACES]
X0 = [(island_id(*p), island_id(p[0], neighbour(p[1], p[2], 0), p[2])) for p in PLACES]
X1 = [(island_id(*p), island_id(p[0], neighbour(p[1], p[2], 1), p[2])) for p in PLACES]
YZ = [(y, h) for y in range(4) for h in range(2)]
Y0 = [(y * 2 + h, (y ^ 1) * 2 + h) for y, h in YZ]
Y1 = [(y * 2 + h, ((y + (1 if y % 2 else -1)) % 4) * 2 + h) for y, h in YZ]
H = [(y * 2 + h, y * 2 + (1 - h)) for y, h in YZ]


def hop(value, pairs, axis="island"):
    return lax.ppermute(value, axis, pairs)


WA, WB = 3456, 3456
VMEM = pl.BlockSpec(memory_space=pltpu.VMEM)
SMEM = pl.BlockSpec(memory_space=pltpu.SMEM)
HBM = pl.BlockSpec(memory_space=pltpu.HBM)


def diagonal():
    pairs = []
    for z, x, core in PLACES:
        pairs.append((island_id(z, x, core), island_id(z + 1, neighbour(x, core, 0), core)))
    return pairs


ZX = diagonal()
FSDP_STEPS = ((Y0, "fsdp"), (Y1, "fsdp"), (H, "fsdp"))


def fetches(source, target, frag_a, frag_bc, sem):
    width = source.shape[2]
    return [
        pltpu.make_async_copy(source.at[frag_a, :, pl.ds(0, WA)], target.at[:, pl.ds(0, WA)], sem.at[0]),
        pltpu.make_async_copy(source.at[frag_bc, :, pl.ds(WA, width - WA)], target.at[:, pl.ds(WA, width - WA)], sem.at[1]),
    ]


def pick_kernel(ids, inner, send, keep, sem):
    copies = fetches(inner, send, ids[0], ids[1], sem.at[0]) + fetches(inner, keep, ids[2], ids[3], sem.at[1])
    for copy in copies:
        copy.start()
    for copy in copies:
        copy.wait()


def pick(ids, inner):
    rows, width = inner.shape[1:]
    shape = jax.ShapeDtypeStruct((rows, width), inner.dtype)
    return pl.pallas_call(
        pick_kernel,
        out_shape=(shape, shape),
        in_specs=[SMEM, HBM],
        out_specs=(VMEM, VMEM),
        scratch_shapes=[pltpu.SemaphoreType.DMA((2, 2))],
        compiler_params=pltpu.CompilerParams(vmem_limit_bytes=60 << 20),
        cost_estimate=pl.CostEstimate(flops=0, bytes_accessed=1024, transcendentals=0),
    )(ids, inner)


def differ_kernel(ids, inner, anchor, *refs):
    *outs, sem = refs
    groups = []
    for i in range(2):
        diff, base = outs[2 * i : 2 * i + 2]
        groups.append(
            fetches(inner, diff, ids[2 * i], ids[2 * i + 1], sem.at[i, 0])
            + fetches(anchor, base, ids[2 * i], ids[2 * i + 1], sem.at[i, 1])
        )
        for copy in groups[-1]:
            copy.start()
    for i in range(2):
        diff, base = outs[2 * i : 2 * i + 2]
        for copy in groups[i]:
            copy.wait()
        diff[...] = base[...] - diff[...]


def differ(ids, inner, anchor):
    rows, width = inner.shape[1:]
    shape = jax.ShapeDtypeStruct((rows, width), inner.dtype)
    return pl.pallas_call(
        differ_kernel,
        out_shape=(shape,) * 4,
        in_specs=[SMEM, HBM, HBM],
        out_specs=(VMEM,) * 4,
        scratch_shapes=[pltpu.SemaphoreType.DMA((2, 2, 2))],
        compiler_params=pltpu.CompilerParams(vmem_limit_bytes=50 << 20),
        cost_estimate=pl.CostEstimate(flops=0, bytes_accessed=1024, transcendentals=0),
    )(ids, inner, anchor)


def total_kernel(ids, a, b, c, a_r, b_r, c_r, near, bc, sq):
    width = near.shape[1]
    sums = []
    for mine, got, lo in ((a, a_r, 0), (b, b_r, WA), (c, c_r, WA + WB)):
        size = mine.shape[1]
        part = jnp.zeros((mine.shape[0], 128), jnp.float32)
        for start in range(0, size, 128):
            value = mine[:, start : start + 128] + got[:, start : start + 128]
            near[:, lo + start : lo + start + 128] = value
            if lo:
                bc[:, lo - WA + start : lo - WA + start + 128] = value
            part = part + value * value
        sums.append(part)
    row = lax.broadcasted_iota(jnp.int32, (8, 128), 0)
    left, right = jnp.sum(sums[0]), jnp.sum(sums[1] + sums[2])
    sq[...] = jnp.where(row == ids[0], left, 0.0) + jnp.where(row == ids[1], right, 0.0)


def total(ids, *pieces):
    rows = pieces[0].shape[0]
    width = sum(p.shape[1] for p in pieces[:3])
    shape = lambda *dims: jax.ShapeDtypeStruct(dims, jnp.float32)
    return pl.pallas_call(
        total_kernel,
        out_shape=(shape(rows, width), shape(rows, width - WA), shape(8, 128)),
        in_specs=[SMEM] + [VMEM] * 6,
        out_specs=(VMEM,) * 3,
        compiler_params=pltpu.CompilerParams(vmem_limit_bytes=12 << 20),
        cost_estimate=pl.CostEstimate(flops=0, bytes_accessed=1024, transcendentals=0),
    )(ids, *pieces)


def update_kernel(ids, scale, *refs):
    sums, (anchor, momentum, out_a, out_m, va, vm, sem_in, sem_out) = refs[:4], refs[4:]
    width = anchor.shape[2]
    chunks = []
    for i in range(4):
        for j, (lo, hi) in enumerate(((0, WA), (WA, width))):
            middle = lo + (hi - lo) // 256 * 128
            for start, stop in ((lo, middle), (middle, hi)):
                chunks.append((i, ids[2 * i + j], start, stop - start))

    def loads(n):
        i, frag, start, size = chunks[n]
        cols = pl.ds(start, size)
        return [
            pltpu.make_async_copy(anchor.at[frag, :, cols], va.at[i, :, cols], sem_in.at[0, n]),
            pltpu.make_async_copy(momentum.at[frag, :, cols], vm.at[i, :, cols], sem_in.at[1, n]),
        ]

    def stores(n):
        i, frag, start, size = chunks[n]
        cols = pl.ds(start, size)
        return [
            pltpu.make_async_copy(va.at[i, :, cols], out_a.at[frag, :, cols], sem_out.at[0, n]),
            pltpu.make_async_copy(vm.at[i, :, cols], out_m.at[frag, :, cols], sem_out.at[1, n]),
        ]

    for n in range(len(chunks)):
        for copy in loads(n):
            copy.start()
    for n, (i, frag, start, size) in enumerate(chunks):
        for copy in loads(n):
            copy.wait()
        cols = slice(start, start + size)
        clipped = sums[i][:, cols] * scale[frag]
        new_m = MU * vm[i, :, cols] + clipped
        va[i, :, cols] = va[i, :, cols] - LR * (clipped + MU * new_m)
        vm[i, :, cols] = new_m
        for copy in stores(n):
            copy.start()
    for n in range(len(chunks)):
        for copy in stores(n):
            copy.wait()


def update(pieces, ids, scale, anchor, momentum):
    shape = jax.ShapeDtypeStruct(anchor.shape, anchor.dtype)
    total = anchor.size * 4
    any_spec = pl.BlockSpec(memory_space=pl.ANY)
    return pl.pallas_call(
        update_kernel,
        out_shape=(shape, shape),
        in_specs=[SMEM, SMEM] + [VMEM] * 4 + [any_spec] * 2,
        out_specs=(HBM, HBM),
        scratch_shapes=[pltpu.VMEM(anchor.shape, jnp.float32)] * 2 + [pltpu.SemaphoreType.DMA((2, 16))] * 2,
        compiler_params=pltpu.CompilerParams(vmem_limit_bytes=56 << 20),
        cost_estimate=pl.CostEstimate(flops=2 * total, bytes_accessed=5 * total, transcendentals=0),
    )(ids, scale, *pieces, anchor, momentum)


def on_device(inner, anchor, momentum):
    inner = inner[0]
    rows, width = anchor.shape[1:]
    islands = lax.axis_size("island")
    entries = rows * 8 * width
    me = lax.axis_index("island").astype(jnp.uint32)
    core, x, z = me % 2, (me // 2) % X, me // 8
    bit, peer_bit = ((x + 1 - core) // 2) % 2, ((x + core) // 2) % 2
    core, z, bit, peer_bit = (v.astype(jnp.int32) for v in (core, z, bit, peer_bit))
    own, other = 2 * core, 2 * (1 - core)
    order = []

    def turn(value):
        return lax.optimization_barrier((value, order[-1]))[0] if order else value

    def note(value):
        order.append(value)
        return value

    far_own, near_own = (own + 1 - z, own + 1 - bit), (own + z, own + bit)
    far_other, near_other = (other + 1 - z, other + 1 - peer_bit), (other + z, other + peer_bit)
    send, keep = pick(jnp.stack(far_other + near_other), inner)
    got_send = hop(send, CORE)
    got_keep = hop(keep, CORE)
    diff_send, base_send, diff_keep, base_keep = differ(jnp.stack(far_own + near_own), inner, anchor)
    send = diff_send + (base_send - got_send)
    a_r, bc_r = hop(send[:, :WA], Z), hop(send[:, WA:], X0)
    note(send)
    kept = note(diff_keep + (base_keep - turn(got_keep)))
    a = turn(a_r) + kept[:, :WA]
    bc = turn(bc_r) + kept[:, WA:]
    b, c = bc[:, :WB], bc[:, WB:]
    ab = note(jnp.concatenate([a, b], axis=1))
    c_r, ab_r = hop(c, Z), hop(ab, X1)
    c = note(turn(c_r) + c)
    ab = note(turn(ab_r) + ab)
    a, b = ab[:, :WA], ab[:, WA:]
    b_r, a_r, c_r = hop(b, Z), hop(a, X0), hop(c, X1)
    near, bc, sq = total(jnp.stack(near_own), a, b, c, a_r, b_r, c_r)
    note(sq)
    steps = ((ZX, "island"), (CORE, "island")) + FSDP_STEPS
    for k, step in enumerate(steps):
        sq = note(sq + turn(hop(sq, *step)))
        if k == 0:
            a_far, bc_far = hop(turn(near)[:, :WA], Z), hop(turn(bc), X0)
        if k == 1:
            near_peer = hop(turn(near), CORE)
        if k == 3:
            far = jnp.concatenate([turn(v) for v in (a_far, bc_far)], axis=1)
            far_peer = hop(far, CORE)
            note(far)
    mean_sq = sq[:4, 0] * (1.0 / (islands * islands)) / entries
    factor = jnp.minimum(1.0, RMS_MAX / jnp.sqrt(mean_sq + EPS)) / islands
    ids = jnp.stack(near_own + near_other + far_own + far_other)
    return tuple(update([near, near_peer, far, far_peer], ids, factor, anchor, momentum))


def solution(mesh):
    spec = P(None, "fsdp", None)
    return jax.shard_map(
        on_device,
        mesh=mesh,
        in_specs=(P("island", None, "fsdp", None), spec, spec),
        out_specs=(spec, spec),
        check_vma=False,
    )
```

time: 196 us -> 90.8 us (0.46)
  waiting for transfers between devices: 135 us -> 44.7 us
  blocking collectives: 24 us -> 0 us
  starting transfers between devices: 0.04 us -> 21.2 us
  Pallas kernels: 0 us -> 20.4 us
  other arithmetic: 22.2 us -> 2.1 us
  between operations: 14 us -> 0.84 us
    psum x1 -> x0, waiting for transfers between devices: 135 us -> none  [on_device(): average = lax.psum(delta, 'island') / islands]
    ppermute x0 -> x18, waiting for transfers between devices: none -> 44.7 us  [hop(): return lax.ppermute(value, axis, pairs)]
    psum x1 -> x0, blocking collectives: 24 us -> none  [on_device(): total_sq = lax.psum(local_sq, 'fsdp')]
    ppermute x0 -> x18, starting transfers between devices: none -> 21.2 us  [hop(): return lax.ppermute(value, axis, pairs)]
    pallas_call x0 -> x4, Pallas kernels: none -> 20.4 us  [the longest x1 11.3 us: update(): pl.pallas_call(update_kernel, out_shape=(shape, shape), in_specs=[SMEM, S...]
    sub x2 -> x0, other arithmetic: 18.9 us -> none  [the longest x1 11.8 us: apply_update(): new_anchor = anchor - LR * (clipped + MU * new_momentum)]
    reduce_sum x1 -> x0, other arithmetic: 3.25 us -> none  [on_device(): local_sq = jnp.sum(average * average, axis=(1, 2))]
  transfers between devices with their start and end apart: 1 -> 18, of which waited for: 1 -> 13; matrix products, arithmetic and copies ran while one was open for 0% -> 2% of each run, Pallas kernels for 0% -> 5%
where the time goes in v2:
time: 90.8 us; the launch traced here: 90.2 us
  waiting for transfers between devices  44.7 us (49%)
  starting transfers between devices  21.2 us (23%)
  Pallas kernels  20.4 us (22%)
  other arithmetic  2.1 us (2%)
  local copies, waits for them, and re-layouts  0.97 us (1%)
    ppermute x18, waiting for transfers between devices, hop(): return lax.ppermute(value, axis, pairs)  44.7 us
    ppermute x18, starting transfers between devices, hop(): return lax.ppermute(value, axis, pairs)  21.2 us
    pallas_call x1, Pallas kernels, update(): pl.pallas_call(update_kernel, out_shape=(shape, shape), in_specs=[SMEM, S...  11.3 us
    pallas_call x1, Pallas kernels, differ(): pl.pallas_call(differ_kernel, out_shape=(shape,) * 4, in_specs=[SMEM, HBM...  4.29 us
    pallas_call x1, Pallas kernels, pick(): pl.pallas_call(pick_kernel, out_shape=(shape, shape), in_specs=[SMEM, HBM...  3.9 us
  transfers between devices with their start and end apart: 18, of which 13 were waited for; matrix products, arithmetic and copies ran while one was open for 2% of the time, Pallas kernels for 5%

profile of v2, /device:TPU:0, one launch (start us, length us, event | category | flops | bytes accessed | tf_op | source)
XLA Modules:
  0.0 90.2 jit_solution(15795282925635575128)
XLA Ops:
  0.6 0.6 pad_add_fusion.2.ids
  1.2 3.9 %shard_map.51 = (f32[32,10240]{1,0:T(8,128)}, f32[32,10240]{1,0:T(8,128)}) custom-call(s32[4]{0:T(128)} %pad_add_fusion.2.ids, f32[4,32,10240]{2,1,0:T(8,128)} %bitcast.9), custom_call_target="tpu_custom_call" | custom-call | bytes 1024 | tf_op jit(solution)/shard_map/pallas_call | solution.py:74
  5.2 0.5 collective-permute-start.2
  5.8 4.3 %shard_map.50 = (f32[32,10240]{1,0:T(8,128)S(1)}, f32[32,10240]{1,0:T(8,128)S(1)}, f32[32,10240]{1,0:T(8,128)S(1)}, f32[32,10240]{1,0:T(8,128)}) custom-call(s32[4]{0:T(128)S(1)} %pad_add_fusion.1.ids, f32[4,32,10240]{2,1,0:T(8,128)} %bitcast.10, f32[4,32,10240]{2,1,0:T(8,128)} %refs_4_.1), custom_call_target="tpu_custom_call" | custom-call | bytes 1024 | tf_op jit(solution)/shard_map/pallas_call | solution.py:106
  10.4 2.1 %collective-permute-start.1 = (f32[32,3456]{1,0:T(8,128)S(1)}, f32[32,3456]{1,0:T(8,128)S(1)}, u32[]{:S(2)}, u32[]{:S(2)}) collective-permute-start(f32[32,3456]{1,0:T(8,128)S(1)} %slice.40), channel_id=1, source_target_pairs={{0,64},{8,72},{16,80},{24,88},{32,96},{40,104},{48,112},{56,120},{... | collective-permute-start | bytes 1327112 | tf_op jit(solution)/shard_map/ppermute | solution.py:35
  12.5 1.5 %collective-permute-start.3 = (f32[32,6784]{1,0:T(8,128)S(1)}, f32[32,6784]{1,0:T(8,128)S(1)}, u32[]{:S(2)}, u32[]{:S(2)}) collective-permute-start(f32[32,6784]{1,0:T(8,128)S(1)} %slice.42), channel_id=1, source_target_pairs={{0,16},{8,56},{16,0},{24,40},{32,48},{40,24},{48,32},{56,8},{64,80... | collective-permute-start | bytes 2605064 | tf_op jit(solution)/shard_map/ppermute | solution.py:35
  14.2 8.7 %collective-permute-done.1 = f32[32,3456]{1,0:T(8,128)S(1)} collective-permute-done((f32[32,3456]{1,0:T(8,128)S(1)}, f32[32,3456]{1,0:T(8,128)S(1)}, u32[]{:S(2)}, u32[]{:S(2)}) %collective-permute-start.1) | collective-permute-done | bytes 442400 | tf_op jit(solution)/shard_map/ppermute | solution.py:35
  23.0 2.4 %collective-permute-done.3 = f32[32,6784]{1,0:T(8,128)S(1)} collective-permute-done((f32[32,6784]{1,0:T(8,128)S(1)}, f32[32,6784]{1,0:T(8,128)S(1)}, u32[]{:S(2)}, u32[]{:S(2)}) %collective-permute-start.3) | collective-permute-done | bytes 868384 | tf_op jit(solution)/shard_map/ppermute | solution.py:35
  25.8 2.9 %collective-permute-start.4 = (f32[32,6912]{1,0:T(8,128)S(1)}, f32[32,6912]{1,0:T(8,128)S(1)}, u32[]{:S(2)}, u32[]{:S(2)}) collective-permute-start(f32[32,6912]{1,0:T(8,128)S(1)} %pad_maximum_fusion), channel_id=1, source_target_pairs={{0,48},{8,24},{16,32},{24,8},{32,16},{40,56},{48,0},{56,40},{64,11... | collective-permute-start | bytes 2654216 | tf_op jit(solution)/shard_map/ppermute | solution.py:35
  28.6 8.6 %collective-permute-done.5 = f32[32,3328]{1,0:T(8,128)S(1)} collective-permute-done((f32[32,3328]{1,0:T(8,128)S(1)}, f32[32,3328]{1,0:T(8,128)S(1)}, u32[]{:S(2)}, u32[]{:S(2)}) %collective-permute-start.5) | collective-permute-done | bytes 426016 | tf_op jit(solution)/shard_map/ppermute | solution.py:35
  37.3 2.8 %collective-permute-done.4 = f32[32,6912]{1,0:T(8,128)S(1)} collective-permute-done((f32[32,6912]{1,0:T(8,128)S(1)}, f32[32,6912]{1,0:T(8,128)S(1)}, u32[]{:S(2)}, u32[]{:S(2)}) %collective-permute-start.4) | collective-permute-done | bytes 884768 | tf_op jit(solution)/shard_map/ppermute | solution.py:35
  40.3 2.0 %collective-permute-start.7 = (f32[32,3456]{1,0:T(8,128)S(1)}, f32[32,3456]{1,0:T(8,128)S(1)}, u32[]{:S(2)}, u32[]{:S(2)}) collective-permute-start(f32[32,3456]{1,0:T(8,128)S(1)} %get-tuple-element.50.b), channel_id=1, source_target_pairs={{0,64},{8,72},{16,80},{24,88},{32,96},{40,104},{48,112},{56,120},{... | collective-permute-start | bytes 1327112 | tf_op jit(solution)/shard_map/ppermute | solution.py:35
  42.3 0.3 collective-permute-start.6
  42.6 2.5 %collective-permute-start.8 = (f32[32,3328]{1,0:T(8,128)S(1)}, f32[32,3328]{1,0:T(8,128)S(1)}, u32[]{:S(2)}, u32[]{:S(2)}) collective-permute-start(f32[32,3328]{1,0:T(8,128)S(1)} %slice_add_fusion.2.c), channel_id=1, source_target_pairs={{0,48},{8,24},{16,32},{24,8},{32,16},{40,56},{48,0},{56,40},{64,11... | collective-permute-start | bytes 1277960 | tf_op jit(solution)/shard_map/ppermute | solution.py:35
  45.1 7.5 %collective-permute-done.8.c_r = f32[32,3328]{1,0:T(8,128)S(1)} collective-permute-done((f32[32,3328]{1,0:T(8,128)S(1)}, f32[32,3328]{1,0:T(8,128)S(1)}, u32[]{:S(2)}, u32[]{:S(2)}) %collective-permute-start.8) | collective-permute-done | bytes 426016 | tf_op jit(solution)/shard_map/ppermute | solution.py:35
  52.7 1.3 %collective-permute-done.6.a_r = f32[32,3456]{1,0:T(8,128)S(1)} collective-permute-done((f32[32,3456]{1,0:T(8,128)S(1)}, f32[32,3456]{1,0:T(8,128)S(1)}, u32[]{:S(2)}, u32[]{:S(2)}) %collective-permute-start.6) | collective-permute-done | bytes 442400 | tf_op jit(solution)/shard_map/ppermute | solution.py:35
  53.9 0.8 shard_map.52
  54.9 4.4 %collective-permute-done.9 = f32[8,128]{1,0:T(8,128)S(1)} collective-permute-done((f32[8,128]{1,0:T(8,128)S(1)}, f32[8,128]{1,0:T(8,128)S(1)}, u32[]{:S(2)}, u32[]{:S(2)}) %collective-permute-start.9) | collective-permute-done | bytes 4128 | tf_op jit(solution)/shard_map/ppermute | solution.py:35
  59.4 0.5 collective-permute-start.14
  59.8 0.3 collective-permute-start.15
  60.1 1.2 %collective-permute-done.10 = f32[8,128]{1,0:T(8,128)S(1)} collective-permute-done((f32[8,128]{1,0:T(8,128)S(1)}, f32[8,128]{1,0:T(8,128)S(1)}, u32[]{:S(2)}, u32[]{:S(2)}) %collective-permute-start.10) | collective-permute-done | bytes 4128 | tf_op jit(solution)/shard_map/ppermute | solution.py:35
  61.3 1.6 %collective-permute-start.11 = (f32[8,128]{1,0:T(8,128)S(1)}, f32[8,128]{1,0:T(8,128)S(1)}, u32[]{:S(2)}, u32[]{:S(2)}) collective-permute-start(f32[8,128]{1,0:T(8,128)S(1)} %add.83), channel_id=1, source_target_pairs={{0,2},{1,3},{2,0},{3,1},{4,6},{5,7},{6,4},{7,5},{8,10},{9,11},{10,... | collective-permute-start | bytes 12296 | tf_op jit(solution)/shard_map/ppermute | solution.py:35
  62.9 2.0 %collective-permute-done.11 = f32[8,128]{1,0:T(8,128)S(1)} collective-permute-done((f32[8,128]{1,0:T(8,128)S(1)}, f32[8,128]{1,0:T(8,128)S(1)}, u32[]{:S(2)}, u32[]{:S(2)}) %collective-permute-start.11) | collective-permute-done | bytes 4128 | tf_op jit(solution)/shard_map/ppermute | solution.py:35
  64.9 3.0 %collective-permute-start.12 = (f32[8,128]{1,0:T(8,128)S(1)}, f32[8,128]{1,0:T(8,128)S(1)}, u32[]{:S(2)}, u32[]{:S(2)}) collective-permute-start(f32[8,128]{1,0:T(8,128)S(1)} %add.84), channel_id=1, source_target_pairs={{0,6},{1,7},{2,4},{3,5},{4,2},{5,3},{6,0},{7,1},{8,14},{9,15},{10,... | collective-permute-start | bytes 12296 | tf_op jit(solution)/shard_map/ppermute | solution.py:35
  67.9 1.8 %collective-permute-done.12 = f32[8,128]{1,0:T(8,128)S(1)} collective-permute-done((f32[8,128]{1,0:T(8,128)S(1)}, f32[8,128]{1,0:T(8,128)S(1)}, u32[]{:S(2)}, u32[]{:S(2)}) %collective-permute-start.12) | collective-permute-done | bytes 4128 | tf_op jit(solution)/shard_map/ppermute | solution.py:35
  69.7 0.6 collective-permute-done.14
  70.3 2.4 %collective-permute-done.15 = f32[32,6784]{1,0:T(8,128)S(1)} collective-permute-done((f32[32,6784]{1,0:T(8,128)S(1)}, f32[32,6784]{1,0:T(8,128)S(1)}, u32[]{:S(2)}, u32[]{:S(2)}) %collective-permute-start.15) | collective-permute-done | bytes 868384 | tf_op jit(solution)/shard_map/ppermute | solution.py:35
  72.9 3.7 %collective-permute-start.13 = (f32[8,128]{1,0:T(8,128)S(1)}, f32[8,128]{1,0:T(8,128)S(1)}, u32[]{:S(2)}, u32[]{:S(2)}) collective-permute-start(f32[8,128]{1,0:T(8,128)S(1)} %add.85), channel_id=1, source_target_pairs={{0,1},{1,0},{2,3},{3,2},{4,5},{5,4},{6,7},{7,6},{8,9},{9,8},{10,11... | collective-permute-start | bytes 12296 | tf_op jit(solution)/shard_map/ppermute | solution.py:35
  76.6 0.6 stack.54.ids
  77.2 1.0 %collective-permute-done.13 = f32[8,128]{1,0:T(8,128)S(1)} collective-permute-done((f32[8,128]{1,0:T(8,128)S(1)}, f32[8,128]{1,0:T(8,128)S(1)}, u32[]{:S(2)}, u32[]{:S(2)}) %collective-permute-start.13) | collective-permute-done | bytes 4128 | tf_op jit(solution)/shard_map/ppermute | solution.py:35
  78.2 0.6 multiply_reduce_fusion.scale
  78.8 11.3 %shard_map.53 = (f32[4,32,10240]{2,1,0:T(8,128)}, f32[4,32,10240]{2,1,0:T(8,128)}) custom-call(s32[8]{0:T(128)} %stack.54.ids, f32[4]{0:T(128)} %multiply_reduce_fusion.scale, f32[32,10240]{1,0:T(8,128)} %copy-done, f32[32,10240]{1,0:T(8,128)} %collective-permute-done.16.refs_1_, f32[32,10240]{1,0:T(8,128)} %copy-done.1, ...), custom_call_target="tpu_custom_call" | custom-call | flops 10485760 | bytes 26214400 | tf_op jit(solution)/shard_map/pallas_call | solution.py:197
  (39 shorter events, 1.7 us)
Async XLA Ops:
  5.1 5.0 %collective-permute-start = (f32[32,10240]{1,0:T(8,128)}, f32[32,10240]{1,0:T(8,128)S(1)}, u32[]{:S(2)}, u32[]{:S(2)}) collective-permute-start(f32[32,10240]{1,0:T(8,128)} %get-tuple-element.28), channel_id=1, source_target_pairs={{0,8},{8,0},{16,24},{24,16},{32,40},{40,32},{48,56},{56,48},{64,72... | collective-permute-start | bytes 3932168 | tf_op jit(solution)/shard_map/ppermute | solution.py:35
  5.2 5.2 %collective-permute-start.2 = (f32[32,10240]{1,0:T(8,128)}, f32[32,10240]{1,0:T(8,128)S(1)}, u32[]{:S(2)}, u32[]{:S(2)}) collective-permute-start(f32[32,10240]{1,0:T(8,128)} %get-tuple-element.31), channel_id=1, source_target_pairs={{0,8},{8,0},{16,24},{24,16},{32,40},{40,32},{48,56},{56,48},{64,72... | collective-permute-start | bytes 3932168 | tf_op jit(solution)/shard_map/ppermute | solution.py:35
  10.3 3.7 %copy-start.2 = (f32[32,10240]{1,0:T(8,128)S(1)}, f32[32,10240]{1,0:T(8,128)}, u32[]{:S(2)}) copy-start(f32[32,10240]{1,0:T(8,128)} %get-tuple-element.30) | copy-start | bytes 3932164
  10.4 12.5 %collective-permute-start.1 = (f32[32,3456]{1,0:T(8,128)S(1)}, f32[32,3456]{1,0:T(8,128)S(1)}, u32[]{:S(2)}, u32[]{:S(2)}) collective-permute-start(f32[32,3456]{1,0:T(8,128)S(1)} %slice.40), channel_id=1, source_target_pairs={{0,64},{8,72},{16,80},{24,88},{32,96},{40,104},{48,112},{56,120},{... | collective-permute-start | bytes 1327112 | tf_op jit(solution)/shard_map/ppermute | solution.py:35
  12.5 12.9 %collective-permute-start.3 = (f32[32,6784]{1,0:T(8,128)S(1)}, f32[32,6784]{1,0:T(8,128)S(1)}, u32[]{:S(2)}, u32[]{:S(2)}) collective-permute-start(f32[32,6784]{1,0:T(8,128)S(1)} %slice.42), channel_id=1, source_target_pairs={{0,16},{8,56},{16,0},{24,40},{32,48},{40,24},{48,32},{56,8},{64,80... | collective-permute-start | bytes 2605064 | tf_op jit(solution)/shard_map/ppermute | solution.py:35
  25.6 11.7 %collective-permute-start.5 = (f32[32,3328]{1,0:T(8,128)S(1)}, f32[32,3328]{1,0:T(8,128)S(1)}, u32[]{:S(2)}, u32[]{:S(2)}) collective-permute-start(f32[32,3328]{1,0:T(8,128)S(1)} %slice.45), channel_id=1, source_target_pairs={{0,64},{8,72},{16,80},{24,88},{32,96},{40,104},{48,112},{56,120},{... | collective-permute-start | bytes 1277960 | tf_op jit(solution)/shard_map/ppermute | solution.py:35
  25.8 14.3 %collective-permute-start.4 = (f32[32,6912]{1,0:T(8,128)S(1)}, f32[32,6912]{1,0:T(8,128)S(1)}, u32[]{:S(2)}, u32[]{:S(2)}) collective-permute-start(f32[32,6912]{1,0:T(8,128)S(1)} %pad_maximum_fusion), channel_id=1, source_target_pairs={{0,48},{8,24},{16,32},{24,8},{32,16},{40,56},{48,0},{56,40},{64,11... | collective-permute-start | bytes 2654216 | tf_op jit(solution)/shard_map/ppermute | solution.py:35
  40.3 12.4 %collective-permute-start.7 = (f32[32,3456]{1,0:T(8,128)S(1)}, f32[32,3456]{1,0:T(8,128)S(1)}, u32[]{:S(2)}, u32[]{:S(2)}) collective-permute-start(f32[32,3456]{1,0:T(8,128)S(1)} %get-tuple-element.50.b), channel_id=1, source_target_pairs={{0,64},{8,72},{16,80},{24,88},{32,96},{40,104},{48,112},{56,120},{... | collective-permute-start | bytes 1327112 | tf_op jit(solution)/shard_map/ppermute | solution.py:35
  42.3 11.6 %collective-permute-start.6 = (f32[32,3456]{1,0:T(8,128)S(1)}, f32[32,3456]{1,0:T(8,128)S(1)}, u32[]{:S(2)}, u32[]{:S(2)}) collective-permute-start(f32[32,3456]{1,0:T(8,128)S(1)} %get-tuple-element.51.a), channel_id=1, source_target_pairs={{0,16},{8,56},{16,0},{24,40},{32,48},{40,24},{48,32},{56,8},{64,80... | collective-permute-start | bytes 1327112 | tf_op jit(solution)/shard_map/ppermute | solution.py:35
  42.6 10.1 %collective-permute-start.8 = (f32[32,3328]{1,0:T(8,128)S(1)}, f32[32,3328]{1,0:T(8,128)S(1)}, u32[]{:S(2)}, u32[]{:S(2)}) collective-permute-start(f32[32,3328]{1,0:T(8,128)S(1)} %slice_add_fusion.2.c), channel_id=1, source_target_pairs={{0,48},{8,24},{16,32},{24,8},{32,16},{40,56},{48,0},{56,40},{64,11... | collective-permute-start | bytes 1277960 | tf_op jit(solution)/shard_map/ppermute | solution.py:35
  54.8 18.0 %copy-start = (f32[32,10240]{1,0:T(8,128)}, f32[32,10240]{1,0:T(8,128)S(1)}, u32[]{:S(2)}) copy-start(f32[32,10240]{1,0:T(8,128)S(1)} %get-tuple-element.49.refs_0_) | copy-start | bytes 3932164
  54.8 4.6 %collective-permute-start.9 = (f32[8,128]{1,0:T(8,128)S(1)}, f32[8,128]{1,0:T(8,128)S(1)}, u32[]{:S(2)}, u32[]{:S(2)}) collective-permute-start(f32[8,128]{1,0:T(8,128)S(1)} %get-tuple-element.37), channel_id=1, source_target_pairs={{0,80},{8,120},{16,64},{24,104},{32,112},{40,88},{48,96},{56,72},{... | collective-permute-start | bytes 12296 | tf_op jit(solution)/shard_map/ppermute | solution.py:35
  59.4 10.9 %collective-permute-start.14 = (f32[32,3456]{1,0:T(8,128)S(1)}, f32[32,3456]{1,0:T(8,128)S(1)}, u32[]{:S(2)}, u32[]{:S(2)}) collective-permute-start(f32[32,3456]{1,0:T(8,128)S(1)} %slice.38), channel_id=1, source_target_pairs={{0,64},{8,72},{16,80},{24,88},{32,96},{40,104},{48,112},{56,120},{... | collective-permute-start | bytes 1327112 | tf_op jit(solution)/shard_map/ppermute | solution.py:35
  59.8 12.9 %collective-permute-start.15 = (f32[32,6784]{1,0:T(8,128)S(1)}, f32[32,6784]{1,0:T(8,128)S(1)}, u32[]{:S(2)}, u32[]{:S(2)}) collective-permute-start(f32[32,6784]{1,0:T(8,128)S(1)} %get-tuple-element.46), channel_id=1, source_target_pairs={{0,16},{8,56},{16,0},{24,40},{32,48},{40,24},{48,32},{56,8},{64,80... | collective-permute-start | bytes 2605064 | tf_op jit(solution)/shard_map/ppermute | solution.py:35
  60.1 1.2 %collective-permute-start.10 = (f32[8,128]{1,0:T(8,128)S(1)}, f32[8,128]{1,0:T(8,128)S(1)}, u32[]{:S(2)}, u32[]{:S(2)}) collective-permute-start(f32[8,128]{1,0:T(8,128)S(1)} %add.82), channel_id=1, source_target_pairs={{0,8},{8,0},{16,24},{24,16},{32,40},{40,32},{48,56},{56,48},{64,72... | collective-permute-start | bytes 12296 | tf_op jit(solution)/shard_map/ppermute | solution.py:35
  61.3 3.6 %collective-permute-start.11 = (f32[8,128]{1,0:T(8,128)S(1)}, f32[8,128]{1,0:T(8,128)S(1)}, u32[]{:S(2)}, u32[]{:S(2)}) collective-permute-start(f32[8,128]{1,0:T(8,128)S(1)} %add.83), channel_id=1, source_target_pairs={{0,2},{1,3},{2,0},{3,1},{4,6},{5,7},{6,4},{7,5},{8,10},{9,11},{10,... | collective-permute-start | bytes 12296 | tf_op jit(solution)/shard_map/ppermute | solution.py:35
  64.9 4.8 %collective-permute-start.12 = (f32[8,128]{1,0:T(8,128)S(1)}, f32[8,128]{1,0:T(8,128)S(1)}, u32[]{:S(2)}, u32[]{:S(2)}) collective-permute-start(f32[8,128]{1,0:T(8,128)S(1)} %add.84), channel_id=1, source_target_pairs={{0,6},{1,7},{2,4},{3,5},{4,2},{5,3},{6,0},{7,1},{8,14},{9,15},{10,... | collective-permute-start | bytes 12296 | tf_op jit(solution)/shard_map/ppermute | solution.py:35
  67.9 10.9 %collective-permute-start.16 = (f32[32,10240]{1,0:T(8,128)S(1)}, f32[32,10240]{1,0:T(8,128)}, u32[]{:S(2)}, u32[]{:S(2)}) collective-permute-start(f32[32,10240]{1,0:T(8,128)S(1)} %get-tuple-element.49.refs_0_), channel_id=1, source_target_pairs={{0,8},{8,0},{16,24},{24,16},{32,40},{40,32},{48,56},{56,48},{64,72... | collective-permute-start | bytes 3932168 | tf_op jit(solution)/shard_map/ppermute | solution.py:35
  72.8 6.0 %copy-start.1 = (f32[32,10240]{1,0:T(8,128)}, f32[32,10240]{1,0:T(8,128)S(1)}, u32[]{:S(2)}) copy-start(f32[32,10240]{1,0:T(8,128)S(1)} %constant_dynamic-update-slice_fusion.refs_2_) | copy-start | bytes 3932164
  72.8 6.0 %collective-permute-start.17 = (f32[32,10240]{1,0:T(8,128)S(1)}, f32[32,10240]{1,0:T(8,128)}, u32[]{:S(2)}, u32[]{:S(2)}) collective-permute-start(f32[32,10240]{1,0:T(8,128)S(1)} %constant_dynamic-update-slice_fusion.refs_2_), channel_id=1, source_target_pairs={{0,8},{8,0},{16,24},{24,16},{32,40},{40,32},{48,56},{56,48},{64,72... | collective-permute-start | bytes 3932168 | tf_op jit(solution)/shard_map/ppermute | solution.py:35
  72.9 5.3 %collective-permute-start.13 = (f32[8,128]{1,0:T(8,128)S(1)}, f32[8,128]{1,0:T(8,128)S(1)}, u32[]{:S(2)}, u32[]{:S(2)}) collective-permute-start(f32[8,128]{1,0:T(8,128)S(1)} %add.85), channel_id=1, source_target_pairs={{0,1},{1,0},{2,3},{3,2},{4,5},{5,4},{6,7},{7,6},{8,9},{9,8},{10,11... | collective-permute-start | bytes 12296 | tf_op jit(solution)/shard_map/ppermute | solution.py:35

commit v3 on v2

v3 whole, which is shorter than its diff:
```python
import jax
import jax.numpy as jnp
from jax import lax
from jax.sharding import PartitionSpec as P
from jax.experimental import pallas as pl
from jax.experimental.pallas import tpu as pltpu

EPS = 1e-06
RMS_MAX = 0.5
MU = 0.9
LR = 0.7
X, CORES = 4, 2


def island_id(z, x, core):
    return ((z % 2) * X + x % X) * CORES + core % CORES


def neighbour(x, core, parity):
    return x + 1 if (x + core + parity) % 2 == 0 else x - 1


PLACES = [(z, x, core) for z in range(2) for x in range(X) for core in range(CORES)]
CORE = [(island_id(*p), island_id(p[0], p[1], p[2] + 1)) for p in PLACES]
Z = [(island_id(*p), island_id(p[0] + 1, p[1], p[2])) for p in PLACES]
X0 = [(island_id(*p), island_id(p[0], neighbour(p[1], p[2], 0), p[2])) for p in PLACES]
X1 = [(island_id(*p), island_id(p[0], neighbour(p[1], p[2], 1), p[2])) for p in PLACES]
YZ = [(y, h) for y in range(4) for h in range(2)]
Y0 = [(y * 2 + h, (y ^ 1) * 2 + h) for y, h in YZ]
Y1 = [(y * 2 + h, ((y + (1 if y % 2 else -1)) % 4) * 2 + h) for y, h in YZ]
H = [(y * 2 + h, y * 2 + (1 - h)) for y, h in YZ]


def hop(value, pairs, axis="island"):
    return lax.ppermute(value, axis, pairs)


WA, WB = 3456, 3456
VMEM = pl.BlockSpec(memory_space=pltpu.VMEM)
SMEM = pl.BlockSpec(memory_space=pltpu.SMEM)
HBM = pl.BlockSpec(memory_space=pltpu.HBM)


def diagonal():
    pairs = []
    for z, x, core in PLACES:
        pairs.append((island_id(z, x, core), island_id(z + 1, x + 2, core)))
    return pairs


ZX = diagonal()
FSDP_STEPS = ((Y0, "fsdp"), (Y1, "fsdp"), (H, "fsdp"))


def position():
    me = lax.axis_index("island")
    core, x, z = me & 1, (me >> 1) & (X - 1), me >> 3
    return core, z, ((x + 1 - core) >> 1) & 1, ((x + core) >> 1) & 1


def fragments(mine, kept):
    core, z, bit, peer_bit = position()
    flip = 0 if kept else 1
    if mine:
        return 2 * core + (z ^ flip), 2 * core + (bit ^ flip)
    return 2 * (1 - core) + (z ^ flip), 2 * (1 - core) + (peer_bit ^ flip)


def fetches(source, target, frags, sem):
    rows, width = source.shape[1:]
    copies = []
    for k in range(rows // 8):
        for j, (lo, size) in enumerate(((0, WA), (WA, width - WA))):
            block = (pl.ds(8 * k, 8), pl.ds(lo, size))
            copies.append(pltpu.make_async_copy(source.at[(frags[j], *block)], target.at[block], sem.at[2 * k + j]))
    return copies


def pick_kernel(kept, inner, out, sem):
    copies = fetches(inner, out, fragments(False, kept), sem)
    for copy in copies:
        copy.start()
    for copy in copies:
        copy.wait()


def pick(kept, inner):
    rows, width = inner.shape[1:]
    return pl.pallas_call(
        lambda *refs: pick_kernel(kept, *refs),
        out_shape=jax.ShapeDtypeStruct((rows, width), inner.dtype),
        in_specs=[HBM],
        out_specs=VMEM,
        scratch_shapes=[pltpu.SemaphoreType.DMA((8,))],
        compiler_params=pltpu.CompilerParams(vmem_limit_bytes=(44 if kept else 48) << 20),
        cost_estimate=pl.CostEstimate(flops=0, bytes_accessed=1024, transcendentals=0),
    )(inner)


def differ_kernel(kept, inner, anchor, diff, base, sem):
    frags = fragments(True, kept)
    copies = fetches(inner, diff, frags, sem.at[0]) + fetches(anchor, base, frags, sem.at[1])
    for copy in copies:
        copy.start()
    for copy in copies:
        copy.wait()
    for start in range(0, diff.shape[1], 128):
        cols = slice(start, start + 128)
        diff[:, cols] = base[:, cols] - diff[:, cols]


def differ(kept, inner, anchor):
    rows, width = inner.shape[1:]
    shape = jax.ShapeDtypeStruct((rows, width), inner.dtype)
    return pl.pallas_call(
        lambda *refs: differ_kernel(kept, *refs),
        out_shape=(shape, shape),
        in_specs=[HBM, HBM],
        out_specs=(VMEM, VMEM),
        scratch_shapes=[pltpu.SemaphoreType.DMA((2, 8))],
        compiler_params=pltpu.CompilerParams(vmem_limit_bytes=(44 if kept else 48) << 20),
        cost_estimate=pl.CostEstimate(flops=0, bytes_accessed=1024, transcendentals=0),
    )(inner, anchor)


def first_kernel(diff, base, got, a_r, bc_r, ab, c):
    for start in range(0, diff.shape[1], 128):
        cols = slice(start, start + 128)
        far = a_r[:, cols] if start < WA else bc_r[:, start - WA : start - WA + 128]
        value = diff[:, cols] + (base[:, cols] - got[:, cols]) + far
        if start < WA + WB:
            ab[:, cols] = value
        else:
            c[:, start - WA - WB : start - WA - WB + 128] = value


def second_kernel(ab, c, ab_r, c_r, a_out, b_out, c_out):
    for start in range(0, ab.shape[1], 128):
        cols = slice(start, start + 128)
        out, at = (a_out, start) if start < WA else (b_out, start - WA)
        out[:, at : at + 128] = ab[:, cols] + ab_r[:, cols]
    c_out[...] = c[...] + c_r[...]


def in_vmem(kernel, widths, *arrays):
    shapes = [jax.ShapeDtypeStruct((arrays[0].shape[0], w), jnp.float32) for w in widths]
    return pl.pallas_call(
        kernel,
        out_shape=tuple(shapes),
        in_specs=[VMEM] * len(arrays),
        out_specs=(VMEM,) * len(widths),
        compiler_params=pltpu.CompilerParams(vmem_limit_bytes=16 << 20),
        cost_estimate=pl.CostEstimate(flops=0, bytes_accessed=1024, transcendentals=0),
    )(*arrays)


def total_kernel(a, b, c, a_r, b_r, c_r, near, bc, sq):
    frags = fragments(True, True)
    sums = []
    for mine, got, lo in ((a, a_r, 0), (b, b_r, WA), (c, c_r, WA + WB)):
        size = mine.shape[1]
        part = jnp.zeros((mine.shape[0], 128), jnp.float32)
        for start in range(0, size, 128):
            value = mine[:, start : start + 128] + got[:, start : start + 128]
            near[:, lo + start : lo + start + 128] = value
            if lo:
                bc[:, lo - WA + start : lo - WA + start + 128] = value
            part = part + value * value
        sums.append(part)
    row = lax.broadcasted_iota(jnp.int32, (8, 128), 0)
    left, right = jnp.sum(sums[0]), jnp.sum(sums[1] + sums[2])
    sq[...] = jnp.where(row == frags[0], left, 0.0) + jnp.where(row == frags[1], right, 0.0)


def total(*pieces):
    rows = pieces[0].shape[0]
    width = sum(p.shape[1] for p in pieces[:3])
    shape = lambda *dims: jax.ShapeDtypeStruct(dims, jnp.float32)
    return pl.pallas_call(
        total_kernel,
        out_shape=(shape(rows, width), shape(rows, width - WA), shape(8, 128)),
        in_specs=[VMEM] * 6,
        out_specs=(VMEM,) * 3,
        compiler_params=pltpu.CompilerParams(vmem_limit_bytes=12 << 20),
        cost_estimate=pl.CostEstimate(flops=0, bytes_accessed=1024, transcendentals=0),
    )(*pieces)


def update_kernel(entries, islands, sq, *refs):
    sums, (anchor, momentum, out_a, out_m, va, vm, sem_in, sem_out) = refs[:4], refs[4:]
    width = anchor.shape[2]
    frags = [fragments(*which) for which in ((True, True), (False, True), (True, False), (False, False))]
    chunks = []
    for i in range(4):
        for j, (lo, hi) in enumerate(((0, WA), (WA, width))):
            middle = lo + (hi - lo) // 256 * 128
            for start, stop in ((lo, middle), (middle, hi)):
                chunks.append((i, frags[i][j], start, stop - start))

    def loads(n):
        i, frag, start, size = chunks[n]
        cols = pl.ds(start, size)
        return [
            pltpu.make_async_copy(anchor.at[frag, :, cols], va.at[i, :, cols], sem_in.at[0, n]),
            pltpu.make_async_copy(momentum.at[frag, :, cols], vm.at[i, :, cols], sem_in.at[1, n]),
        ]

    def stores(n):
        i, frag, start, size = chunks[n]
        cols = pl.ds(start, size)
        return [
            pltpu.make_async_copy(va.at[i, :, cols], out_a.at[frag, :, cols], sem_out.at[0, n]),
            pltpu.make_async_copy(vm.at[i, :, cols], out_m.at[frag, :, cols], sem_out.at[1, n]),
        ]

    for n in range(len(chunks)):
        for copy in loads(n):
            copy.start()
    for n, (i, frag, start, size) in enumerate(chunks):
        mean_sq = jnp.broadcast_to(sq[pl.ds(frag, 1), :], (8, 128)) * (1.0 / (islands * islands)) / entries
        factor = jnp.minimum(1.0, RMS_MAX / jnp.sqrt(mean_sq + EPS)) / islands
        for copy in loads(n):
            copy.wait()
        for at in range(start, start + size, 128):
            for row in range(0, 32, 8):
                block = (slice(row, row + 8), slice(at, at + 128))
                clipped = sums[i][block] * factor
                new_m = MU * vm[(i, *block)] + clipped
                va[(i, *block)] = va[(i, *block)] - LR * (clipped + MU * new_m)
                vm[(i, *block)] = new_m
        for copy in stores(n):
            copy.start()
    for n in range(len(chunks)):
        for copy in stores(n):
            copy.wait()


def update(sq, pieces, anchor, momentum, entries, islands):
    shape = jax.ShapeDtypeStruct(anchor.shape, anchor.dtype)
    total = anchor.size * 4
    any_spec = pl.BlockSpec(memory_space=pl.ANY)
    return pl.pallas_call(
        lambda *refs: update_kernel(entries, islands, *refs),
        out_shape=(shape, shape),
        in_specs=[VMEM] * 5 + [any_spec] * 2,
        out_specs=(HBM, HBM),
        scratch_shapes=[pltpu.VMEM(anchor.shape, jnp.float32)] * 2 + [pltpu.SemaphoreType.DMA((2, 16))] * 2,
        compiler_params=pltpu.CompilerParams(vmem_limit_bytes=40 << 20),
        cost_estimate=pl.CostEstimate(flops=2 * total, bytes_accessed=5 * total, transcendentals=0),
    )(sq, *pieces, anchor, momentum)


def on_device(inner, anchor, momentum):
    inner = inner[0]
    rows, width = anchor.shape[1:]
    islands = lax.axis_size("island")
    entries = rows * 8 * width
    order = []

    def turn(value):
        return lax.optimization_barrier((value, order[-1]))[0] if order else value

    def note(value):
        order.append(value)
        return value

    got_send = hop(pick(False, inner), CORE)
    diff_send, base_send = differ(False, inner, anchor)
    send = note(diff_send + (base_send - got_send))
    got_keep = hop(pick(True, turn(inner)), CORE)
    diff_keep, base_keep = differ(True, turn(inner), anchor)
    a_r, bc_r = hop(send[:, :WA], Z), hop(send[:, WA:], X0)
    ab, c = in_vmem(first_kernel, (WA + WB, width - WA - WB), diff_keep, base_keep, got_keep, a_r, bc_r)
    c_r, ab_r = hop(c, Z), hop(ab, X1)
    a, b, c = in_vmem(second_kernel, (WA, WB, width - WA - WB), ab, c, ab_r, c_r)
    b_r, a_r, c_r = hop(b, Z), hop(a, X0), hop(c, X1)
    near, bc, sq = total(a, b, c, a_r, b_r, c_r)
    note(sq)
    a_far, bc_far = hop(near[:, :WA], Z), hop(bc, X0)
    for k, step in enumerate(STEPS):
        if k == 1:
            near_peer = hop(turn(near), CORE)
        if k == 3:
            far = jnp.concatenate([turn(v) for v in (a_far, bc_far)], axis=1)
            far_peer = hop(far, CORE)
            note(far)
        sq = note(sq + turn(hop(turn(sq), *step)))
    return tuple(update(sq, [near, near_peer, far, far_peer], anchor, momentum, entries, islands))


STEPS = (*FSDP_STEPS[:2], (CORE, "island"), FSDP_STEPS[2], (ZX, "island"))


def solution(mesh):
    spec = P(None, "fsdp", None)
    return jax.shard_map(
        on_device,
        mesh=mesh,
        in_specs=(P("island", None, "fsdp", None), spec, spec),
        out_specs=(spec, spec),
        check_vma=False,
    )
```

time: 90.8 us -> 81.1 us (0.89)
  Pallas kernels: 20.4 us -> 15.4 us
  waiting for transfers between devices: 44.7 us -> 41.9 us
  other arithmetic: 2.1 us -> 0.2 us
  starting transfers between devices: 21.2 us -> 22.3 us
    pallas_call x3 -> x7, Pallas kernels: 19.5 us -> 15.1 us  [the longest x1 5.77 us: update(): pl.pallas_call(lambda *refs: update_kernel(entries, islands, *refs), out_...]
    ppermute x18, waiting for transfers between devices: 44.7 us -> 41.9 us  [hop(): return lax.ppermute(value, axis, pairs)]
    ppermute x18, starting transfers between devices: 21.2 us -> 22.3 us  [hop(): return lax.ppermute(value, axis, pairs)]
  transfers between devices with their start and end apart: 18 -> 18, of which waited for: 13 -> 13; matrix products, arithmetic and copies ran while one was open for 2% -> 0% of each run, Pallas kernels for 5% -> 7%
where the time goes in v3:
time: 81.1 us; the launch traced here: 80.9 us
  waiting for transfers between devices  41.9 us (52%)
  starting transfers between devices  22.3 us (27%)
  Pallas kernels  15.4 us (19%)
  between operations  0.82 us (1%)
    ppermute x18, waiting for transfers between devices, hop(): return lax.ppermute(value, axis, pairs)  41.9 us
    ppermute x18, starting transfers between devices, hop(): return lax.ppermute(value, axis, pairs)  22.3 us
    pallas_call x1, Pallas kernels, update(): pl.pallas_call(lambda *refs: update_kernel(entries, islands, *refs), out_...  5.77 us
    pallas_call x2, Pallas kernels, differ(): pl.pallas_call(lambda *refs: differ_kernel(kept, *refs), out_shape=(shape...  5.56 us
    pallas_call x2, Pallas kernels, pick(): pl.pallas_call(lambda *refs: pick_kernel(kept, *refs), out_shape=jax.Shap...  3.4 us
  transfers between devices with their start and end apart: 18, of which 13 were waited for; matrix products, arithmetic and copies ran while one was open for 0% of the time, Pallas kernels for 7%

profile of v3, /device:TPU:0, one launch (start us, length us, event | category | flops | bytes accessed | tf_op | source)
XLA Modules:
  0.0 80.9 jit_solution(1316227630860983718)
XLA Ops:
  0.6 1.6 %shard_map.51 = f32[32,10240]{1,0:T(8,128)S(1)} custom-call(f32[4,32,10240]{2,1,0:T(8,128)} %bitcast.1), custom_call_target="tpu_custom_call" | custom-call | bytes 1024 | tf_op jit(solution)/shard_map/pallas_call | solution.py:89
  2.4 2.2 %shard_map.50 = (f32[32,10240]{1,0:T(8,128)S(1)}, f32[32,10240]{1,0:T(8,128)S(1)}) custom-call(f32[4,32,10240]{2,1,0:T(8,128)} %bitcast.2, f32[4,32,10240]{2,1,0:T(8,128)} %refs_5_.1), custom_call_target="tpu_custom_call" | custom-call | bytes 1024 | tf_op jit(solution)/shard_map/pallas_call | solution.py:115
  4.6 0.8 collective-permute-done
  5.6 1.8 %shard_map.53 = f32[32,10240]{1,0:T(8,128)S(1)} custom-call(f32[4,32,10240]{2,1,0:T(8,128)S(1)} %bitcast.5), custom_call_target="tpu_custom_call" | custom-call | bytes 1024 | tf_op jit(solution)/shard_map/pallas_call | solution.py:89
  7.7 1.7 %collective-permute-start.3 = (f32[32,6784]{1,0:T(8,128)S(1)}, f32[32,6784]{1,0:T(8,128)S(1)}, u32[]{:S(2)}, u32[]{:S(2)}) collective-permute-start(f32[32,6784]{1,0:T(8,128)S(1)} %slice.13), channel_id=1, source_target_pairs={{0,16},{8,56},{16,0},{24,40},{32,48},{40,24},{48,32},{56,8},{64,80... | collective-permute-start | bytes 2605064 | tf_op jit(solution)/shard_map/ppermute | solution.py:35
  9.4 2.0 %collective-permute-start.2 = (f32[32,3456]{1,0:T(8,128)S(1)}, f32[32,3456]{1,0:T(8,128)S(1)}, u32[]{:S(2)}, u32[]{:S(2)}) collective-permute-start(f32[32,3456]{1,0:T(8,128)S(1)} %slice.12), channel_id=1, source_target_pairs={{0,64},{8,72},{16,80},{24,88},{32,96},{40,104},{48,112},{56,120},{... | collective-permute-start | bytes 1327112 | tf_op jit(solution)/shard_map/ppermute | solution.py:35
  11.4 3.3 %shard_map.52 = (f32[32,10240]{1,0:T(8,128)S(1)}, f32[32,10240]{1,0:T(8,128)S(1)}) custom-call(f32[4,32,10240]{2,1,0:T(8,128)S(1)} %bitcast.6, f32[4,32,10240]{2,1,0:T(8,128)} %refs_5_.1), custom_call_target="tpu_custom_call" | custom-call | bytes 1024 | tf_op jit(solution)/shard_map/pallas_call | solution.py:115
  14.7 7.3 %collective-permute-done.2.a_r = f32[32,3456]{1,0:T(8,128)S(1)} collective-permute-done((f32[32,3456]{1,0:T(8,128)S(1)}, f32[32,3456]{1,0:T(8,128)S(1)}, u32[]{:S(2)}, u32[]{:S(2)}) %collective-permute-start.2) | collective-permute-done | bytes 442400 | tf_op jit(solution)/shard_map/ppermute | solution.py:35
  22.0 0.2 shard_map.54
  22.2 1.6 %collective-permute-start.4 = (f32[32,6912]{1,0:T(8,128)S(1)}, f32[32,6912]{1,0:T(8,128)S(1)}, u32[]{:S(2)}, u32[]{:S(2)}) collective-permute-start(f32[32,6912]{1,0:T(8,128)S(1)} %get-tuple-element.33.ab), channel_id=1, source_target_pairs={{0,48},{8,24},{16,32},{24,8},{32,16},{40,56},{48,0},{56,40},{64,11... | collective-permute-start | bytes 2654216 | tf_op jit(solution)/shard_map/ppermute | solution.py:35
  23.9 1.8 %collective-permute-start.5 = (f32[32,3328]{1,0:T(8,128)S(1)}, f32[32,3328]{1,0:T(8,128)S(1)}, u32[]{:S(2)}, u32[]{:S(2)}) collective-permute-start(f32[32,3328]{1,0:T(8,128)S(1)} %get-tuple-element.34.c), channel_id=1, source_target_pairs={{0,64},{8,72},{16,80},{24,88},{32,96},{40,104},{48,112},{56,120},{... | collective-permute-start | bytes 1277960 | tf_op jit(solution)/shard_map/ppermute | solution.py:35
  25.7 9.3 %collective-permute-done.5.c_r = f32[32,3328]{1,0:T(8,128)S(1)} collective-permute-done((f32[32,3328]{1,0:T(8,128)S(1)}, f32[32,3328]{1,0:T(8,128)S(1)}, u32[]{:S(2)}, u32[]{:S(2)}) %collective-permute-start.5) | collective-permute-done | bytes 426016 | tf_op jit(solution)/shard_map/ppermute | solution.py:35
  35.0 1.6 %collective-permute-done.4.ab_r = f32[32,6912]{1,0:T(8,128)S(1)} collective-permute-done((f32[32,6912]{1,0:T(8,128)S(1)}, f32[32,6912]{1,0:T(8,128)S(1)}, u32[]{:S(2)}, u32[]{:S(2)}) %collective-permute-start.4) | collective-permute-done | bytes 884768 | tf_op jit(solution)/shard_map/ppermute | solution.py:35
  36.8 2.2 %collective-permute-start.7 = (f32[32,3456]{1,0:T(8,128)S(1)}, f32[32,3456]{1,0:T(8,128)S(1)}, u32[]{:S(2)}, u32[]{:S(2)}) collective-permute-start(f32[32,3456]{1,0:T(8,128)S(1)} %get-tuple-element.36.b), channel_id=1, source_target_pairs={{0,64},{8,72},{16,80},{24,88},{32,96},{40,104},{48,112},{56,120},{... | collective-permute-start | bytes 1327112 | tf_op jit(solution)/shard_map/ppermute | solution.py:35
  39.0 1.3 %collective-permute-start.8 = (f32[32,3328]{1,0:T(8,128)S(1)}, f32[32,3328]{1,0:T(8,128)S(1)}, u32[]{:S(2)}, u32[]{:S(2)}) collective-permute-start(f32[32,3328]{1,0:T(8,128)S(1)} %get-tuple-element.37.c), channel_id=1, source_target_pairs={{0,48},{8,24},{16,32},{24,8},{32,16},{40,56},{48,0},{56,40},{64,11... | collective-permute-start | bytes 1277960 | tf_op jit(solution)/shard_map/ppermute | solution.py:35
  40.3 8.1 %collective-permute-done.8.c_r = f32[32,3328]{1,0:T(8,128)S(1)} collective-permute-done((f32[32,3328]{1,0:T(8,128)S(1)}, f32[32,3328]{1,0:T(8,128)S(1)}, u32[]{:S(2)}, u32[]{:S(2)}) %collective-permute-start.8) | collective-permute-done | bytes 426016 | tf_op jit(solution)/shard_map/ppermute | solution.py:35
  48.3 1.3 %collective-permute-done.6.a_r = f32[32,3456]{1,0:T(8,128)S(1)} collective-permute-done((f32[32,3456]{1,0:T(8,128)S(1)}, f32[32,3456]{1,0:T(8,128)S(1)}, u32[]{:S(2)}, u32[]{:S(2)}) %collective-permute-start.6) | collective-permute-done | bytes 442400 | tf_op jit(solution)/shard_map/ppermute | solution.py:35
  49.6 0.3 shard_map.56
  50.0 0.8 %collective-permute-start.12 = (f32[32,3456]{1,0:T(8,128)S(1)}, f32[32,3456]{1,0:T(8,128)S(1)}, u32[]{:S(2)}, u32[]{:S(2)}) collective-permute-start(f32[32,3456]{1,0:T(8,128)S(1)} %slice.11), channel_id=1, source_target_pairs={{0,64},{8,72},{16,80},{24,88},{32,96},{40,104},{48,112},{56,120},{... | collective-permute-start | bytes 1327112 | tf_op jit(solution)/shard_map/ppermute | solution.py:35
  50.9 1.6 %collective-permute-start.9 = (f32[8,128]{1,0:T(8,128)S(1)}, f32[8,128]{1,0:T(8,128)S(1)}, u32[]{:S(2)}, u32[]{:S(2)}) collective-permute-start(f32[8,128]{1,0:T(8,128)S(1)} %get-tuple-element.39), channel_id=1, source_target_pairs={{0,2},{1,3},{2,0},{3,1},{4,6},{5,7},{6,4},{7,5},{8,10},{9,11},{10,... | collective-permute-start | bytes 12296 | tf_op jit(solution)/shard_map/ppermute | solution.py:35
  52.5 2.0 %collective-permute-done.9 = f32[8,128]{1,0:T(8,128)S(1)} collective-permute-done((f32[8,128]{1,0:T(8,128)S(1)}, f32[8,128]{1,0:T(8,128)S(1)}, u32[]{:S(2)}, u32[]{:S(2)}) %collective-permute-start.9) | collective-permute-done | bytes 4128 | tf_op jit(solution)/shard_map/ppermute | solution.py:35
  54.5 3.0 %collective-permute-start.10 = (f32[8,128]{1,0:T(8,128)S(1)}, f32[8,128]{1,0:T(8,128)S(1)}, u32[]{:S(2)}, u32[]{:S(2)}) collective-permute-start(f32[8,128]{1,0:T(8,128)S(1)} %add.19), channel_id=1, source_target_pairs={{0,6},{1,7},{2,4},{3,5},{4,2},{5,3},{6,0},{7,1},{8,14},{9,15},{10,... | collective-permute-start | bytes 12296 | tf_op jit(solution)/shard_map/ppermute | solution.py:35
  57.5 1.8 %collective-permute-done.10 = f32[8,128]{1,0:T(8,128)S(1)} collective-permute-done((f32[8,128]{1,0:T(8,128)S(1)}, f32[8,128]{1,0:T(8,128)S(1)}, u32[]{:S(2)}, u32[]{:S(2)}) %collective-permute-start.10) | collective-permute-done | bytes 4128 | tf_op jit(solution)/shard_map/ppermute | solution.py:35
  59.4 0.5 collective-permute-start.16
  59.9 0.7 collective-permute-done.11
  60.5 1.7 %collective-permute-done.12 = f32[32,3456]{1,0:T(8,128)S(1)} collective-permute-done((f32[32,3456]{1,0:T(8,128)S(1)}, f32[32,3456]{1,0:T(8,128)S(1)}, u32[]{:S(2)}, u32[]{:S(2)}) %collective-permute-start.12) | collective-permute-done | bytes 442400 | tf_op jit(solution)/shard_map/ppermute | solution.py:35
  62.3 1.4 %collective-permute-done.13 = f32[32,6784]{1,0:T(8,128)S(1)} collective-permute-done((f32[32,6784]{1,0:T(8,128)S(1)}, f32[32,6784]{1,0:T(8,128)S(1)}, u32[]{:S(2)}, u32[]{:S(2)}) %collective-permute-start.13) | collective-permute-done | bytes 868384 | tf_op jit(solution)/shard_map/ppermute | solution.py:35
  63.8 3.7 %collective-permute-start.14 = (f32[8,128]{1,0:T(8,128)S(1)}, f32[8,128]{1,0:T(8,128)S(1)}, u32[]{:S(2)}, u32[]{:S(2)}) collective-permute-start(f32[8,128]{1,0:T(8,128)S(1)} %add.21), channel_id=1, source_target_pairs={{0,1},{1,0},{2,3},{3,2},{4,5},{5,4},{6,7},{7,6},{8,9},{9,8},{10,11... | collective-permute-start | bytes 12296 | tf_op jit(solution)/shard_map/ppermute | solution.py:35
  67.5 1.6 %collective-permute-done.14 = f32[8,128]{1,0:T(8,128)S(1)} collective-permute-done((f32[8,128]{1,0:T(8,128)S(1)}, f32[8,128]{1,0:T(8,128)S(1)}, u32[]{:S(2)}, u32[]{:S(2)}) %collective-permute-start.14) | collective-permute-done | bytes 4128 | tf_op jit(solution)/shard_map/ppermute | solution.py:35
  69.1 1.6 %collective-permute-start.15 = (f32[8,128]{1,0:T(8,128)S(1)}, f32[8,128]{1,0:T(8,128)S(1)}, u32[]{:S(2)}, u32[]{:S(2)}) collective-permute-start(f32[8,128]{1,0:T(8,128)S(1)} %add.22), channel_id=1, source_target_pairs={{0,96},{8,104},{16,112},{24,120},{32,64},{40,72},{48,80},{56,88},{... | collective-permute-start | bytes 12296 | tf_op jit(solution)/shard_map/ppermute | solution.py:35
  70.6 4.5 %collective-permute-done.15 = f32[8,128]{1,0:T(8,128)S(1)} collective-permute-done((f32[8,128]{1,0:T(8,128)S(1)}, f32[8,128]{1,0:T(8,128)S(1)}, u32[]{:S(2)}, u32[]{:S(2)}) %collective-permute-start.15) | collective-permute-done | bytes 4128 | tf_op jit(solution)/shard_map/ppermute | solution.py:35
  75.1 5.8 %shard_map.57 = (f32[4,32,10240]{2,1,0:T(8,128)}, f32[4,32,10240]{2,1,0:T(8,128)}) custom-call(f32[8,128]{1,0:T(8,128)S(1)} %add.23.refs_0_, f32[32,10240]{1,0:T(8,128)S(1)} %get-tuple-element.53.refs_1_, f32[32,10240]{1,0:T(8,128)S(1)} %collective-permute-done.16.refs_2_, f32[32,10240]{1,0:T(8,128)S(1)} %constant_dynamic-update-slice_fusion.refs_3_, ...), custom_call_target="tpu_custom_call" | custom-call | flops 10485760 | bytes 26214400 | tf_op jit(solution)/shard_map/pallas_call | solution.py:242
  (33 shorter events, 1.2 us)
Async XLA Ops:
  0.6 5.0 %slice-start = ((s8[5242880]{0:T(1024)(128)(4,1)}), s8[4194304]{0:T(1024)(128)(4,1)S(1)}, s32[]{:S(2)}) async-start(s8[5242880]{0:T(1024)(128)(4,1)} %bitcast.3), calls=%async_computation | async-start | bytes 8388608
  2.3 3.3 %slice-start.1 = ((s8[5242880]{0:T(1024)(128)(4,1)}), s8[1048576]{0:T(1024)(128)(4,1)S(1)}, s32[]{:S(2)}) async-start(s8[5242880]{0:T(1024)(128)(4,1)} %bitcast.3), calls=%async_computation.1 | async-start | bytes 2097152
  2.3 3.1 %collective-permute-start = (f32[32,10240]{1,0:T(8,128)S(1)}, f32[32,10240]{1,0:T(8,128)S(1)}, u32[]{:S(2)}, u32[]{:S(2)}) collective-permute-start(f32[32,10240]{1,0:T(8,128)S(1)} %shard_map.51), channel_id=1, source_target_pairs={{0,8},{8,0},{16,24},{24,16},{32,40},{40,32},{48,56},{56,48},{64,72... | collective-permute-start | bytes 3932168 | tf_op jit(solution)/shard_map/ppermute | solution.py:35
  7.4 14.6 %collective-permute-start.1 = (f32[32,10240]{1,0:T(8,128)S(1)}, f32[32,10240]{1,0:T(8,128)S(1)}, u32[]{:S(2)}, u32[]{:S(2)}) collective-permute-start(f32[32,10240]{1,0:T(8,128)S(1)} %shard_map.53), channel_id=1, source_target_pairs={{0,8},{8,0},{16,24},{24,16},{32,40},{40,32},{48,56},{56,48},{64,72... | collective-permute-start | bytes 3932168 | tf_op jit(solution)/shard_map/ppermute | solution.py:35
  7.7 14.3 %collective-permute-start.3 = (f32[32,6784]{1,0:T(8,128)S(1)}, f32[32,6784]{1,0:T(8,128)S(1)}, u32[]{:S(2)}, u32[]{:S(2)}) collective-permute-start(f32[32,6784]{1,0:T(8,128)S(1)} %slice.13), channel_id=1, source_target_pairs={{0,16},{8,56},{16,0},{24,40},{32,48},{40,24},{48,32},{56,8},{64,80... | collective-permute-start | bytes 2605064 | tf_op jit(solution)/shard_map/ppermute | solution.py:35
  9.4 12.6 %collective-permute-start.2 = (f32[32,3456]{1,0:T(8,128)S(1)}, f32[32,3456]{1,0:T(8,128)S(1)}, u32[]{:S(2)}, u32[]{:S(2)}) collective-permute-start(f32[32,3456]{1,0:T(8,128)S(1)} %slice.12), channel_id=1, source_target_pairs={{0,64},{8,72},{16,80},{24,88},{32,96},{40,104},{48,112},{56,120},{... | collective-permute-start | bytes 1327112 | tf_op jit(solution)/shard_map/ppermute | solution.py:35
  22.0 53.1 %slice-start.2 = ((s8[5242880]{0:T(1024)(128)(4,1)}), s8[4194304]{0:T(1024)(128)(4,1)S(1)}, s32[]{:S(2)}) async-start(s8[5242880]{0:T(1024)(128)(4,1)} %bitcast.7), calls=%async_computation.2 | async-start | bytes 8388608
  22.2 14.3 %collective-permute-start.4 = (f32[32,6912]{1,0:T(8,128)S(1)}, f32[32,6912]{1,0:T(8,128)S(1)}, u32[]{:S(2)}, u32[]{:S(2)}) collective-permute-start(f32[32,6912]{1,0:T(8,128)S(1)} %get-tuple-element.33.ab), channel_id=1, source_target_pairs={{0,48},{8,24},{16,32},{24,8},{32,16},{40,56},{48,0},{56,40},{64,11... | collective-permute-start | bytes 2654216 | tf_op jit(solution)/shard_map/ppermute | solution.py:35
  23.9 51.2 %slice-start.3 = ((s8[5242880]{0:T(1024)(128)(4,1)}), s8[1048576]{0:T(1024)(128)(4,1)S(1)}, s32[]{:S(2)}) async-start(s8[5242880]{0:T(1024)(128)(4,1)} %bitcast.7), calls=%async_computation.3 | async-start | bytes 2097152
  23.9 11.1 %collective-permute-start.5 = (f32[32,3328]{1,0:T(8,128)S(1)}, f32[32,3328]{1,0:T(8,128)S(1)}, u32[]{:S(2)}, u32[]{:S(2)}) collective-permute-start(f32[32,3328]{1,0:T(8,128)S(1)} %get-tuple-element.34.c), channel_id=1, source_target_pairs={{0,64},{8,72},{16,80},{24,88},{32,96},{40,104},{48,112},{56,120},{... | collective-permute-start | bytes 1277960 | tf_op jit(solution)/shard_map/ppermute | solution.py:35
  36.7 12.9 %collective-permute-start.6 = (f32[32,3456]{1,0:T(8,128)S(1)}, f32[32,3456]{1,0:T(8,128)S(1)}, u32[]{:S(2)}, u32[]{:S(2)}) collective-permute-start(f32[32,3456]{1,0:T(8,128)S(1)} %get-tuple-element.35.a), channel_id=1, source_target_pairs={{0,16},{8,56},{16,0},{24,40},{32,48},{40,24},{48,32},{56,8},{64,80... | collective-permute-start | bytes 1327112 | tf_op jit(solution)/shard_map/ppermute | solution.py:35
  36.8 12.8 %collective-permute-start.7 = (f32[32,3456]{1,0:T(8,128)S(1)}, f32[32,3456]{1,0:T(8,128)S(1)}, u32[]{:S(2)}, u32[]{:S(2)}) collective-permute-start(f32[32,3456]{1,0:T(8,128)S(1)} %get-tuple-element.36.b), channel_id=1, source_target_pairs={{0,64},{8,72},{16,80},{24,88},{32,96},{40,104},{48,112},{56,120},{... | collective-permute-start | bytes 1327112 | tf_op jit(solution)/shard_map/ppermute | solution.py:35
  39.0 9.3 %collective-permute-start.8 = (f32[32,3328]{1,0:T(8,128)S(1)}, f32[32,3328]{1,0:T(8,128)S(1)}, u32[]{:S(2)}, u32[]{:S(2)}) collective-permute-start(f32[32,3328]{1,0:T(8,128)S(1)} %get-tuple-element.37.c), channel_id=1, source_target_pairs={{0,48},{8,24},{16,32},{24,8},{32,16},{40,56},{48,0},{56,40},{64,11... | collective-permute-start | bytes 1277960 | tf_op jit(solution)/shard_map/ppermute | solution.py:35
  50.0 12.3 %collective-permute-start.12 = (f32[32,3456]{1,0:T(8,128)S(1)}, f32[32,3456]{1,0:T(8,128)S(1)}, u32[]{:S(2)}, u32[]{:S(2)}) collective-permute-start(f32[32,3456]{1,0:T(8,128)S(1)} %slice.11), channel_id=1, source_target_pairs={{0,64},{8,72},{16,80},{24,88},{32,96},{40,104},{48,112},{56,120},{... | collective-permute-start | bytes 1327112 | tf_op jit(solution)/shard_map/ppermute | solution.py:35
  50.8 12.9 %collective-permute-start.13 = (f32[32,6784]{1,0:T(8,128)S(1)}, f32[32,6784]{1,0:T(8,128)S(1)}, u32[]{:S(2)}, u32[]{:S(2)}) collective-permute-start(f32[32,6784]{1,0:T(8,128)S(1)} %get-tuple-element.47), channel_id=1, source_target_pairs={{0,16},{8,56},{16,0},{24,40},{32,48},{40,24},{48,32},{56,8},{64,80... | collective-permute-start | bytes 2605064 | tf_op jit(solution)/shard_map/ppermute | solution.py:35
  50.9 3.6 %collective-permute-start.9 = (f32[8,128]{1,0:T(8,128)S(1)}, f32[8,128]{1,0:T(8,128)S(1)}, u32[]{:S(2)}, u32[]{:S(2)}) collective-permute-start(f32[8,128]{1,0:T(8,128)S(1)} %get-tuple-element.39), channel_id=1, source_target_pairs={{0,2},{1,3},{2,0},{3,1},{4,6},{5,7},{6,4},{7,5},{8,10},{9,11},{10,... | collective-permute-start | bytes 12296 | tf_op jit(solution)/shard_map/ppermute | solution.py:35
  54.5 4.8 %collective-permute-start.10 = (f32[8,128]{1,0:T(8,128)S(1)}, f32[8,128]{1,0:T(8,128)S(1)}, u32[]{:S(2)}, u32[]{:S(2)}) collective-permute-start(f32[8,128]{1,0:T(8,128)S(1)} %add.19), channel_id=1, source_target_pairs={{0,6},{1,7},{2,4},{3,5},{4,2},{5,3},{6,0},{7,1},{8,14},{9,15},{10,... | collective-permute-start | bytes 12296 | tf_op jit(solution)/shard_map/ppermute | solution.py:35
  59.4 1.2 %collective-permute-start.11 = (f32[8,128]{1,0:T(8,128)S(1)}, f32[8,128]{1,0:T(8,128)S(1)}, u32[]{:S(2)}, u32[]{:S(2)}) collective-permute-start(f32[8,128]{1,0:T(8,128)S(1)} %add.20), channel_id=1, source_target_pairs={{0,8},{8,0},{16,24},{24,16},{32,40},{40,32},{48,56},{56,48},{64,72... | collective-permute-start | bytes 12296 | tf_op jit(solution)/shard_map/ppermute | solution.py:35
  59.4 15.7 %collective-permute-start.16 = (f32[32,10240]{1,0:T(8,128)S(1)}, f32[32,10240]{1,0:T(8,128)S(1)}, u32[]{:S(2)}, u32[]{:S(2)}) collective-permute-start(f32[32,10240]{1,0:T(8,128)S(1)} %get-tuple-element.53.refs_1_), channel_id=1, source_target_pairs={{0,8},{8,0},{16,24},{24,16},{32,40},{40,32},{48,56},{56,48},{64,72... | collective-permute-start | bytes 3932168 | tf_op jit(solution)/shard_map/ppermute | solution.py:35
  63.7 11.4 %collective-permute-start.17 = (f32[32,10240]{1,0:T(8,128)S(1)}, f32[32,10240]{1,0:T(8,128)S(1)}, u32[]{:S(2)}, u32[]{:S(2)}) collective-permute-start(f32[32,10240]{1,0:T(8,128)S(1)} %constant_dynamic-update-slice_fusion.refs_3_), channel_id=1, source_target_pairs={{0,8},{8,0},{16,24},{24,16},{32,40},{40,32},{48,56},{56,48},{64,72... | collective-permute-start | bytes 3932168 | tf_op jit(solution)/shard_map/ppermute | solution.py:35
  63.8 5.2 %collective-permute-start.14 = (f32[8,128]{1,0:T(8,128)S(1)}, f32[8,128]{1,0:T(8,128)S(1)}, u32[]{:S(2)}, u32[]{:S(2)}) collective-permute-start(f32[8,128]{1,0:T(8,128)S(1)} %add.21), channel_id=1, source_target_pairs={{0,1},{1,0},{2,3},{3,2},{4,5},{5,4},{6,7},{7,6},{8,9},{9,8},{10,11... | collective-permute-start | bytes 12296 | tf_op jit(solution)/shard_map/ppermute | solution.py:35
  69.1 6.0 %collective-permute-start.15 = (f32[8,128]{1,0:T(8,128)S(1)}, f32[8,128]{1,0:T(8,128)S(1)}, u32[]{:S(2)}, u32[]{:S(2)}) collective-permute-start(f32[8,128]{1,0:T(8,128)S(1)} %add.22), channel_id=1, source_target_pairs={{0,96},{8,104},{16,112},{24,120},{32,64},{40,72},{48,80},{56,88},{... | collective-permute-start | bytes 12296 | tf_op jit(solution)/shard_map/ppermute | solution.py:35

commit v4 on v3

--- a/solution.py
+++ b/solution.py
@@ -28,7 +28,11 @@
 YZ = [(y, h) for y in range(4) for h in range(2)]
 Y0 = [(y * 2 + h, (y ^ 1) * 2 + h) for y, h in YZ]
 Y1 = [(y * 2 + h, ((y + (1 if y % 2 else -1)) % 4) * 2 + h) for y, h in YZ]
-H = [(y * 2 + h, y * 2 + (1 - h)) for y, h in YZ]
+ZZ = [
+    (island_id(z, x, core) * 8 + y * 2 + h, island_id(z + 1, x, core) * 8 + y * 2 + 1 - h)
+    for z, x, core in PLACES
+    for y, h in YZ
+]
 
 
 def hop(value, pairs, axis="island"):
@@ -49,7 +53,7 @@
 
 
 ZX = diagonal()
-FSDP_STEPS = ((Y0, "fsdp"), (Y1, "fsdp"), (H, "fsdp"))
+FSDP_STEPS = ((Y0, "fsdp"), (Y1, "fsdp"), (ZZ, ("island", "fsdp")))
 
 
 def position():
@@ -76,23 +80,25 @@
     return copies
 
 
-def pick_kernel(kept, inner, out, sem):
-    copies = fetches(inner, out, fragments(False, kept), sem)
+def pick_kernel(inner, send, keep, sem):
+    copies = fetches(inner, send, fragments(False, False), sem.at[0])
+    copies += fetches(inner, keep, fragments(False, True), sem.at[1])
     for copy in copies:
         copy.start()
     for copy in copies:
         copy.wait()
 
 
-def pick(kept, inner):
+def pick(inner):
     rows, width = inner.shape[1:]
-    return pl.pallas_call(
-        lambda *refs: pick_kernel(kept, *refs),
-        out_shape=jax.ShapeDtypeStruct((rows, width), inner.dtype),
+    shape = jax.ShapeDtypeStruct((rows, width), inner.dtype)
+    return pl.pallas_call(
+        pick_kernel,
+        out_shape=(shape, shape),
         in_specs=[HBM],
-        out_specs=VMEM,
-        scratch_shapes=[pltpu.SemaphoreType.DMA((8,))],
-        compiler_params=pltpu.CompilerParams(vmem_limit_bytes=(44 if kept else 48) << 20),
+        out_specs=(VMEM, VMEM),
+        scratch_shapes=[pltpu.SemaphoreType.DMA((2, 8))],
+        compiler_params=pltpu.CompilerParams(vmem_limit_bytes=48 << 20),
         cost_estimate=pl.CostEstimate(flops=0, bytes_accessed=1024, transcendentals=0),
     )(inner)
 
@@ -193,9 +199,7 @@
     chunks = []
     for i in range(4):
         for j, (lo, hi) in enumerate(((0, WA), (WA, width))):
-            middle = lo + (hi - lo) // 256 * 128
-            for start, stop in ((lo, middle), (middle, hi)):
-                chunks.append((i, frags[i][j], start, stop - start))
+            chunks.append((i, frags[i][j], lo, hi - lo))
 
     def loads(n):
         i, frag, start, size = chunks[n]
@@ -244,7 +248,7 @@
         out_shape=(shape, shape),
         in_specs=[VMEM] * 5 + [any_spec] * 2,
         out_specs=(HBM, HBM),
-        scratch_shapes=[pltpu.VMEM(anchor.shape, jnp.float32)] * 2 + [pltpu.SemaphoreType.DMA((2, 16))] * 2,
+        scratch_shapes=[pltpu.VMEM(anchor.shape, jnp.float32)] * 2 + [pltpu.SemaphoreType.DMA((2, 8))] * 2,
         compiler_params=pltpu.CompilerParams(vmem_limit_bytes=40 << 20),
         cost_estimate=pl.CostEstimate(flops=2 * total, bytes_accessed=5 * total, transcendentals=0),
     )(sq, *pieces, anchor, momentum)
@@ -264,10 +268,10 @@
         order.append(value)
         return value
 
-    got_send = hop(pick(False, inner), CORE)
+    send, keep = pick(inner)
+    got_send, got_keep = hop(send, CORE), hop(keep, CORE)
     diff_send, base_send = differ(False, inner, anchor)
     send = note(diff_send + (base_send - got_send))
-    got_keep = hop(pick(True, turn(inner)), CORE)
     diff_keep, base_keep = differ(True, turn(inner), anchor)
     a_r, bc_r = hop(send[:, :WA], Z), hop(send[:, WA:], X0)
     ab, c = in_vmem(first_kernel, (WA + WB, width - WA - WB), diff_keep, base_keep, got_keep, a_r, bc_r)
@@ -280,7 +284,7 @@
     for k, step in enumerate(STEPS):
         if k == 1:
             near_peer = hop(turn(near), CORE)
-        if k == 3:
+        if k == 4:
             far = jnp.concatenate([turn(v) for v in (a_far, bc_far)], axis=1)
             far_peer = hop(far, CORE)
             note(far)
@@ -288,7 +292,7 @@
     return tuple(update(sq, [near, near_peer, far, far_peer], anchor, momentum, entries, islands))
 
 
-STEPS = (*FSDP_STEPS[:2], (CORE, "island"), FSDP_STEPS[2], (ZX, "island"))
+STEPS = (*FSDP_STEPS, (CORE, "island"), (ZX, "island"))
 
 
 def solution(mesh):

time: 81.1 us -> 76.5 us (0.943)
  waiting for transfers between devices: 41.9 us -> 37.9 us
  Pallas kernels: 15.4 us -> 13.7 us
  starting transfers between devices: 22.3 us -> 23.3 us
    ppermute x18, waiting for transfers between devices: 41.9 us -> 37.9 us  [hop(): return lax.ppermute(value, axis, pairs)]
    pallas_call x2 -> x1, Pallas kernels: 3.4 us -> 2.08 us  [pick(): pl.pallas_call(pick_kernel, out_shape=(shape, shape), in_specs=[HBM], out...]
    ppermute x18, starting transfers between devices: 22.3 us -> 23.3 us  [hop(): return lax.ppermute(value, axis, pairs)]
  transfers between devices with their start and end apart: 18 -> 18, of which waited for: 13 -> 11; matrix products, arithmetic and copies ran while one was open for 0% -> 0% of each run, Pallas kernels for 7% -> 7%
where the time goes in v4:
time: 76.5 us; the launch traced here: 76.1 us
  waiting for transfers between devices  37.9 us (50%)
  starting transfers between devices  23.3 us (30%)
  Pallas kernels  13.7 us (18%)
  between operations  0.8 us (1%)
    ppermute x18, waiting for transfers between devices, hop(): return lax.ppermute(value, axis, pairs)  37.9 us
    ppermute x18, starting transfers between devices, hop(): return lax.ppermute(value, axis, pairs)  23.3 us
    pallas_call x1, Pallas kernels, update(): pl.pallas_call(lambda *refs: update_kernel(entries, islands, *refs), out_...  5.55 us
    pallas_call x2, Pallas kernels, differ(): pl.pallas_call(lambda *refs: differ_kernel(kept, *refs), out_shape=(shape...  5.39 us
    pallas_call x1, Pallas kernels, pick(): pl.pallas_call(pick_kernel, out_shape=(shape, shape), in_specs=[HBM], out...  2.08 us
  transfers between devices with their start and end apart: 18, of which 11 were waited for; matrix products, arithmetic and copies ran while one was open for 0% of the time, Pallas kernels for 7%

profile of v4, /device:TPU:0, one launch (start us, length us, event | category | flops | bytes accessed | tf_op | source)
XLA Modules:
  0.0 76.1 jit_solution(13134544529735799633)
XLA Ops:
  0.6 2.1 %shard_map.51 = (f32[32,10240]{1,0:T(8,128)S(1)}, f32[32,10240]{1,0:T(8,128)S(1)}) custom-call(f32[4,32,10240]{2,1,0:T(8,128)} %bitcast.1), custom_call_target="tpu_custom_call" | custom-call | bytes 1024 | tf_op jit(solution)/shard_map/pallas_call | solution.py:95
  2.8 0.5 collective-permute-start.1
  3.3 2.1 %shard_map.50 = (f32[32,10240]{1,0:T(8,128)S(1)}, f32[32,10240]{1,0:T(8,128)S(1)}) custom-call(f32[4,32,10240]{2,1,0:T(8,128)} %bitcast.2, f32[4,32,10240]{2,1,0:T(8,128)} %refs_5_.1), custom_call_target="tpu_custom_call" | custom-call | bytes 1024 | tf_op jit(solution)/shard_map/pallas_call | solution.py:121
  5.4 0.5 collective-permute-done
  5.8 0.2 subtract_add_fusion
  6.1 1.7 %collective-permute-start.3 = (f32[32,6784]{1,0:T(8,128)S(1)}, f32[32,6784]{1,0:T(8,128)S(1)}, u32[]{:S(2)}, u32[]{:S(2)}) collective-permute-start(f32[32,6784]{1,0:T(8,128)S(1)} %slice.13), channel_id=1, source_target_pairs={{0,16},{8,56},{16,0},{24,40},{32,48},{40,24},{48,32},{56,8},{64,80... | collective-permute-start | bytes 2605064 | tf_op jit(solution)/shard_map/ppermute | solution.py:39
  7.8 2.0 %collective-permute-start.2 = (f32[32,3456]{1,0:T(8,128)S(1)}, f32[32,3456]{1,0:T(8,128)S(1)}, u32[]{:S(2)}, u32[]{:S(2)}) collective-permute-start(f32[32,3456]{1,0:T(8,128)S(1)} %slice.12), channel_id=1, source_target_pairs={{0,64},{8,72},{16,80},{24,88},{32,96},{40,104},{48,112},{56,120},{... | collective-permute-start | bytes 1327112 | tf_op jit(solution)/shard_map/ppermute | solution.py:39
  9.8 3.3 %shard_map.52 = (f32[32,10240]{1,0:T(8,128)S(1)}, f32[32,10240]{1,0:T(8,128)S(1)}) custom-call(f32[4,32,10240]{2,1,0:T(8,128)S(1)} %bitcast.5, f32[4,32,10240]{2,1,0:T(8,128)} %refs_5_.1), custom_call_target="tpu_custom_call" | custom-call | bytes 1024 | tf_op jit(solution)/shard_map/pallas_call | solution.py:121
  13.1 7.4 %collective-permute-done.2.a_r = f32[32,3456]{1,0:T(8,128)S(1)} collective-permute-done((f32[32,3456]{1,0:T(8,128)S(1)}, f32[32,3456]{1,0:T(8,128)S(1)}, u32[]{:S(2)}, u32[]{:S(2)}) %collective-permute-start.2) | collective-permute-done | bytes 442400 | tf_op jit(solution)/shard_map/ppermute | solution.py:39
  20.6 0.2 shard_map.53
  20.8 1.4 %collective-permute-start.4 = (f32[32,6912]{1,0:T(8,128)S(1)}, f32[32,6912]{1,0:T(8,128)S(1)}, u32[]{:S(2)}, u32[]{:S(2)}) collective-permute-start(f32[32,6912]{1,0:T(8,128)S(1)} %get-tuple-element.37.ab), channel_id=1, source_target_pairs={{0,48},{8,24},{16,32},{24,8},{32,16},{40,56},{48,0},{56,40},{64,11... | collective-permute-start | bytes 2654216 | tf_op jit(solution)/shard_map/ppermute | solution.py:39
  22.2 1.9 %collective-permute-start.5 = (f32[32,3328]{1,0:T(8,128)S(1)}, f32[32,3328]{1,0:T(8,128)S(1)}, u32[]{:S(2)}, u32[]{:S(2)}) collective-permute-start(f32[32,3328]{1,0:T(8,128)S(1)} %get-tuple-element.38.c), channel_id=1, source_target_pairs={{0,64},{8,72},{16,80},{24,88},{32,96},{40,104},{48,112},{56,120},{... | collective-permute-start | bytes 1277960 | tf_op jit(solution)/shard_map/ppermute | solution.py:39
  24.1 9.1 %collective-permute-done.5.c_r = f32[32,3328]{1,0:T(8,128)S(1)} collective-permute-done((f32[32,3328]{1,0:T(8,128)S(1)}, f32[32,3328]{1,0:T(8,128)S(1)}, u32[]{:S(2)}, u32[]{:S(2)}) %collective-permute-start.5) | collective-permute-done | bytes 426016 | tf_op jit(solution)/shard_map/ppermute | solution.py:39
  33.2 2.0 %collective-permute-done.4.ab_r = f32[32,6912]{1,0:T(8,128)S(1)} collective-permute-done((f32[32,6912]{1,0:T(8,128)S(1)}, f32[32,6912]{1,0:T(8,128)S(1)}, u32[]{:S(2)}, u32[]{:S(2)}) %collective-permute-start.4) | collective-permute-done | bytes 884768 | tf_op jit(solution)/shard_map/ppermute | solution.py:39
  35.4 2.2 %collective-permute-start.7 = (f32[32,3456]{1,0:T(8,128)S(1)}, f32[32,3456]{1,0:T(8,128)S(1)}, u32[]{:S(2)}, u32[]{:S(2)}) collective-permute-start(f32[32,3456]{1,0:T(8,128)S(1)} %get-tuple-element.40.b), channel_id=1, source_target_pairs={{0,64},{8,72},{16,80},{24,88},{32,96},{40,104},{48,112},{56,120},{... | collective-permute-start | bytes 1327112 | tf_op jit(solution)/shard_map/ppermute | solution.py:39
  37.6 1.1 %collective-permute-start.8 = (f32[32,3328]{1,0:T(8,128)S(1)}, f32[32,3328]{1,0:T(8,128)S(1)}, u32[]{:S(2)}, u32[]{:S(2)}) collective-permute-start(f32[32,3328]{1,0:T(8,128)S(1)} %get-tuple-element.41.c), channel_id=1, source_target_pairs={{0,48},{8,24},{16,32},{24,8},{32,16},{40,56},{48,0},{56,40},{64,11... | collective-permute-start | bytes 1277960 | tf_op jit(solution)/shard_map/ppermute | solution.py:39
  38.7 8.2 %collective-permute-done.8.c_r = f32[32,3328]{1,0:T(8,128)S(1)} collective-permute-done((f32[32,3328]{1,0:T(8,128)S(1)}, f32[32,3328]{1,0:T(8,128)S(1)}, u32[]{:S(2)}, u32[]{:S(2)}) %collective-permute-start.8) | collective-permute-done | bytes 426016 | tf_op jit(solution)/shard_map/ppermute | solution.py:39
  46.9 1.2 %collective-permute-done.6.a_r = f32[32,3456]{1,0:T(8,128)S(1)} collective-permute-done((f32[32,3456]{1,0:T(8,128)S(1)}, f32[32,3456]{1,0:T(8,128)S(1)}, u32[]{:S(2)}, u32[]{:S(2)}) %collective-permute-start.6) | collective-permute-done | bytes 442400 | tf_op jit(solution)/shard_map/ppermute | solution.py:39
  48.1 0.3 shard_map.55
  48.4 0.6 collective-permute-start.13
  49.1 1.6 %collective-permute-start.9 = (f32[8,128]{1,0:T(8,128)S(1)}, f32[8,128]{1,0:T(8,128)S(1)}, u32[]{:S(2)}, u32[]{:S(2)}) collective-permute-start(f32[8,128]{1,0:T(8,128)S(1)} %get-tuple-element.43), channel_id=1, source_target_pairs={{0,2},{1,3},{2,0},{3,1},{4,6},{5,7},{6,4},{7,5},{8,10},{9,11},{10,... | collective-permute-start | bytes 12296 | tf_op jit(solution)/shard_map/ppermute | solution.py:39
  50.7 2.0 %collective-permute-done.9 = f32[8,128]{1,0:T(8,128)S(1)} collective-permute-done((f32[8,128]{1,0:T(8,128)S(1)}, f32[8,128]{1,0:T(8,128)S(1)}, u32[]{:S(2)}, u32[]{:S(2)}) %collective-permute-start.9) | collective-permute-done | bytes 4128 | tf_op jit(solution)/shard_map/ppermute | solution.py:39
  52.8 3.0 %collective-permute-start.10 = (f32[8,128]{1,0:T(8,128)S(1)}, f32[8,128]{1,0:T(8,128)S(1)}, u32[]{:S(2)}, u32[]{:S(2)}) collective-permute-start(f32[8,128]{1,0:T(8,128)S(1)} %add.19), channel_id=1, source_target_pairs={{0,6},{1,7},{2,4},{3,5},{4,2},{5,3},{6,0},{7,1},{8,14},{9,15},{10,... | collective-permute-start | bytes 12296 | tf_op jit(solution)/shard_map/ppermute | solution.py:39
  55.8 1.8 %collective-permute-done.10 = f32[8,128]{1,0:T(8,128)S(1)} collective-permute-done((f32[8,128]{1,0:T(8,128)S(1)}, f32[8,128]{1,0:T(8,128)S(1)}, u32[]{:S(2)}, u32[]{:S(2)}) %collective-permute-start.10) | collective-permute-done | bytes 4128 | tf_op jit(solution)/shard_map/ppermute | solution.py:39
  57.6 3.8 %collective-permute-start.11 = (f32[8,128]{1,0:T(8,128)S(1)}, f32[8,128]{1,0:T(8,128)S(1)}, u32[]{:S(2)}, u32[]{:S(2)}) collective-permute-start(f32[8,128]{1,0:T(8,128)S(1)} %add.20), channel_id=1, source_target_pairs={{0,65},{1,64},{2,67},{3,66},{4,69},{5,68},{6,71},{7,70},{8,73},{9,... | collective-permute-start | bytes 12296 | tf_op jit(solution)/shard_map/ppermute | solution.py:39
  61.4 1.6 %collective-permute-done.11 = f32[8,128]{1,0:T(8,128)S(1)} collective-permute-done((f32[8,128]{1,0:T(8,128)S(1)}, f32[8,128]{1,0:T(8,128)S(1)}, u32[]{:S(2)}, u32[]{:S(2)}) %collective-permute-start.11) | collective-permute-done | bytes 4128 | tf_op jit(solution)/shard_map/ppermute | solution.py:39
  63.0 0.5 collective-permute-start.16
  63.5 0.7 collective-permute-done.12
  64.3 0.2 collective-permute-start.17
  64.5 2.4 %collective-permute-start.15 = (f32[8,128]{1,0:T(8,128)S(1)}, f32[8,128]{1,0:T(8,128)S(1)}, u32[]{:S(2)}, u32[]{:S(2)}) collective-permute-start(f32[8,128]{1,0:T(8,128)S(1)} %add.22), channel_id=1, source_target_pairs={{0,96},{8,104},{16,112},{24,120},{32,64},{40,72},{48,80},{56,88},{... | collective-permute-start | bytes 12296 | tf_op jit(solution)/shard_map/ppermute | solution.py:39
  67.0 3.6 %collective-permute-done.15 = f32[8,128]{1,0:T(8,128)S(1)} collective-permute-done((f32[8,128]{1,0:T(8,128)S(1)}, f32[8,128]{1,0:T(8,128)S(1)}, u32[]{:S(2)}, u32[]{:S(2)}) %collective-permute-start.15) | collective-permute-done | bytes 4128 | tf_op jit(solution)/shard_map/ppermute | solution.py:39
  70.6 5.5 %shard_map.56 = (f32[4,32,10240]{2,1,0:T(8,128)}, f32[4,32,10240]{2,1,0:T(8,128)}) custom-call(f32[8,128]{1,0:T(8,128)S(1)} %add.23.refs_0_, f32[32,10240]{1,0:T(8,128)S(1)} %get-tuple-element.57.refs_1_, f32[32,10240]{1,0:T(8,128)S(1)} %collective-permute-done.16.refs_2_, f32[32,10240]{1,0:T(8,128)S(1)} %constant_dynamic-update-slice_fusion.refs_3_, ...), custom_call_target="tpu_custom_call" | custom-call | flops 10485760 | bytes 26214400 | tf_op jit(solution)/shard_map/pallas_call | solution.py:246
  (32 shorter events, 0.6 us)
Async XLA Ops:
  0.6 9.2 %slice-start = ((s8[5242880]{0:T(1024)(128)(4,1)}), s8[4194304]{0:T(1024)(128)(4,1)S(1)}, s32[]{:S(2)}) async-start(s8[5242880]{0:T(1024)(128)(4,1)} %bitcast.3), calls=%async_computation | async-start | bytes 8388608
  2.7 3.1 %collective-permute-start = (f32[32,10240]{1,0:T(8,128)S(1)}, f32[32,10240]{1,0:T(8,128)S(1)}, u32[]{:S(2)}, u32[]{:S(2)}) collective-permute-start(f32[32,10240]{1,0:T(8,128)S(1)} %get-tuple-element.32), channel_id=1, source_target_pairs={{0,8},{8,0},{16,24},{24,16},{32,40},{40,32},{48,56},{56,48},{64,72... | collective-permute-start | bytes 3932168 | tf_op jit(solution)/shard_map/ppermute | solution.py:39
  2.8 7.0 %slice-start.1 = ((s8[5242880]{0:T(1024)(128)(4,1)}), s8[1048576]{0:T(1024)(128)(4,1)S(1)}, s32[]{:S(2)}) async-start(s8[5242880]{0:T(1024)(128)(4,1)} %bitcast.3), calls=%async_computation.1 | async-start | bytes 2097152
  2.8 10.3 %collective-permute-start.1 = (f32[32,10240]{1,0:T(8,128)S(1)}, f32[32,10240]{1,0:T(8,128)S(1)}, u32[]{:S(2)}, u32[]{:S(2)}) collective-permute-start(f32[32,10240]{1,0:T(8,128)S(1)} %get-tuple-element.36), channel_id=1, source_target_pairs={{0,8},{8,0},{16,24},{24,16},{32,40},{40,32},{48,56},{56,48},{64,72... | collective-permute-start | bytes 3932168 | tf_op jit(solution)/shard_map/ppermute | solution.py:39
  6.1 14.5 %collective-permute-start.3 = (f32[32,6784]{1,0:T(8,128)S(1)}, f32[32,6784]{1,0:T(8,128)S(1)}, u32[]{:S(2)}, u32[]{:S(2)}) collective-permute-start(f32[32,6784]{1,0:T(8,128)S(1)} %slice.13), channel_id=1, source_target_pairs={{0,16},{8,56},{16,0},{24,40},{32,48},{40,24},{48,32},{56,8},{64,80... | collective-permute-start | bytes 2605064 | tf_op jit(solution)/shard_map/ppermute | solution.py:39
  7.8 12.8 %collective-permute-start.2 = (f32[32,3456]{1,0:T(8,128)S(1)}, f32[32,3456]{1,0:T(8,128)S(1)}, u32[]{:S(2)}, u32[]{:S(2)}) collective-permute-start(f32[32,3456]{1,0:T(8,128)S(1)} %slice.12), channel_id=1, source_target_pairs={{0,64},{8,72},{16,80},{24,88},{32,96},{40,104},{48,112},{56,120},{... | collective-permute-start | bytes 1327112 | tf_op jit(solution)/shard_map/ppermute | solution.py:39
  20.6 50.0 %slice-start.2 = ((s8[5242880]{0:T(1024)(128)(4,1)}), s8[4194304]{0:T(1024)(128)(4,1)S(1)}, s32[]{:S(2)}) async-start(s8[5242880]{0:T(1024)(128)(4,1)} %bitcast.6), calls=%async_computation.2 | async-start | bytes 8388608
  20.8 14.3 %collective-permute-start.4 = (f32[32,6912]{1,0:T(8,128)S(1)}, f32[32,6912]{1,0:T(8,128)S(1)}, u32[]{:S(2)}, u32[]{:S(2)}) collective-permute-start(f32[32,6912]{1,0:T(8,128)S(1)} %get-tuple-element.37.ab), channel_id=1, source_target_pairs={{0,48},{8,24},{16,32},{24,8},{32,16},{40,56},{48,0},{56,40},{64,11... | collective-permute-start | bytes 2654216 | tf_op jit(solution)/shard_map/ppermute | solution.py:39
  22.2 48.4 %slice-start.3 = ((s8[5242880]{0:T(1024)(128)(4,1)}), s8[1048576]{0:T(1024)(128)(4,1)S(1)}, s32[]{:S(2)}) async-start(s8[5242880]{0:T(1024)(128)(4,1)} %bitcast.6), calls=%async_computation.3 | async-start | bytes 2097152
  22.2 11.0 %collective-permute-start.5 = (f32[32,3328]{1,0:T(8,128)S(1)}, f32[32,3328]{1,0:T(8,128)S(1)}, u32[]{:S(2)}, u32[]{:S(2)}) collective-permute-start(f32[32,3328]{1,0:T(8,128)S(1)} %get-tuple-element.38.c), channel_id=1, source_target_pairs={{0,64},{8,72},{16,80},{24,88},{32,96},{40,104},{48,112},{56,120},{... | collective-permute-start | bytes 1277960 | tf_op jit(solution)/shard_map/ppermute | solution.py:39
  35.3 12.8 %collective-permute-start.6 = (f32[32,3456]{1,0:T(8,128)S(1)}, f32[32,3456]{1,0:T(8,128)S(1)}, u32[]{:S(2)}, u32[]{:S(2)}) collective-permute-start(f32[32,3456]{1,0:T(8,128)S(1)} %get-tuple-element.39.a), channel_id=1, source_target_pairs={{0,16},{8,56},{16,0},{24,40},{32,48},{40,24},{48,32},{56,8},{64,80... | collective-permute-start | bytes 1327112 | tf_op jit(solution)/shard_map/ppermute | solution.py:39
  35.4 12.7 %collective-permute-start.7 = (f32[32,3456]{1,0:T(8,128)S(1)}, f32[32,3456]{1,0:T(8,128)S(1)}, u32[]{:S(2)}, u32[]{:S(2)}) collective-permute-start(f32[32,3456]{1,0:T(8,128)S(1)} %get-tuple-element.40.b), channel_id=1, source_target_pairs={{0,64},{8,72},{16,80},{24,88},{32,96},{40,104},{48,112},{56,120},{... | collective-permute-start | bytes 1327112 | tf_op jit(solution)/shard_map/ppermute | solution.py:39
  37.6 9.3 %collective-permute-start.8 = (f32[32,3328]{1,0:T(8,128)S(1)}, f32[32,3328]{1,0:T(8,128)S(1)}, u32[]{:S(2)}, u32[]{:S(2)}) collective-permute-start(f32[32,3328]{1,0:T(8,128)S(1)} %get-tuple-element.41.c), channel_id=1, source_target_pairs={{0,48},{8,24},{16,32},{24,8},{32,16},{40,56},{48,0},{56,40},{64,11... | collective-permute-start | bytes 1277960 | tf_op jit(solution)/shard_map/ppermute | solution.py:39
  48.4 15.7 %collective-permute-start.13 = (f32[32,3456]{1,0:T(8,128)S(1)}, f32[32,3456]{1,0:T(8,128)S(1)}, u32[]{:S(2)}, u32[]{:S(2)}) collective-permute-start(f32[32,3456]{1,0:T(8,128)S(1)} %slice.11), channel_id=1, source_target_pairs={{0,64},{8,72},{16,80},{24,88},{32,96},{40,104},{48,112},{56,120},{... | collective-permute-start | bytes 1327112 | tf_op jit(solution)/shard_map/ppermute | solution.py:39
  49.1 15.1 %collective-permute-start.14 = (f32[32,6784]{1,0:T(8,128)S(1)}, f32[32,6784]{1,0:T(8,128)S(1)}, u32[]{:S(2)}, u32[]{:S(2)}) collective-permute-start(f32[32,6784]{1,0:T(8,128)S(1)} %get-tuple-element.53), channel_id=1, source_target_pairs={{0,16},{8,56},{16,0},{24,40},{32,48},{40,24},{48,32},{56,8},{64,80... | collective-permute-start | bytes 2605064 | tf_op jit(solution)/shard_map/ppermute | solution.py:39
  49.1 3.6 %collective-permute-start.9 = (f32[8,128]{1,0:T(8,128)S(1)}, f32[8,128]{1,0:T(8,128)S(1)}, u32[]{:S(2)}, u32[]{:S(2)}) collective-permute-start(f32[8,128]{1,0:T(8,128)S(1)} %get-tuple-element.43), channel_id=1, source_target_pairs={{0,2},{1,3},{2,0},{3,1},{4,6},{5,7},{6,4},{7,5},{8,10},{9,11},{10,... | collective-permute-start | bytes 12296 | tf_op jit(solution)/shard_map/ppermute | solution.py:39
  52.8 4.8 %collective-permute-start.10 = (f32[8,128]{1,0:T(8,128)S(1)}, f32[8,128]{1,0:T(8,128)S(1)}, u32[]{:S(2)}, u32[]{:S(2)}) collective-permute-start(f32[8,128]{1,0:T(8,128)S(1)} %add.19), channel_id=1, source_target_pairs={{0,6},{1,7},{2,4},{3,5},{4,2},{5,3},{6,0},{7,1},{8,14},{9,15},{10,... | collective-permute-start | bytes 12296 | tf_op jit(solution)/shard_map/ppermute | solution.py:39
  57.6 5.4 %collective-permute-start.11 = (f32[8,128]{1,0:T(8,128)S(1)}, f32[8,128]{1,0:T(8,128)S(1)}, u32[]{:S(2)}, u32[]{:S(2)}) collective-permute-start(f32[8,128]{1,0:T(8,128)S(1)} %add.20), channel_id=1, source_target_pairs={{0,65},{1,64},{2,67},{3,66},{4,69},{5,68},{6,71},{7,70},{8,73},{9,... | collective-permute-start | bytes 12296 | tf_op jit(solution)/shard_map/ppermute | solution.py:39
  63.0 1.2 %collective-permute-start.12 = (f32[8,128]{1,0:T(8,128)S(1)}, f32[8,128]{1,0:T(8,128)S(1)}, u32[]{:S(2)}, u32[]{:S(2)}) collective-permute-start(f32[8,128]{1,0:T(8,128)S(1)} %add.21), channel_id=1, source_target_pairs={{0,8},{8,0},{16,24},{24,16},{32,40},{40,32},{48,56},{56,48},{64,72... | collective-permute-start | bytes 12296 | tf_op jit(solution)/shard_map/ppermute | solution.py:39
  63.0 7.5 %collective-permute-start.16 = (f32[32,10240]{1,0:T(8,128)S(1)}, f32[32,10240]{1,0:T(8,128)S(1)}, u32[]{:S(2)}, u32[]{:S(2)}) collective-permute-start(f32[32,10240]{1,0:T(8,128)S(1)} %get-tuple-element.57.refs_1_), channel_id=1, source_target_pairs={{0,8},{8,0},{16,24},{24,16},{32,40},{40,32},{48,56},{56,48},{64,72... | collective-permute-start | bytes 3932168 | tf_op jit(solution)/shard_map/ppermute | solution.py:39
  64.3 6.3 %collective-permute-start.17 = (f32[32,10240]{1,0:T(8,128)S(1)}, f32[32,10240]{1,0:T(8,128)S(1)}, u32[]{:S(2)}, u32[]{:S(2)}) collective-permute-start(f32[32,10240]{1,0:T(8,128)S(1)} %constant_dynamic-update-slice_fusion.refs_3_), channel_id=1, source_target_pairs={{0,8},{8,0},{16,24},{24,16},{32,40},{40,32},{48,56},{56,48},{64,72... | collective-permute-start | bytes 3932168 | tf_op jit(solution)/shard_map/ppermute | solution.py:39
  64.5 6.0 %collective-permute-start.15 = (f32[8,128]{1,0:T(8,128)S(1)}, f32[8,128]{1,0:T(8,128)S(1)}, u32[]{:S(2)}, u32[]{:S(2)}) collective-permute-start(f32[8,128]{1,0:T(8,128)S(1)} %add.22), channel_id=1, source_target_pairs={{0,96},{8,104},{16,112},{24,120},{32,64},{40,72},{48,80},{56,88},{... | collective-permute-start | bytes 12296 | tf_op jit(solution)/shard_map/ppermute | solution.py:39

commit v5 on v4

--- a/solution.py
+++ b/solution.py
@@ -80,53 +80,54 @@
     return copies
 
 
-def pick_kernel(inner, send, keep, sem):
-    copies = fetches(inner, send, fragments(False, False), sem.at[0])
-    copies += fetches(inner, keep, fragments(False, True), sem.at[1])
+def run(copies):
     for copy in copies:
         copy.start()
     for copy in copies:
         copy.wait()
 
 
-def pick(inner):
-    rows, width = inner.shape[1:]
-    shape = jax.ShapeDtypeStruct((rows, width), inner.dtype)
-    return pl.pallas_call(
-        pick_kernel,
-        out_shape=(shape, shape),
-        in_specs=[HBM],
-        out_specs=(VMEM, VMEM),
-        scratch_shapes=[pltpu.SemaphoreType.DMA((2, 8))],
-        compiler_params=pltpu.CompilerParams(vmem_limit_bytes=48 << 20),
-        cost_estimate=pl.CostEstimate(flops=0, bytes_accessed=1024, transcendentals=0),
-    )(inner)
-
-
-def differ_kernel(kept, inner, anchor, diff, base, sem):
-    frags = fragments(True, kept)
+def subtract(base, diff):
+    for start in range(0, diff.shape[1], 128):
+        cols = slice(start, start + 128)
+        diff[:, cols] = base[:, cols] - diff[:, cols]
+
+
+def pick_kernel(inner, send, sem):
+    run(fetches(inner, send, fragments(False, False), sem.at[0]))
+
+
+def send_kernel(inner, anchor, diff, base, keep, sem):
+    frags = fragments(True, False)
+    kept = fetches(inner, keep, fragments(False, True), sem.at[2])
     copies = fetches(inner, diff, frags, sem.at[0]) + fetches(anchor, base, frags, sem.at[1])
-    for copy in copies:
+    for copy in copies + kept:
         copy.start()
     for copy in copies:
         copy.wait()
-    for start in range(0, diff.shape[1], 128):
-        cols = slice(start, start + 128)
-        diff[:, cols] = base[:, cols] - diff[:, cols]
-
-
-def differ(kept, inner, anchor):
-    rows, width = inner.shape[1:]
-    shape = jax.ShapeDtypeStruct((rows, width), inner.dtype)
+    subtract(base, diff)
+    for copy in kept:
+        copy.wait()
+
+
+def keep_kernel(inner, anchor, diff, base, sem):
+    frags = fragments(True, True)
+    run(fetches(inner, diff, frags, sem.at[0]) + fetches(anchor, base, frags, sem.at[1]))
+    subtract(base, diff)
+
+
+def fetch(kernel, count, mib, *arrays):
+    rows, width = arrays[0].shape[1:]
+    shape = jax.ShapeDtypeStruct((rows, width), jnp.float32)
     return pl.pallas_call(
-        lambda *refs: differ_kernel(kept, *refs),
-        out_shape=(shape, shape),
-        in_specs=[HBM, HBM],
-        out_specs=(VMEM, VMEM),
-        scratch_shapes=[pltpu.SemaphoreType.DMA((2, 8))],
-        compiler_params=pltpu.CompilerParams(vmem_limit_bytes=(44 if kept else 48) << 20),
+        kernel,
+        out_shape=(shape,) * count,
+        in_specs=[HBM] * len(arrays),
+        out_specs=(VMEM,) * count,
+        scratch_shapes=[pltpu.SemaphoreType.DMA((3, 8))],
+        compiler_params=pltpu.CompilerParams(vmem_limit_bytes=mib << 20),
         cost_estimate=pl.CostEstimate(flops=0, bytes_accessed=1024, transcendentals=0),
-    )(inner, anchor)
+    )(*arrays)
 
 
 def first_kernel(diff, base, got, a_r, bc_r, ab, c):
@@ -268,11 +269,12 @@
         order.append(value)
         return value
 
-    send, keep = pick(inner)
-    got_send, got_keep = hop(send, CORE), hop(keep, CORE)
-    diff_send, base_send = differ(False, inner, anchor)
+    (send,) = fetch(pick_kernel, 1, 48, inner)
+    got_send = hop(send, CORE)
+    diff_send, base_send, keep = fetch(send_kernel, 3, 46, inner, anchor)
+    got_keep = hop(keep, CORE)
     send = note(diff_send + (base_send - got_send))
-    diff_keep, base_keep = differ(True, turn(inner), anchor)
+    diff_keep, base_keep = fetch(keep_kernel, 2, 50, turn(inner), anchor)
     a_r, bc_r = hop(send[:, :WA], Z), hop(send[:, WA:], X0)
     ab, c = in_vmem(first_kernel, (WA + WB, width - WA - WB), diff_keep, base_keep, got_keep, a_r, bc_r)
     c_r, ab_r = hop(c, Z), hop(ab, X1)

time: 76.5 us -> 76 us (level)
  Pallas kernels: 13.7 us -> 12.4 us
  waiting for transfers between devices: 37.9 us -> 38.7 us
    pallas_call x3, Pallas kernels: 7.47 us -> 6.15 us  [fetch(): pl.pallas_call(kernel, out_shape=(shape,) * count, in_specs=[HBM] * len(a...]
    ppermute x18, waiting for transfers between devices: 37.9 us -> 38.7 us  [hop(): return lax.ppermute(value, axis, pairs)]
  transfers between devices with their start and end apart: 18 -> 18, of which waited for: 11 -> 10; matrix products, arithmetic and copies ran while one was open for 0% -> 1% of each run, Pallas kernels for 7% -> 6%
where the time goes in v5:
time: 76 us; the launch traced here: 75.7 us
  waiting for transfers between devices  38.7 us (51%)
  starting transfers between devices  23.3 us (31%)
  Pallas kernels  12.4 us (16%)
  between operations  0.78 us (1%)
    ppermute x18, waiting for transfers between devices, hop(): return lax.ppermute(value, axis, pairs)  38.7 us
    ppermute x18, starting transfers between devices, hop(): return lax.ppermute(value, axis, pairs)  23.3 us
    pallas_call x3, Pallas kernels, fetch(): pl.pallas_call(kernel, out_shape=(shape,) * count, in_specs=[HBM] * len(a...  6.15 us
    pallas_call x1, Pallas kernels, update(): pl.pallas_call(lambda *refs: update_kernel(entries, islands, *refs), out_...  5.55 us
  transfers between devices with their start and end apart: 18, of which 10 were waited for; matrix products, arithmetic and copies ran while one was open for 1% of the time, Pallas kernels for 6%

profile of v5, /device:TPU:0, one launch (start us, length us, event | category | flops | bytes accessed | tf_op | source)
XLA Modules:
  0.0 75.7 jit_solution(15275740850282623980)
XLA Ops:
  0.6 1.6 %shard_map.51 = f32[32,10240]{1,0:T(8,128)S(1)} custom-call(f32[4,32,10240]{2,1,0:T(8,128)} %bitcast.3), custom_call_target="tpu_custom_call" | custom-call | bytes 1024 | tf_op jit(solution)/shard_map/pallas_call | solution.py:122
  2.3 2.4 %shard_map.50 = (f32[32,10240]{1,0:T(8,128)S(1)}, f32[32,10240]{1,0:T(8,128)S(1)}, f32[32,10240]{1,0:T(8,128)S(1)}) custom-call(f32[4,32,10240]{2,1,0:T(8,128)} %bitcast.4, f32[4,32,10240]{2,1,0:T(8,128)} %refs_5_.1), custom_call_target="tpu_custom_call" | custom-call | bytes 1024 | tf_op jit(solution)/shard_map/pallas_call | solution.py:122
  4.8 0.6 collective-permute-start.1
  5.4 0.2 subtract_add_fusion
  5.6 1.7 %collective-permute-start.3 = (f32[32,6784]{1,0:T(8,128)S(1)}, f32[32,6784]{1,0:T(8,128)S(1)}, u32[]{:S(2)}, u32[]{:S(2)}) collective-permute-start(f32[32,6784]{1,0:T(8,128)S(1)} %slice.13), channel_id=1, source_target_pairs={{0,16},{8,56},{16,0},{24,40},{32,48},{40,24},{48,32},{56,8},{64,80... | collective-permute-start | bytes 2605064 | tf_op jit(solution)/shard_map/ppermute | solution.py:39
  7.3 2.0 %collective-permute-start.2 = (f32[32,3456]{1,0:T(8,128)S(1)}, f32[32,3456]{1,0:T(8,128)S(1)}, u32[]{:S(2)}, u32[]{:S(2)}) collective-permute-start(f32[32,3456]{1,0:T(8,128)S(1)} %slice.12), channel_id=1, source_target_pairs={{0,64},{8,72},{16,80},{24,88},{32,96},{40,104},{48,112},{56,120},{... | collective-permute-start | bytes 1327112 | tf_op jit(solution)/shard_map/ppermute | solution.py:39
  9.3 2.1 %shard_map.52 = (f32[32,10240]{1,0:T(8,128)S(1)}, f32[32,10240]{1,0:T(8,128)S(1)}) custom-call(f32[4,32,10240]{2,1,0:T(8,128)} %bitcast.5, f32[4,32,10240]{2,1,0:T(8,128)} %refs_5_.1), custom_call_target="tpu_custom_call" | custom-call | bytes 1024 | tf_op jit(solution)/shard_map/pallas_call | solution.py:122
  11.4 8.7 %collective-permute-done.2.a_r = f32[32,3456]{1,0:T(8,128)S(1)} collective-permute-done((f32[32,3456]{1,0:T(8,128)S(1)}, f32[32,3456]{1,0:T(8,128)S(1)}, u32[]{:S(2)}, u32[]{:S(2)}) %collective-permute-start.2) | collective-permute-done | bytes 442400 | tf_op jit(solution)/shard_map/ppermute | solution.py:39
  20.1 0.2 shard_map.53
  20.4 1.4 %collective-permute-start.4 = (f32[32,6912]{1,0:T(8,128)S(1)}, f32[32,6912]{1,0:T(8,128)S(1)}, u32[]{:S(2)}, u32[]{:S(2)}) collective-permute-start(f32[32,6912]{1,0:T(8,128)S(1)} %get-tuple-element.35.ab), channel_id=1, source_target_pairs={{0,48},{8,24},{16,32},{24,8},{32,16},{40,56},{48,0},{56,40},{64,11... | collective-permute-start | bytes 2654216 | tf_op jit(solution)/shard_map/ppermute | solution.py:39
  21.7 1.9 %collective-permute-start.5 = (f32[32,3328]{1,0:T(8,128)S(1)}, f32[32,3328]{1,0:T(8,128)S(1)}, u32[]{:S(2)}, u32[]{:S(2)}) collective-permute-start(f32[32,3328]{1,0:T(8,128)S(1)} %get-tuple-element.36.c), channel_id=1, source_target_pairs={{0,64},{8,72},{16,80},{24,88},{32,96},{40,104},{48,112},{56,120},{... | collective-permute-start | bytes 1277960 | tf_op jit(solution)/shard_map/ppermute | solution.py:39
  23.7 9.1 %collective-permute-done.5.c_r = f32[32,3328]{1,0:T(8,128)S(1)} collective-permute-done((f32[32,3328]{1,0:T(8,128)S(1)}, f32[32,3328]{1,0:T(8,128)S(1)}, u32[]{:S(2)}, u32[]{:S(2)}) %collective-permute-start.5) | collective-permute-done | bytes 426016 | tf_op jit(solution)/shard_map/ppermute | solution.py:39
  32.7 2.0 %collective-permute-done.4.ab_r = f32[32,6912]{1,0:T(8,128)S(1)} collective-permute-done((f32[32,6912]{1,0:T(8,128)S(1)}, f32[32,6912]{1,0:T(8,128)S(1)}, u32[]{:S(2)}, u32[]{:S(2)}) %collective-permute-start.4) | collective-permute-done | bytes 884768 | tf_op jit(solution)/shard_map/ppermute | solution.py:39
  34.7 0.1 shard_map.54
  34.9 2.2 %collective-permute-start.7 = (f32[32,3456]{1,0:T(8,128)S(1)}, f32[32,3456]{1,0:T(8,128)S(1)}, u32[]{:S(2)}, u32[]{:S(2)}) collective-permute-start(f32[32,3456]{1,0:T(8,128)S(1)} %get-tuple-element.38.b), channel_id=1, source_target_pairs={{0,64},{8,72},{16,80},{24,88},{32,96},{40,104},{48,112},{56,120},{... | collective-permute-start | bytes 1327112 | tf_op jit(solution)/shard_map/ppermute | solution.py:39
  37.1 1.1 %collective-permute-start.8 = (f32[32,3328]{1,0:T(8,128)S(1)}, f32[32,3328]{1,0:T(8,128)S(1)}, u32[]{:S(2)}, u32[]{:S(2)}) collective-permute-start(f32[32,3328]{1,0:T(8,128)S(1)} %get-tuple-element.39.c), channel_id=1, source_target_pairs={{0,48},{8,24},{16,32},{24,8},{32,16},{40,56},{48,0},{56,40},{64,11... | collective-permute-start | bytes 1277960 | tf_op jit(solution)/shard_map/ppermute | solution.py:39
  38.2 8.2 %collective-permute-done.8.c_r = f32[32,3328]{1,0:T(8,128)S(1)} collective-permute-done((f32[32,3328]{1,0:T(8,128)S(1)}, f32[32,3328]{1,0:T(8,128)S(1)}, u32[]{:S(2)}, u32[]{:S(2)}) %collective-permute-start.8) | collective-permute-done | bytes 426016 | tf_op jit(solution)/shard_map/ppermute | solution.py:39
  46.4 1.2 %collective-permute-done.6.a_r = f32[32,3456]{1,0:T(8,128)S(1)} collective-permute-done((f32[32,3456]{1,0:T(8,128)S(1)}, f32[32,3456]{1,0:T(8,128)S(1)}, u32[]{:S(2)}, u32[]{:S(2)}) %collective-permute-start.6) | collective-permute-done | bytes 442400 | tf_op jit(solution)/shard_map/ppermute | solution.py:39
  47.6 0.3 shard_map.55
  48.0 0.6 collective-permute-start.13
  48.7 1.6 %collective-permute-start.9 = (f32[8,128]{1,0:T(8,128)S(1)}, f32[8,128]{1,0:T(8,128)S(1)}, u32[]{:S(2)}, u32[]{:S(2)}) collective-permute-start(f32[8,128]{1,0:T(8,128)S(1)} %get-tuple-element.41), channel_id=1, source_target_pairs={{0,2},{1,3},{2,0},{3,1},{4,6},{5,7},{6,4},{7,5},{8,10},{9,11},{10,... | collective-permute-start | bytes 12296 | tf_op jit(solution)/shard_map/ppermute | solution.py:39
  50.2 2.0 %collective-permute-done.9 = f32[8,128]{1,0:T(8,128)S(1)} collective-permute-done((f32[8,128]{1,0:T(8,128)S(1)}, f32[8,128]{1,0:T(8,128)S(1)}, u32[]{:S(2)}, u32[]{:S(2)}) %collective-permute-start.9) | collective-permute-done | bytes 4128 | tf_op jit(solution)/shard_map/ppermute | solution.py:39
  52.3 3.0 %collective-permute-start.10 = (f32[8,128]{1,0:T(8,128)S(1)}, f32[8,128]{1,0:T(8,128)S(1)}, u32[]{:S(2)}, u32[]{:S(2)}) collective-permute-start(f32[8,128]{1,0:T(8,128)S(1)} %add.19), channel_id=1, source_target_pairs={{0,6},{1,7},{2,4},{3,5},{4,2},{5,3},{6,0},{7,1},{8,14},{9,15},{10,... | collective-permute-start | bytes 12296 | tf_op jit(solution)/shard_map/ppermute | solution.py:39
  55.3 1.8 %collective-permute-done.10 = f32[8,128]{1,0:T(8,128)S(1)} collective-permute-done((f32[8,128]{1,0:T(8,128)S(1)}, f32[8,128]{1,0:T(8,128)S(1)}, u32[]{:S(2)}, u32[]{:S(2)}) %collective-permute-start.10) | collective-permute-done | bytes 4128 | tf_op jit(solution)/shard_map/ppermute | solution.py:39
  57.1 3.8 %collective-permute-start.11 = (f32[8,128]{1,0:T(8,128)S(1)}, f32[8,128]{1,0:T(8,128)S(1)}, u32[]{:S(2)}, u32[]{:S(2)}) collective-permute-start(f32[8,128]{1,0:T(8,128)S(1)} %add.20), channel_id=1, source_target_pairs={{0,65},{1,64},{2,67},{3,66},{4,69},{5,68},{6,71},{7,70},{8,73},{9,... | collective-permute-start | bytes 12296 | tf_op jit(solution)/shard_map/ppermute | solution.py:39
  60.9 1.6 %collective-permute-done.11 = f32[8,128]{1,0:T(8,128)S(1)} collective-permute-done((f32[8,128]{1,0:T(8,128)S(1)}, f32[8,128]{1,0:T(8,128)S(1)}, u32[]{:S(2)}, u32[]{:S(2)}) %collective-permute-start.11) | collective-permute-done | bytes 4128 | tf_op jit(solution)/shard_map/ppermute | solution.py:39
  62.5 0.5 collective-permute-start.16
  63.0 0.7 collective-permute-done.12
  63.8 0.2 collective-permute-start.17
  64.1 2.4 %collective-permute-start.15 = (f32[8,128]{1,0:T(8,128)S(1)}, f32[8,128]{1,0:T(8,128)S(1)}, u32[]{:S(2)}, u32[]{:S(2)}) collective-permute-start(f32[8,128]{1,0:T(8,128)S(1)} %add.22), channel_id=1, source_target_pairs={{0,96},{8,104},{16,112},{24,120},{32,64},{40,72},{48,80},{56,88},{... | collective-permute-start | bytes 12296 | tf_op jit(solution)/shard_map/ppermute | solution.py:39
  66.5 3.6 %collective-permute-done.15 = f32[8,128]{1,0:T(8,128)S(1)} collective-permute-done((f32[8,128]{1,0:T(8,128)S(1)}, f32[8,128]{1,0:T(8,128)S(1)}, u32[]{:S(2)}, u32[]{:S(2)}) %collective-permute-start.15) | collective-permute-done | bytes 4128 | tf_op jit(solution)/shard_map/ppermute | solution.py:39
  70.1 5.5 %shard_map.56 = (f32[4,32,10240]{2,1,0:T(8,128)}, f32[4,32,10240]{2,1,0:T(8,128)}) custom-call(f32[8,128]{1,0:T(8,128)S(1)} %add.23.refs_0_, f32[32,10240]{1,0:T(8,128)S(1)} %get-tuple-element.55.refs_1_, f32[32,10240]{1,0:T(8,128)S(1)} %collective-permute-done.16.refs_2_, f32[32,10240]{1,0:T(8,128)S(1)} %constant_dynamic-update-slice_fusion.refs_3_, ...), custom_call_target="tpu_custom_call" | custom-call | flops 10485760 | bytes 26214400 | tf_op jit(solution)/shard_map/pallas_call | solution.py:247
  (27 shorter events, 0.5 us)
Async XLA Ops:
  2.3 3.1 %collective-permute-start = (f32[32,10240]{1,0:T(8,128)S(1)}, f32[32,10240]{1,0:T(8,128)S(1)}, u32[]{:S(2)}, u32[]{:S(2)}) collective-permute-start(f32[32,10240]{1,0:T(8,128)S(1)} %shard_map.51), channel_id=1, source_target_pairs={{0,8},{8,0},{16,24},{24,16},{32,40},{40,32},{48,56},{56,48},{64,72... | collective-permute-start | bytes 3932168 | tf_op jit(solution)/shard_map/ppermute | solution.py:39
  4.8 6.7 %collective-permute-start.1 = (f32[32,10240]{1,0:T(8,128)S(1)}, f32[32,10240]{1,0:T(8,128)S(1)}, u32[]{:S(2)}, u32[]{:S(2)}) collective-permute-start(f32[32,10240]{1,0:T(8,128)S(1)} %get-tuple-element.34), channel_id=1, source_target_pairs={{0,8},{8,0},{16,24},{24,16},{32,40},{40,32},{48,56},{56,48},{64,72... | collective-permute-start | bytes 3932168 | tf_op jit(solution)/shard_map/ppermute | solution.py:39
  5.6 14.5 %collective-permute-start.3 = (f32[32,6784]{1,0:T(8,128)S(1)}, f32[32,6784]{1,0:T(8,128)S(1)}, u32[]{:S(2)}, u32[]{:S(2)}) collective-permute-start(f32[32,6784]{1,0:T(8,128)S(1)} %slice.13), channel_id=1, source_target_pairs={{0,16},{8,56},{16,0},{24,40},{32,48},{40,24},{48,32},{56,8},{64,80... | collective-permute-start | bytes 2605064 | tf_op jit(solution)/shard_map/ppermute | solution.py:39
  7.3 12.8 %collective-permute-start.2 = (f32[32,3456]{1,0:T(8,128)S(1)}, f32[32,3456]{1,0:T(8,128)S(1)}, u32[]{:S(2)}, u32[]{:S(2)}) collective-permute-start(f32[32,3456]{1,0:T(8,128)S(1)} %slice.12), channel_id=1, source_target_pairs={{0,64},{8,72},{16,80},{24,88},{32,96},{40,104},{48,112},{56,120},{... | collective-permute-start | bytes 1327112 | tf_op jit(solution)/shard_map/ppermute | solution.py:39
  20.1 50.0 %slice-start = ((s8[5242880]{0:T(1024)(128)(4,1)}), s8[4194304]{0:T(1024)(128)(4,1)S(1)}, s32[]{:S(2)}) async-start(s8[5242880]{0:T(1024)(128)(4,1)} %bitcast.1), calls=%async_computation | async-start | bytes 8388608
  20.4 14.3 %collective-permute-start.4 = (f32[32,6912]{1,0:T(8,128)S(1)}, f32[32,6912]{1,0:T(8,128)S(1)}, u32[]{:S(2)}, u32[]{:S(2)}) collective-permute-start(f32[32,6912]{1,0:T(8,128)S(1)} %get-tuple-element.35.ab), channel_id=1, source_target_pairs={{0,48},{8,24},{16,32},{24,8},{32,16},{40,56},{48,0},{56,40},{64,11... | collective-permute-start | bytes 2654216 | tf_op jit(solution)/shard_map/ppermute | solution.py:39
  21.7 48.4 %slice-start.1 = ((s8[5242880]{0:T(1024)(128)(4,1)}), s8[1048576]{0:T(1024)(128)(4,1)S(1)}, s32[]{:S(2)}) async-start(s8[5242880]{0:T(1024)(128)(4,1)} %bitcast.1), calls=%async_computation.1 | async-start | bytes 2097152
  21.7 11.0 %collective-permute-start.5 = (f32[32,3328]{1,0:T(8,128)S(1)}, f32[32,3328]{1,0:T(8,128)S(1)}, u32[]{:S(2)}, u32[]{:S(2)}) collective-permute-start(f32[32,3328]{1,0:T(8,128)S(1)} %get-tuple-element.36.c), channel_id=1, source_target_pairs={{0,64},{8,72},{16,80},{24,88},{32,96},{40,104},{48,112},{56,120},{... | collective-permute-start | bytes 1277960 | tf_op jit(solution)/shard_map/ppermute | solution.py:39
  34.8 12.8 %collective-permute-start.6 = (f32[32,3456]{1,0:T(8,128)S(1)}, f32[32,3456]{1,0:T(8,128)S(1)}, u32[]{:S(2)}, u32[]{:S(2)}) collective-permute-start(f32[32,3456]{1,0:T(8,128)S(1)} %get-tuple-element.37.a), channel_id=1, source_target_pairs={{0,16},{8,56},{16,0},{24,40},{32,48},{40,24},{48,32},{56,8},{64,80... | collective-permute-start | bytes 1327112 | tf_op jit(solution)/shard_map/ppermute | solution.py:39
  34.9 12.7 %collective-permute-start.7 = (f32[32,3456]{1,0:T(8,128)S(1)}, f32[32,3456]{1,0:T(8,128)S(1)}, u32[]{:S(2)}, u32[]{:S(2)}) collective-permute-start(f32[32,3456]{1,0:T(8,128)S(1)} %get-tuple-element.38.b), channel_id=1, source_target_pairs={{0,64},{8,72},{16,80},{24,88},{32,96},{40,104},{48,112},{56,120},{... | collective-permute-start | bytes 1327112 | tf_op jit(solution)/shard_map/ppermute | solution.py:39
  37.1 9.3 %collective-permute-start.8 = (f32[32,3328]{1,0:T(8,128)S(1)}, f32[32,3328]{1,0:T(8,128)S(1)}, u32[]{:S(2)}, u32[]{:S(2)}) collective-permute-start(f32[32,3328]{1,0:T(8,128)S(1)} %get-tuple-element.39.c), channel_id=1, source_target_pairs={{0,48},{8,24},{16,32},{24,8},{32,16},{40,56},{48,0},{56,40},{64,11... | collective-permute-start | bytes 1277960 | tf_op jit(solution)/shard_map/ppermute | solution.py:39
  48.0 15.7 %collective-permute-start.13 = (f32[32,3456]{1,0:T(8,128)S(1)}, f32[32,3456]{1,0:T(8,128)S(1)}, u32[]{:S(2)}, u32[]{:S(2)}) collective-permute-start(f32[32,3456]{1,0:T(8,128)S(1)} %slice.11), channel_id=1, source_target_pairs={{0,64},{8,72},{16,80},{24,88},{32,96},{40,104},{48,112},{56,120},{... | collective-permute-start | bytes 1327112 | tf_op jit(solution)/shard_map/ppermute | solution.py:39
  48.6 15.1 %collective-permute-start.14 = (f32[32,6784]{1,0:T(8,128)S(1)}, f32[32,6784]{1,0:T(8,128)S(1)}, u32[]{:S(2)}, u32[]{:S(2)}) collective-permute-start(f32[32,6784]{1,0:T(8,128)S(1)} %get-tuple-element.51), channel_id=1, source_target_pairs={{0,16},{8,56},{16,0},{24,40},{32,48},{40,24},{48,32},{56,8},{64,80... | collective-permute-start | bytes 2605064 | tf_op jit(solution)/shard_map/ppermute | solution.py:39
  48.7 3.6 %collective-permute-start.9 = (f32[8,128]{1,0:T(8,128)S(1)}, f32[8,128]{1,0:T(8,128)S(1)}, u32[]{:S(2)}, u32[]{:S(2)}) collective-permute-start(f32[8,128]{1,0:T(8,128)S(1)} %get-tuple-element.41), channel_id=1, source_target_pairs={{0,2},{1,3},{2,0},{3,1},{4,6},{5,7},{6,4},{7,5},{8,10},{9,11},{10,... | collective-permute-start | bytes 12296 | tf_op jit(solution)/shard_map/ppermute | solution.py:39
  52.3 4.8 %collective-permute-start.10 = (f32[8,128]{1,0:T(8,128)S(1)}, f32[8,128]{1,0:T(8,128)S(1)}, u32[]{:S(2)}, u32[]{:S(2)}) collective-permute-start(f32[8,128]{1,0:T(8,128)S(1)} %add.19), channel_id=1, source_target_pairs={{0,6},{1,7},{2,4},{3,5},{4,2},{5,3},{6,0},{7,1},{8,14},{9,15},{10,... | collective-permute-start | bytes 12296 | tf_op jit(solution)/shard_map/ppermute | solution.py:39
  57.1 5.4 %collective-permute-start.11 = (f32[8,128]{1,0:T(8,128)S(1)}, f32[8,128]{1,0:T(8,128)S(1)}, u32[]{:S(2)}, u32[]{:S(2)}) collective-permute-start(f32[8,128]{1,0:T(8,128)S(1)} %add.20), channel_id=1, source_target_pairs={{0,65},{1,64},{2,67},{3,66},{4,69},{5,68},{6,71},{7,70},{8,73},{9,... | collective-permute-start | bytes 12296 | tf_op jit(solution)/shard_map/ppermute | solution.py:39
  62.5 1.2 %collective-permute-start.12 = (f32[8,128]{1,0:T(8,128)S(1)}, f32[8,128]{1,0:T(8,128)S(1)}, u32[]{:S(2)}, u32[]{:S(2)}) collective-permute-start(f32[8,128]{1,0:T(8,128)S(1)} %add.21), channel_id=1, source_target_pairs={{0,8},{8,0},{16,24},{24,16},{32,40},{40,32},{48,56},{56,48},{64,72... | collective-permute-start | bytes 12296 | tf_op jit(solution)/shard_map/ppermute | solution.py:39
  62.5 7.5 %collective-permute-start.16 = (f32[32,10240]{1,0:T(8,128)S(1)}, f32[32,10240]{1,0:T(8,128)S(1)}, u32[]{:S(2)}, u32[]{:S(2)}) collective-permute-start(f32[32,10240]{1,0:T(8,128)S(1)} %get-tuple-element.55.refs_1_), channel_id=1, source_target_pairs={{0,8},{8,0},{16,24},{24,16},{32,40},{40,32},{48,56},{56,48},{64,72... | collective-permute-start | bytes 3932168 | tf_op jit(solution)/shard_map/ppermute | solution.py:39
  63.8 6.3 %collective-permute-start.17 = (f32[32,10240]{1,0:T(8,128)S(1)}, f32[32,10240]{1,0:T(8,128)S(1)}, u32[]{:S(2)}, u32[]{:S(2)}) collective-permute-start(f32[32,10240]{1,0:T(8,128)S(1)} %constant_dynamic-update-slice_fusion.refs_3_), channel_id=1, source_target_pairs={{0,8},{8,0},{16,24},{24,16},{32,40},{40,32},{48,56},{56,48},{64,72... | collective-permute-start | bytes 3932168 | tf_op jit(solution)/shard_map/ppermute | solution.py:39
  64.1 6.0 %collective-permute-start.15 = (f32[8,128]{1,0:T(8,128)S(1)}, f32[8,128]{1,0:T(8,128)S(1)}, u32[]{:S(2)}, u32[]{:S(2)}) collective-permute-start(f32[8,128]{1,0:T(8,128)S(1)} %add.22), channel_id=1, source_target_pairs={{0,96},{8,104},{16,112},{24,120},{32,64},{40,72},{48,80},{56,88},{... | collective-permute-start | bytes 12296 | tf_op jit(solution)/shard_map/ppermute | solution.py:39

commit v6 on v5

--- a/solution.py
+++ b/solution.py
@@ -39,7 +39,7 @@
     return lax.ppermute(value, axis, pairs)
 
 
-WA, WB = 3456, 3456
+WA, WB = 3328, 3584
 VMEM = pl.BlockSpec(memory_space=pltpu.VMEM)
 SMEM = pl.BlockSpec(memory_space=pltpu.SMEM)
 HBM = pl.BlockSpec(memory_space=pltpu.HBM)
@@ -48,7 +48,7 @@
 def diagonal():
     pairs = []
     for z, x, core in PLACES:
-        pairs.append((island_id(z, x, core), island_id(z + 1, x + 2, core)))
+        pairs.append((island_id(z, x, core), island_id(z + 1, neighbour(x, core, 0), core)))
     return pairs
 
 
@@ -286,7 +286,7 @@
     for k, step in enumerate(STEPS):
         if k == 1:
             near_peer = hop(turn(near), CORE)
-        if k == 4:
+        if k == 3:
             far = jnp.concatenate([turn(v) for v in (a_far, bc_far)], axis=1)
             far_peer = hop(far, CORE)
             note(far)
@@ -294,7 +294,7 @@
     return tuple(update(sq, [near, near_peer, far, far_peer], anchor, momentum, entries, islands))
 
 
-STEPS = (*FSDP_STEPS, (CORE, "island"), (ZX, "island"))
+STEPS = (*FSDP_STEPS, (ZX, "island"), (CORE, "island"))
 
 
 def solution(mesh):

time: 76 us -> 75.7 us (level); the launches traced: 75.7 us -> 74.2 us
    ppermute x18, waiting for transfers between devices: 38.7 us -> 38 us  [hop(): return lax.ppermute(value, axis, pairs)]
where the time goes in v6:
time: 75.7 us; the launch traced here: 74.2 us
  waiting for transfers between devices  38 us (50%)
  starting transfers between devices  22.7 us (30%)
  Pallas kernels  12.4 us (16%)
  between operations  0.78 us (1%)
    ppermute x18, waiting for transfers between devices, hop(): return lax.ppermute(value, axis, pairs)  38 us
    ppermute x18, starting transfers between devices, hop(): return lax.ppermute(value, axis, pairs)  22.7 us
    pallas_call x3, Pallas kernels, fetch(): pl.pallas_call(kernel, out_shape=(shape,) * count, in_specs=[HBM] * len(a...  6.14 us
    pallas_call x1, Pallas kernels, update(): pl.pallas_call(lambda *refs: update_kernel(entries, islands, *refs), out_...  5.56 us
  transfers between devices with their start and end apart: 18, of which 10 were waited for; matrix products, arithmetic and copies ran while one was open for 1% of the time, Pallas kernels for 6%

profile of v6, /device:TPU:0, one launch (start us, length us, event | category | flops | bytes accessed | tf_op | source)
XLA Modules:
  0.0 74.2 jit_solution(1075434793113222131)
XLA Ops:
  0.6 1.6 %shard_map.51 = f32[32,10240]{1,0:T(8,128)S(1)} custom-call(f32[4,32,10240]{2,1,0:T(8,128)} %bitcast.3), custom_call_target="tpu_custom_call" | custom-call | bytes 1024 | tf_op jit(solution)/shard_map/pallas_call | solution.py:122
  2.3 2.4 %shard_map.50 = (f32[32,10240]{1,0:T(8,128)S(1)}, f32[32,10240]{1,0:T(8,128)S(1)}, f32[32,10240]{1,0:T(8,128)S(1)}) custom-call(f32[4,32,10240]{2,1,0:T(8,128)} %bitcast.4, f32[4,32,10240]{2,1,0:T(8,128)} %refs_5_.1), custom_call_target="tpu_custom_call" | custom-call | bytes 1024 | tf_op jit(solution)/shard_map/pallas_call | solution.py:122
  4.8 0.6 collective-permute-start.1
  5.4 0.2 subtract_add_fusion
  5.6 1.7 %collective-permute-start.3 = (f32[32,6912]{1,0:T(8,128)S(1)}, f32[32,6912]{1,0:T(8,128)S(1)}, u32[]{:S(2)}, u32[]{:S(2)}) collective-permute-start(f32[32,6912]{1,0:T(8,128)S(1)} %slice.13), channel_id=1, source_target_pairs={{0,16},{8,56},{16,0},{24,40},{32,48},{40,24},{48,32},{56,8},{64,80... | collective-permute-start | bytes 2654216 | tf_op jit(solution)/shard_map/ppermute | solution.py:39
  7.3 2.0 %collective-permute-start.2 = (f32[32,3328]{1,0:T(8,128)S(1)}, f32[32,3328]{1,0:T(8,128)S(1)}, u32[]{:S(2)}, u32[]{:S(2)}) collective-permute-start(f32[32,3328]{1,0:T(8,128)S(1)} %slice.12), channel_id=1, source_target_pairs={{0,64},{8,72},{16,80},{24,88},{32,96},{40,104},{48,112},{56,120},{... | collective-permute-start | bytes 1277960 | tf_op jit(solution)/shard_map/ppermute | solution.py:39
  9.3 2.1 %shard_map.52 = (f32[32,10240]{1,0:T(8,128)S(1)}, f32[32,10240]{1,0:T(8,128)S(1)}) custom-call(f32[4,32,10240]{2,1,0:T(8,128)} %bitcast.5, f32[4,32,10240]{2,1,0:T(8,128)} %refs_5_.1), custom_call_target="tpu_custom_call" | custom-call | bytes 1024 | tf_op jit(solution)/shard_map/pallas_call | solution.py:122
  11.4 8.3 %collective-permute-done.2.a_r = f32[32,3328]{1,0:T(8,128)S(1)} collective-permute-done((f32[32,3328]{1,0:T(8,128)S(1)}, f32[32,3328]{1,0:T(8,128)S(1)}, u32[]{:S(2)}, u32[]{:S(2)}) %collective-permute-start.2) | collective-permute-done | bytes 426016 | tf_op jit(solution)/shard_map/ppermute | solution.py:39
  19.8 0.2 shard_map.53
  20.0 1.9 %collective-permute-start.4 = (f32[32,6912]{1,0:T(8,128)S(1)}, f32[32,6912]{1,0:T(8,128)S(1)}, u32[]{:S(2)}, u32[]{:S(2)}) collective-permute-start(f32[32,6912]{1,0:T(8,128)S(1)} %get-tuple-element.35.ab), channel_id=1, source_target_pairs={{0,48},{8,24},{16,32},{24,8},{32,16},{40,56},{48,0},{56,40},{64,11... | collective-permute-start | bytes 2654216 | tf_op jit(solution)/shard_map/ppermute | solution.py:39
  21.9 1.9 %collective-permute-start.5 = (f32[32,3328]{1,0:T(8,128)S(1)}, f32[32,3328]{1,0:T(8,128)S(1)}, u32[]{:S(2)}, u32[]{:S(2)}) collective-permute-start(f32[32,3328]{1,0:T(8,128)S(1)} %get-tuple-element.36.c), channel_id=1, source_target_pairs={{0,64},{8,72},{16,80},{24,88},{32,96},{40,104},{48,112},{56,120},{... | collective-permute-start | bytes 1277960 | tf_op jit(solution)/shard_map/ppermute | solution.py:39
  23.8 8.5 %collective-permute-done.5.c_r = f32[32,3328]{1,0:T(8,128)S(1)} collective-permute-done((f32[32,3328]{1,0:T(8,128)S(1)}, f32[32,3328]{1,0:T(8,128)S(1)}, u32[]{:S(2)}, u32[]{:S(2)}) %collective-permute-start.5) | collective-permute-done | bytes 426016 | tf_op jit(solution)/shard_map/ppermute | solution.py:39
  32.4 2.0 %collective-permute-done.4.ab_r = f32[32,6912]{1,0:T(8,128)S(1)} collective-permute-done((f32[32,6912]{1,0:T(8,128)S(1)}, f32[32,6912]{1,0:T(8,128)S(1)}, u32[]{:S(2)}, u32[]{:S(2)}) %collective-permute-start.4) | collective-permute-done | bytes 884768 | tf_op jit(solution)/shard_map/ppermute | solution.py:39
  34.3 0.1 shard_map.54
  34.5 2.2 %collective-permute-start.7 = (f32[32,3584]{1,0:T(8,128)S(1)}, f32[32,3584]{1,0:T(8,128)S(1)}, u32[]{:S(2)}, u32[]{:S(2)}) collective-permute-start(f32[32,3584]{1,0:T(8,128)S(1)} %get-tuple-element.38.b), channel_id=1, source_target_pairs={{0,64},{8,72},{16,80},{24,88},{32,96},{40,104},{48,112},{56,120},{... | collective-permute-start | bytes 1376264 | tf_op jit(solution)/shard_map/ppermute | solution.py:39
  36.6 1.7 %collective-permute-start.8 = (f32[32,3328]{1,0:T(8,128)S(1)}, f32[32,3328]{1,0:T(8,128)S(1)}, u32[]{:S(2)}, u32[]{:S(2)}) collective-permute-start(f32[32,3328]{1,0:T(8,128)S(1)} %get-tuple-element.39.c), channel_id=1, source_target_pairs={{0,48},{8,24},{16,32},{24,8},{32,16},{40,56},{48,0},{56,40},{64,11... | collective-permute-start | bytes 1277960 | tf_op jit(solution)/shard_map/ppermute | solution.py:39
  38.3 9.3 %collective-permute-done.6.a_r = f32[32,3328]{1,0:T(8,128)S(1)} collective-permute-done((f32[32,3328]{1,0:T(8,128)S(1)}, f32[32,3328]{1,0:T(8,128)S(1)}, u32[]{:S(2)}, u32[]{:S(2)}) %collective-permute-start.6) | collective-permute-done | bytes 426016 | tf_op jit(solution)/shard_map/ppermute | solution.py:39
  47.6 0.3 shard_map.55
  48.0 0.5 collective-permute-start.12
  48.4 0.4 collective-permute-start.13
  48.8 1.5 %collective-permute-start.9 = (f32[8,128]{1,0:T(8,128)S(1)}, f32[8,128]{1,0:T(8,128)S(1)}, u32[]{:S(2)}, u32[]{:S(2)}) collective-permute-start(f32[8,128]{1,0:T(8,128)S(1)} %get-tuple-element.41), channel_id=1, source_target_pairs={{0,2},{1,3},{2,0},{3,1},{4,6},{5,7},{6,4},{7,5},{8,10},{9,11},{10,... | collective-permute-start | bytes 12296 | tf_op jit(solution)/shard_map/ppermute | solution.py:39
  50.3 2.1 %collective-permute-done.9 = f32[8,128]{1,0:T(8,128)S(1)} collective-permute-done((f32[8,128]{1,0:T(8,128)S(1)}, f32[8,128]{1,0:T(8,128)S(1)}, u32[]{:S(2)}, u32[]{:S(2)}) %collective-permute-start.9) | collective-permute-done | bytes 4128 | tf_op jit(solution)/shard_map/ppermute | solution.py:39
  52.4 3.0 %collective-permute-start.10 = (f32[8,128]{1,0:T(8,128)S(1)}, f32[8,128]{1,0:T(8,128)S(1)}, u32[]{:S(2)}, u32[]{:S(2)}) collective-permute-start(f32[8,128]{1,0:T(8,128)S(1)} %add.19), channel_id=1, source_target_pairs={{0,6},{1,7},{2,4},{3,5},{4,2},{5,3},{6,0},{7,1},{8,14},{9,15},{10,... | collective-permute-start | bytes 12296 | tf_op jit(solution)/shard_map/ppermute | solution.py:39
  55.4 1.9 %collective-permute-done.10 = f32[8,128]{1,0:T(8,128)S(1)} collective-permute-done((f32[8,128]{1,0:T(8,128)S(1)}, f32[8,128]{1,0:T(8,128)S(1)}, u32[]{:S(2)}, u32[]{:S(2)}) %collective-permute-start.10) | collective-permute-done | bytes 4128 | tf_op jit(solution)/shard_map/ppermute | solution.py:39
  57.2 3.7 %collective-permute-start.11 = (f32[8,128]{1,0:T(8,128)S(1)}, f32[8,128]{1,0:T(8,128)S(1)}, u32[]{:S(2)}, u32[]{:S(2)}) collective-permute-start(f32[8,128]{1,0:T(8,128)S(1)} %add.20), channel_id=1, source_target_pairs={{0,65},{1,64},{2,67},{3,66},{4,69},{5,68},{6,71},{7,70},{8,73},{9,... | collective-permute-start | bytes 12296 | tf_op jit(solution)/shard_map/ppermute | solution.py:39
  60.9 1.6 %collective-permute-done.11 = f32[8,128]{1,0:T(8,128)S(1)} collective-permute-done((f32[8,128]{1,0:T(8,128)S(1)}, f32[8,128]{1,0:T(8,128)S(1)}, u32[]{:S(2)}, u32[]{:S(2)}) %collective-permute-start.11) | collective-permute-done | bytes 4128 | tf_op jit(solution)/shard_map/ppermute | solution.py:39
  62.6 0.1 collective-permute-start.17
  62.7 1.1 %collective-permute-start.14 = (f32[8,128]{1,0:T(8,128)S(1)}, f32[8,128]{1,0:T(8,128)S(1)}, u32[]{:S(2)}, u32[]{:S(2)}) collective-permute-start(f32[8,128]{1,0:T(8,128)S(1)} %add.21), channel_id=1, source_target_pairs={{0,80},{8,120},{16,64},{24,104},{32,112},{40,88},{48,96},{56,72},{... | collective-permute-start | bytes 12296 | tf_op jit(solution)/shard_map/ppermute | solution.py:39
  63.9 3.5 %collective-permute-done.14 = f32[8,128]{1,0:T(8,128)S(1)} collective-permute-done((f32[8,128]{1,0:T(8,128)S(1)}, f32[8,128]{1,0:T(8,128)S(1)}, u32[]{:S(2)}, u32[]{:S(2)}) %collective-permute-start.14) | collective-permute-done | bytes 4128 | tf_op jit(solution)/shard_map/ppermute | solution.py:39
  67.3 0.5 collective-permute-start.15
  67.8 0.8 %collective-permute-done.15 = f32[8,128]{1,0:T(8,128)S(1)} collective-permute-done((f32[8,128]{1,0:T(8,128)S(1)}, f32[8,128]{1,0:T(8,128)S(1)}, u32[]{:S(2)}, u32[]{:S(2)}) %collective-permute-start.15) | collective-permute-done | bytes 4128 | tf_op jit(solution)/shard_map/ppermute | solution.py:39
  68.7 5.6 %shard_map.56 = (f32[4,32,10240]{2,1,0:T(8,128)}, f32[4,32,10240]{2,1,0:T(8,128)}) custom-call(f32[8,128]{1,0:T(8,128)S(1)} %add.23.refs_0_, f32[32,10240]{1,0:T(8,128)S(1)} %get-tuple-element.55.refs_1_, f32[32,10240]{1,0:T(8,128)S(1)} %collective-permute-done.16.refs_2_, f32[32,10240]{1,0:T(8,128)S(1)} %constant_dynamic-update-slice_fusion.refs_3_, ...), custom_call_target="tpu_custom_call" | custom-call | flops 10485760 | bytes 26214400 | tf_op jit(solution)/shard_map/pallas_call | solution.py:247
  (27 shorter events, 0.4 us)
Async XLA Ops:
  2.2 3.1 %collective-permute-start = (f32[32,10240]{1,0:T(8,128)S(1)}, f32[32,10240]{1,0:T(8,128)S(1)}, u32[]{:S(2)}, u32[]{:S(2)}) collective-permute-start(f32[32,10240]{1,0:T(8,128)S(1)} %shard_map.51), channel_id=1, source_target_pairs={{0,8},{8,0},{16,24},{24,16},{32,40},{40,32},{48,56},{56,48},{64,72... | collective-permute-start | bytes 3932168 | tf_op jit(solution)/shard_map/ppermute | solution.py:39
  4.8 6.7 %collective-permute-start.1 = (f32[32,10240]{1,0:T(8,128)S(1)}, f32[32,10240]{1,0:T(8,128)S(1)}, u32[]{:S(2)}, u32[]{:S(2)}) collective-permute-start(f32[32,10240]{1,0:T(8,128)S(1)} %get-tuple-element.34), channel_id=1, source_target_pairs={{0,8},{8,0},{16,24},{24,16},{32,40},{40,32},{48,56},{56,48},{64,72... | collective-permute-start | bytes 3932168 | tf_op jit(solution)/shard_map/ppermute | solution.py:39
  5.6 14.1 %collective-permute-start.3 = (f32[32,6912]{1,0:T(8,128)S(1)}, f32[32,6912]{1,0:T(8,128)S(1)}, u32[]{:S(2)}, u32[]{:S(2)}) collective-permute-start(f32[32,6912]{1,0:T(8,128)S(1)} %slice.13), channel_id=1, source_target_pairs={{0,16},{8,56},{16,0},{24,40},{32,48},{40,24},{48,32},{56,8},{64,80... | collective-permute-start | bytes 2654216 | tf_op jit(solution)/shard_map/ppermute | solution.py:39
  7.3 12.4 %collective-permute-start.2 = (f32[32,3328]{1,0:T(8,128)S(1)}, f32[32,3328]{1,0:T(8,128)S(1)}, u32[]{:S(2)}, u32[]{:S(2)}) collective-permute-start(f32[32,3328]{1,0:T(8,128)S(1)} %slice.12), channel_id=1, source_target_pairs={{0,64},{8,72},{16,80},{24,88},{32,96},{40,104},{48,112},{56,120},{... | collective-permute-start | bytes 1277960 | tf_op jit(solution)/shard_map/ppermute | solution.py:39
  19.7 48.9 %slice-start = ((s8[5242880]{0:T(1024)(128)(4,1)}), s8[4194304]{0:T(1024)(128)(4,1)S(1)}, s32[]{:S(2)}) async-start(s8[5242880]{0:T(1024)(128)(4,1)} %bitcast.1), calls=%async_computation | async-start | bytes 8388608
  20.0 14.3 %collective-permute-start.4 = (f32[32,6912]{1,0:T(8,128)S(1)}, f32[32,6912]{1,0:T(8,128)S(1)}, u32[]{:S(2)}, u32[]{:S(2)}) collective-permute-start(f32[32,6912]{1,0:T(8,128)S(1)} %get-tuple-element.35.ab), channel_id=1, source_target_pairs={{0,48},{8,24},{16,32},{24,8},{32,16},{40,56},{48,0},{56,40},{64,11... | collective-permute-start | bytes 2654216 | tf_op jit(solution)/shard_map/ppermute | solution.py:39
  21.9 46.7 %slice-start.1 = ((s8[5242880]{0:T(1024)(128)(4,1)}), s8[1048576]{0:T(1024)(128)(4,1)S(1)}, s32[]{:S(2)}) async-start(s8[5242880]{0:T(1024)(128)(4,1)} %bitcast.1), calls=%async_computation.1 | async-start | bytes 2097152
  21.9 10.5 %collective-permute-start.5 = (f32[32,3328]{1,0:T(8,128)S(1)}, f32[32,3328]{1,0:T(8,128)S(1)}, u32[]{:S(2)}, u32[]{:S(2)}) collective-permute-start(f32[32,3328]{1,0:T(8,128)S(1)} %get-tuple-element.36.c), channel_id=1, source_target_pairs={{0,64},{8,72},{16,80},{24,88},{32,96},{40,104},{48,112},{56,120},{... | collective-permute-start | bytes 1277960 | tf_op jit(solution)/shard_map/ppermute | solution.py:39
  34.5 13.1 %collective-permute-start.7 = (f32[32,3584]{1,0:T(8,128)S(1)}, f32[32,3584]{1,0:T(8,128)S(1)}, u32[]{:S(2)}, u32[]{:S(2)}) collective-permute-start(f32[32,3584]{1,0:T(8,128)S(1)} %get-tuple-element.38.b), channel_id=1, source_target_pairs={{0,64},{8,72},{16,80},{24,88},{32,96},{40,104},{48,112},{56,120},{... | collective-permute-start | bytes 1376264 | tf_op jit(solution)/shard_map/ppermute | solution.py:39
  36.6 11.0 %collective-permute-start.6 = (f32[32,3328]{1,0:T(8,128)S(1)}, f32[32,3328]{1,0:T(8,128)S(1)}, u32[]{:S(2)}, u32[]{:S(2)}) collective-permute-start(f32[32,3328]{1,0:T(8,128)S(1)} %get-tuple-element.37.a), channel_id=1, source_target_pairs={{0,16},{8,56},{16,0},{24,40},{32,48},{40,24},{48,32},{56,8},{64,80... | collective-permute-start | bytes 1277960 | tf_op jit(solution)/shard_map/ppermute | solution.py:39
  36.6 11.0 %collective-permute-start.8 = (f32[32,3328]{1,0:T(8,128)S(1)}, f32[32,3328]{1,0:T(8,128)S(1)}, u32[]{:S(2)}, u32[]{:S(2)}) collective-permute-start(f32[32,3328]{1,0:T(8,128)S(1)} %get-tuple-element.39.c), channel_id=1, source_target_pairs={{0,48},{8,24},{16,32},{24,8},{32,16},{40,56},{48,0},{56,40},{64,11... | collective-permute-start | bytes 1277960 | tf_op jit(solution)/shard_map/ppermute | solution.py:39
  48.0 14.6 %collective-permute-start.12 = (f32[32,3328]{1,0:T(8,128)S(1)}, f32[32,3328]{1,0:T(8,128)S(1)}, u32[]{:S(2)}, u32[]{:S(2)}) collective-permute-start(f32[32,3328]{1,0:T(8,128)S(1)} %slice.11), channel_id=1, source_target_pairs={{0,64},{8,72},{16,80},{24,88},{32,96},{40,104},{48,112},{56,120},{... | collective-permute-start | bytes 1277960 | tf_op jit(solution)/shard_map/ppermute | solution.py:39
  48.4 14.2 %collective-permute-start.13 = (f32[32,6912]{1,0:T(8,128)S(1)}, f32[32,6912]{1,0:T(8,128)S(1)}, u32[]{:S(2)}, u32[]{:S(2)}) collective-permute-start(f32[32,6912]{1,0:T(8,128)S(1)} %get-tuple-element.49), channel_id=1, source_target_pairs={{0,16},{8,56},{16,0},{24,40},{32,48},{40,24},{48,32},{56,8},{64,80... | collective-permute-start | bytes 2654216 | tf_op jit(solution)/shard_map/ppermute | solution.py:39
  48.8 3.6 %collective-permute-start.9 = (f32[8,128]{1,0:T(8,128)S(1)}, f32[8,128]{1,0:T(8,128)S(1)}, u32[]{:S(2)}, u32[]{:S(2)}) collective-permute-start(f32[8,128]{1,0:T(8,128)S(1)} %get-tuple-element.41), channel_id=1, source_target_pairs={{0,2},{1,3},{2,0},{3,1},{4,6},{5,7},{6,4},{7,5},{8,10},{9,11},{10,... | collective-permute-start | bytes 12296 | tf_op jit(solution)/shard_map/ppermute | solution.py:39
  52.4 4.8 %collective-permute-start.10 = (f32[8,128]{1,0:T(8,128)S(1)}, f32[8,128]{1,0:T(8,128)S(1)}, u32[]{:S(2)}, u32[]{:S(2)}) collective-permute-start(f32[8,128]{1,0:T(8,128)S(1)} %add.19), channel_id=1, source_target_pairs={{0,6},{1,7},{2,4},{3,5},{4,2},{5,3},{6,0},{7,1},{8,14},{9,15},{10,... | collective-permute-start | bytes 12296 | tf_op jit(solution)/shard_map/ppermute | solution.py:39
  57.2 5.3 %collective-permute-start.11 = (f32[8,128]{1,0:T(8,128)S(1)}, f32[8,128]{1,0:T(8,128)S(1)}, u32[]{:S(2)}, u32[]{:S(2)}) collective-permute-start(f32[8,128]{1,0:T(8,128)S(1)} %add.20), channel_id=1, source_target_pairs={{0,65},{1,64},{2,67},{3,66},{4,69},{5,68},{6,71},{7,70},{8,73},{9,... | collective-permute-start | bytes 12296 | tf_op jit(solution)/shard_map/ppermute | solution.py:39
  60.9 7.7 %collective-permute-start.16 = (f32[32,10240]{1,0:T(8,128)S(1)}, f32[32,10240]{1,0:T(8,128)S(1)}, u32[]{:S(2)}, u32[]{:S(2)}) collective-permute-start(f32[32,10240]{1,0:T(8,128)S(1)} %get-tuple-element.55.refs_1_), channel_id=1, source_target_pairs={{0,8},{8,0},{16,24},{24,16},{32,40},{40,32},{48,56},{56,48},{64,72... | collective-permute-start | bytes 3932168 | tf_op jit(solution)/shard_map/ppermute | solution.py:39
  62.6 6.0 %collective-permute-start.17 = (f32[32,10240]{1,0:T(8,128)S(1)}, f32[32,10240]{1,0:T(8,128)S(1)}, u32[]{:S(2)}, u32[]{:S(2)}) collective-permute-start(f32[32,10240]{1,0:T(8,128)S(1)} %constant_dynamic-update-slice_fusion.refs_3_), channel_id=1, source_target_pairs={{0,8},{8,0},{16,24},{24,16},{32,40},{40,32},{48,56},{56,48},{64,72... | collective-permute-start | bytes 3932168 | tf_op jit(solution)/shard_map/ppermute | solution.py:39
  62.7 4.6 %collective-permute-start.14 = (f32[8,128]{1,0:T(8,128)S(1)}, f32[8,128]{1,0:T(8,128)S(1)}, u32[]{:S(2)}, u32[]{:S(2)}) collective-permute-start(f32[8,128]{1,0:T(8,128)S(1)} %add.21), channel_id=1, source_target_pairs={{0,80},{8,120},{16,64},{24,104},{32,112},{40,88},{48,96},{56,72},{... | collective-permute-start | bytes 12296 | tf_op jit(solution)/shard_map/ppermute | solution.py:39
  67.3 1.3 %collective-permute-start.15 = (f32[8,128]{1,0:T(8,128)S(1)}, f32[8,128]{1,0:T(8,128)S(1)}, u32[]{:S(2)}, u32[]{:S(2)}) collective-permute-start(f32[8,128]{1,0:T(8,128)S(1)} %add.22), channel_id=1, source_target_pairs={{0,8},{8,0},{16,24},{24,16},{32,40},{40,32},{48,56},{56,48},{64,72... | collective-permute-start | bytes 12296 | tf_op jit(solution)/shard_map/ppermute | solution.py:39

commit v7 on v6

--- a/solution.py
+++ b/solution.py
@@ -39,7 +39,7 @@
     return lax.ppermute(value, axis, pairs)
 
 
-WA, WB = 3328, 3584
+WA, WB = 3328, 3712
 VMEM = pl.BlockSpec(memory_space=pltpu.VMEM)
 SMEM = pl.BlockSpec(memory_space=pltpu.SMEM)
 HBM = pl.BlockSpec(memory_space=pltpu.HBM)
@@ -284,9 +284,8 @@
     note(sq)
     a_far, bc_far = hop(near[:, :WA], Z), hop(bc, X0)
     for k, step in enumerate(STEPS):
-        if k == 1:
+        if k == 3:
             near_peer = hop(turn(near), CORE)
-        if k == 3:
             far = jnp.concatenate([turn(v) for v in (a_far, bc_far)], axis=1)
             far_peer = hop(far, CORE)
             note(far)

time: 75.7 us -> 75.8 us (level)
  transfers between devices with their start and end apart: 18 -> 18, of which waited for: 10 -> 11; matrix products, arithmetic and copies ran while one was open for 1% -> 1% of each run, Pallas kernels for 6% -> 6%
where the time goes in v7:
time: 75.8 us; the launch traced here: 74.5 us
  waiting for transfers between devices  38 us (50%)
  starting transfers between devices  22.9 us (30%)
  Pallas kernels  12.4 us (16%)
  between operations  0.78 us (1%)
    ppermute x18, waiting for transfers between devices, hop(): return lax.ppermute(value, axis, pairs)  38 us
    ppermute x18, starting transfers between devices, hop(): return lax.ppermute(value, axis, pairs)  22.9 us
    pallas_call x3, Pallas kernels, fetch(): pl.pallas_call(kernel, out_shape=(shape,) * count, in_specs=[HBM] * len(a...  6.14 us
    pallas_call x1, Pallas kernels, update(): pl.pallas_call(lambda *refs: update_kernel(entries, islands, *refs), out_...  5.56 us
  transfers between devices with their start and end apart: 18, of which 11 were waited for; matrix products, arithmetic and copies ran while one was open for 1% of the time, Pallas kernels for 6%

profile of v7, /device:TPU:0, one launch (start us, length us, event | category | flops | bytes accessed | tf_op | source)
XLA Modules:
  0.0 74.5 jit_solution(14202446594972678950)
XLA Ops:
  0.6 1.6 %shard_map.51 = f32[32,10240]{1,0:T(8,128)S(1)} custom-call(f32[4,32,10240]{2,1,0:T(8,128)} %bitcast.3), custom_call_target="tpu_custom_call" | custom-call | bytes 1024 | tf_op jit(solution)/shard_map/pallas_call | solution.py:122
  2.3 2.4 %shard_map.50 = (f32[32,10240]{1,0:T(8,128)S(1)}, f32[32,10240]{1,0:T(8,128)S(1)}, f32[32,10240]{1,0:T(8,128)S(1)}) custom-call(f32[4,32,10240]{2,1,0:T(8,128)} %bitcast.4, f32[4,32,10240]{2,1,0:T(8,128)} %refs_5_.1), custom_call_target="tpu_custom_call" | custom-call | bytes 1024 | tf_op jit(solution)/shard_map/pallas_call | solution.py:122
  4.8 0.6 collective-permute-start.1
  5.4 0.2 subtract_add_fusion
  5.6 1.7 %collective-permute-start.3 = (f32[32,6912]{1,0:T(8,128)S(1)}, f32[32,6912]{1,0:T(8,128)S(1)}, u32[]{:S(2)}, u32[]{:S(2)}) collective-permute-start(f32[32,6912]{1,0:T(8,128)S(1)} %slice.13), channel_id=1, source_target_pairs={{0,16},{8,56},{16,0},{24,40},{32,48},{40,24},{48,32},{56,8},{64,80... | collective-permute-start | bytes 2654216 | tf_op jit(solution)/shard_map/ppermute | solution.py:39
  7.3 2.0 %collective-permute-start.2 = (f32[32,3328]{1,0:T(8,128)S(1)}, f32[32,3328]{1,0:T(8,128)S(1)}, u32[]{:S(2)}, u32[]{:S(2)}) collective-permute-start(f32[32,3328]{1,0:T(8,128)S(1)} %slice.12), channel_id=1, source_target_pairs={{0,64},{8,72},{16,80},{24,88},{32,96},{40,104},{48,112},{56,120},{... | collective-permute-start | bytes 1277960 | tf_op jit(solution)/shard_map/ppermute | solution.py:39
  9.3 2.1 %shard_map.52 = (f32[32,10240]{1,0:T(8,128)S(1)}, f32[32,10240]{1,0:T(8,128)S(1)}) custom-call(f32[4,32,10240]{2,1,0:T(8,128)} %bitcast.5, f32[4,32,10240]{2,1,0:T(8,128)} %refs_5_.1), custom_call_target="tpu_custom_call" | custom-call | bytes 1024 | tf_op jit(solution)/shard_map/pallas_call | solution.py:122
  11.4 8.3 %collective-permute-done.2.a_r = f32[32,3328]{1,0:T(8,128)S(1)} collective-permute-done((f32[32,3328]{1,0:T(8,128)S(1)}, f32[32,3328]{1,0:T(8,128)S(1)}, u32[]{:S(2)}, u32[]{:S(2)}) %collective-permute-start.2) | collective-permute-done | bytes 426016 | tf_op jit(solution)/shard_map/ppermute | solution.py:39
  19.8 0.2 shard_map.53
  20.0 1.9 %collective-permute-start.4 = (f32[32,7040]{1,0:T(8,128)S(1)}, f32[32,7040]{1,0:T(8,128)S(1)}, u32[]{:S(2)}, u32[]{:S(2)}) collective-permute-start(f32[32,7040]{1,0:T(8,128)S(1)} %get-tuple-element.35.ab), channel_id=1, source_target_pairs={{0,48},{8,24},{16,32},{24,8},{32,16},{40,56},{48,0},{56,40},{64,11... | collective-permute-start | bytes 2703368 | tf_op jit(solution)/shard_map/ppermute | solution.py:39
  21.9 1.9 %collective-permute-start.5 = (f32[32,3200]{1,0:T(8,128)S(1)}, f32[32,3200]{1,0:T(8,128)S(1)}, u32[]{:S(2)}, u32[]{:S(2)}) collective-permute-start(f32[32,3200]{1,0:T(8,128)S(1)} %get-tuple-element.36.c), channel_id=1, source_target_pairs={{0,64},{8,72},{16,80},{24,88},{32,96},{40,104},{48,112},{56,120},{... | collective-permute-start | bytes 1228808 | tf_op jit(solution)/shard_map/ppermute | solution.py:39
  23.8 8.2 %collective-permute-done.5.c_r = f32[32,3200]{1,0:T(8,128)S(1)} collective-permute-done((f32[32,3200]{1,0:T(8,128)S(1)}, f32[32,3200]{1,0:T(8,128)S(1)}, u32[]{:S(2)}, u32[]{:S(2)}) %collective-permute-start.5) | collective-permute-done | bytes 409632 | tf_op jit(solution)/shard_map/ppermute | solution.py:39
  32.0 2.5 %collective-permute-done.4.ab_r = f32[32,7040]{1,0:T(8,128)S(1)} collective-permute-done((f32[32,7040]{1,0:T(8,128)S(1)}, f32[32,7040]{1,0:T(8,128)S(1)}, u32[]{:S(2)}, u32[]{:S(2)}) %collective-permute-start.4) | collective-permute-done | bytes 901152 | tf_op jit(solution)/shard_map/ppermute | solution.py:39
  34.6 2.2 %collective-permute-start.7 = (f32[32,3712]{1,0:T(8,128)S(1)}, f32[32,3712]{1,0:T(8,128)S(1)}, u32[]{:S(2)}, u32[]{:S(2)}) collective-permute-start(f32[32,3712]{1,0:T(8,128)S(1)} %get-tuple-element.38.b), channel_id=1, source_target_pairs={{0,64},{8,72},{16,80},{24,88},{32,96},{40,104},{48,112},{56,120},{... | collective-permute-start | bytes 1425416 | tf_op jit(solution)/shard_map/ppermute | solution.py:39
  36.8 1.7 %collective-permute-start.8 = (f32[32,3200]{1,0:T(8,128)S(1)}, f32[32,3200]{1,0:T(8,128)S(1)}, u32[]{:S(2)}, u32[]{:S(2)}) collective-permute-start(f32[32,3200]{1,0:T(8,128)S(1)} %get-tuple-element.39.c), channel_id=1, source_target_pairs={{0,48},{8,24},{16,32},{24,8},{32,16},{40,56},{48,0},{56,40},{64,11... | collective-permute-start | bytes 1228808 | tf_op jit(solution)/shard_map/ppermute | solution.py:39
  38.5 8.9 %collective-permute-done.8.c_r = f32[32,3200]{1,0:T(8,128)S(1)} collective-permute-done((f32[32,3200]{1,0:T(8,128)S(1)}, f32[32,3200]{1,0:T(8,128)S(1)}, u32[]{:S(2)}, u32[]{:S(2)}) %collective-permute-start.8) | collective-permute-done | bytes 409632 | tf_op jit(solution)/shard_map/ppermute | solution.py:39
  47.3 0.3 collective-permute-done.6.a_r
  47.6 0.3 shard_map.55
  48.0 0.5 collective-permute-start.12
  48.4 0.3 collective-permute-start.13
  48.7 1.6 %collective-permute-start.9 = (f32[8,128]{1,0:T(8,128)S(1)}, f32[8,128]{1,0:T(8,128)S(1)}, u32[]{:S(2)}, u32[]{:S(2)}) collective-permute-start(f32[8,128]{1,0:T(8,128)S(1)} %get-tuple-element.41), channel_id=1, source_target_pairs={{0,2},{1,3},{2,0},{3,1},{4,6},{5,7},{6,4},{7,5},{8,10},{9,11},{10,... | collective-permute-start | bytes 12296 | tf_op jit(solution)/shard_map/ppermute | solution.py:39
  50.3 2.0 %collective-permute-done.9 = f32[8,128]{1,0:T(8,128)S(1)} collective-permute-done((f32[8,128]{1,0:T(8,128)S(1)}, f32[8,128]{1,0:T(8,128)S(1)}, u32[]{:S(2)}, u32[]{:S(2)}) %collective-permute-start.9) | collective-permute-done | bytes 4128 | tf_op jit(solution)/shard_map/ppermute | solution.py:39
  52.3 3.0 %collective-permute-start.10 = (f32[8,128]{1,0:T(8,128)S(1)}, f32[8,128]{1,0:T(8,128)S(1)}, u32[]{:S(2)}, u32[]{:S(2)}) collective-permute-start(f32[8,128]{1,0:T(8,128)S(1)} %add.19), channel_id=1, source_target_pairs={{0,6},{1,7},{2,4},{3,5},{4,2},{5,3},{6,0},{7,1},{8,14},{9,15},{10,... | collective-permute-start | bytes 12296 | tf_op jit(solution)/shard_map/ppermute | solution.py:39
  55.3 1.8 %collective-permute-done.10 = f32[8,128]{1,0:T(8,128)S(1)} collective-permute-done((f32[8,128]{1,0:T(8,128)S(1)}, f32[8,128]{1,0:T(8,128)S(1)}, u32[]{:S(2)}, u32[]{:S(2)}) %collective-permute-start.10) | collective-permute-done | bytes 4128 | tf_op jit(solution)/shard_map/ppermute | solution.py:39
  57.1 3.8 %collective-permute-start.11 = (f32[8,128]{1,0:T(8,128)S(1)}, f32[8,128]{1,0:T(8,128)S(1)}, u32[]{:S(2)}, u32[]{:S(2)}) collective-permute-start(f32[8,128]{1,0:T(8,128)S(1)} %add.20), channel_id=1, source_target_pairs={{0,65},{1,64},{2,67},{3,66},{4,69},{5,68},{6,71},{7,70},{8,73},{9,... | collective-permute-start | bytes 12296 | tf_op jit(solution)/shard_map/ppermute | solution.py:39
  60.9 1.6 %collective-permute-done.11 = f32[8,128]{1,0:T(8,128)S(1)} collective-permute-done((f32[8,128]{1,0:T(8,128)S(1)}, f32[8,128]{1,0:T(8,128)S(1)}, u32[]{:S(2)}, u32[]{:S(2)}) %collective-permute-start.11) | collective-permute-done | bytes 4128 | tf_op jit(solution)/shard_map/ppermute | solution.py:39
  62.6 0.6 collective-permute-start.17
  63.2 1.1 %collective-permute-start.14 = (f32[8,128]{1,0:T(8,128)S(1)}, f32[8,128]{1,0:T(8,128)S(1)}, u32[]{:S(2)}, u32[]{:S(2)}) collective-permute-start(f32[8,128]{1,0:T(8,128)S(1)} %add.21), channel_id=1, source_target_pairs={{0,80},{8,120},{16,64},{24,104},{32,112},{40,88},{48,96},{56,72},{... | collective-permute-start | bytes 12296 | tf_op jit(solution)/shard_map/ppermute | solution.py:39
  64.3 3.4 %collective-permute-done.14 = f32[8,128]{1,0:T(8,128)S(1)} collective-permute-done((f32[8,128]{1,0:T(8,128)S(1)}, f32[8,128]{1,0:T(8,128)S(1)}, u32[]{:S(2)}, u32[]{:S(2)}) %collective-permute-start.14) | collective-permute-done | bytes 4128 | tf_op jit(solution)/shard_map/ppermute | solution.py:39
  67.7 0.2 collective-permute-start.15
  67.9 1.0 %collective-permute-done.15 = f32[8,128]{1,0:T(8,128)S(1)} collective-permute-done((f32[8,128]{1,0:T(8,128)S(1)}, f32[8,128]{1,0:T(8,128)S(1)}, u32[]{:S(2)}, u32[]{:S(2)}) %collective-permute-start.15) | collective-permute-done | bytes 4128 | tf_op jit(solution)/shard_map/ppermute | solution.py:39
  68.9 5.6 %shard_map.56 = (f32[4,32,10240]{2,1,0:T(8,128)}, f32[4,32,10240]{2,1,0:T(8,128)}) custom-call(f32[8,128]{1,0:T(8,128)S(1)} %add.23.refs_0_, f32[32,10240]{1,0:T(8,128)S(1)} %get-tuple-element.55.refs_1_, f32[32,10240]{1,0:T(8,128)S(1)} %collective-permute-done.16.refs_2_, f32[32,10240]{1,0:T(8,128)S(1)} %constant_dynamic-update-slice_fusion.refs_3_, ...), custom_call_target="tpu_custom_call" | custom-call | flops 10485760 | bytes 26214400 | tf_op jit(solution)/shard_map/pallas_call | solution.py:247
  (27 shorter events, 0.5 us)
Async XLA Ops:
  2.2 3.1 %collective-permute-start = (f32[32,10240]{1,0:T(8,128)S(1)}, f32[32,10240]{1,0:T(8,128)S(1)}, u32[]{:S(2)}, u32[]{:S(2)}) collective-permute-start(f32[32,10240]{1,0:T(8,128)S(1)} %shard_map.51), channel_id=1, source_target_pairs={{0,8},{8,0},{16,24},{24,16},{32,40},{40,32},{48,56},{56,48},{64,72... | collective-permute-start | bytes 3932168 | tf_op jit(solution)/shard_map/ppermute | solution.py:39
  4.8 6.7 %collective-permute-start.1 = (f32[32,10240]{1,0:T(8,128)S(1)}, f32[32,10240]{1,0:T(8,128)S(1)}, u32[]{:S(2)}, u32[]{:S(2)}) collective-permute-start(f32[32,10240]{1,0:T(8,128)S(1)} %get-tuple-element.34), channel_id=1, source_target_pairs={{0,8},{8,0},{16,24},{24,16},{32,40},{40,32},{48,56},{56,48},{64,72... | collective-permute-start | bytes 3932168 | tf_op jit(solution)/shard_map/ppermute | solution.py:39
  5.6 14.1 %collective-permute-start.3 = (f32[32,6912]{1,0:T(8,128)S(1)}, f32[32,6912]{1,0:T(8,128)S(1)}, u32[]{:S(2)}, u32[]{:S(2)}) collective-permute-start(f32[32,6912]{1,0:T(8,128)S(1)} %slice.13), channel_id=1, source_target_pairs={{0,16},{8,56},{16,0},{24,40},{32,48},{40,24},{48,32},{56,8},{64,80... | collective-permute-start | bytes 2654216 | tf_op jit(solution)/shard_map/ppermute | solution.py:39
  7.3 12.4 %collective-permute-start.2 = (f32[32,3328]{1,0:T(8,128)S(1)}, f32[32,3328]{1,0:T(8,128)S(1)}, u32[]{:S(2)}, u32[]{:S(2)}) collective-permute-start(f32[32,3328]{1,0:T(8,128)S(1)} %slice.12), channel_id=1, source_target_pairs={{0,64},{8,72},{16,80},{24,88},{32,96},{40,104},{48,112},{56,120},{... | collective-permute-start | bytes 1277960 | tf_op jit(solution)/shard_map/ppermute | solution.py:39
  19.7 49.1 %slice-start = ((s8[5242880]{0:T(1024)(128)(4,1)}), s8[4194304]{0:T(1024)(128)(4,1)S(1)}, s32[]{:S(2)}) async-start(s8[5242880]{0:T(1024)(128)(4,1)} %bitcast.1), calls=%async_computation | async-start | bytes 8388608
  20.0 14.5 %collective-permute-start.4 = (f32[32,7040]{1,0:T(8,128)S(1)}, f32[32,7040]{1,0:T(8,128)S(1)}, u32[]{:S(2)}, u32[]{:S(2)}) collective-permute-start(f32[32,7040]{1,0:T(8,128)S(1)} %get-tuple-element.35.ab), channel_id=1, source_target_pairs={{0,48},{8,24},{16,32},{24,8},{32,16},{40,56},{48,0},{56,40},{64,11... | collective-permute-start | bytes 2703368 | tf_op jit(solution)/shard_map/ppermute | solution.py:39
  21.9 47.0 %slice-start.1 = ((s8[5242880]{0:T(1024)(128)(4,1)}), s8[1048576]{0:T(1024)(128)(4,1)S(1)}, s32[]{:S(2)}) async-start(s8[5242880]{0:T(1024)(128)(4,1)} %bitcast.1), calls=%async_computation.1 | async-start | bytes 2097152
  21.9 10.1 %collective-permute-start.5 = (f32[32,3200]{1,0:T(8,128)S(1)}, f32[32,3200]{1,0:T(8,128)S(1)}, u32[]{:S(2)}, u32[]{:S(2)}) collective-permute-start(f32[32,3200]{1,0:T(8,128)S(1)} %get-tuple-element.36.c), channel_id=1, source_target_pairs={{0,64},{8,72},{16,80},{24,88},{32,96},{40,104},{48,112},{56,120},{... | collective-permute-start | bytes 1228808 | tf_op jit(solution)/shard_map/ppermute | solution.py:39
  34.6 13.0 %collective-permute-start.7 = (f32[32,3712]{1,0:T(8,128)S(1)}, f32[32,3712]{1,0:T(8,128)S(1)}, u32[]{:S(2)}, u32[]{:S(2)}) collective-permute-start(f32[32,3712]{1,0:T(8,128)S(1)} %get-tuple-element.38.b), channel_id=1, source_target_pairs={{0,64},{8,72},{16,80},{24,88},{32,96},{40,104},{48,112},{56,120},{... | collective-permute-start | bytes 1425416 | tf_op jit(solution)/shard_map/ppermute | solution.py:39
  36.8 10.8 %collective-permute-start.6 = (f32[32,3328]{1,0:T(8,128)S(1)}, f32[32,3328]{1,0:T(8,128)S(1)}, u32[]{:S(2)}, u32[]{:S(2)}) collective-permute-start(f32[32,3328]{1,0:T(8,128)S(1)} %get-tuple-element.37.a), channel_id=1, source_target_pairs={{0,16},{8,56},{16,0},{24,40},{32,48},{40,24},{48,32},{56,8},{64,80... | collective-permute-start | bytes 1277960 | tf_op jit(solution)/shard_map/ppermute | solution.py:39
  36.8 10.5 %collective-permute-start.8 = (f32[32,3200]{1,0:T(8,128)S(1)}, f32[32,3200]{1,0:T(8,128)S(1)}, u32[]{:S(2)}, u32[]{:S(2)}) collective-permute-start(f32[32,3200]{1,0:T(8,128)S(1)} %get-tuple-element.39.c), channel_id=1, source_target_pairs={{0,48},{8,24},{16,32},{24,8},{32,16},{40,56},{48,0},{56,40},{64,11... | collective-permute-start | bytes 1228808 | tf_op jit(solution)/shard_map/ppermute | solution.py:39
  48.0 14.5 %collective-permute-start.12 = (f32[32,3328]{1,0:T(8,128)S(1)}, f32[32,3328]{1,0:T(8,128)S(1)}, u32[]{:S(2)}, u32[]{:S(2)}) collective-permute-start(f32[32,3328]{1,0:T(8,128)S(1)} %slice.11), channel_id=1, source_target_pairs={{0,64},{8,72},{16,80},{24,88},{32,96},{40,104},{48,112},{56,120},{... | collective-permute-start | bytes 1277960 | tf_op jit(solution)/shard_map/ppermute | solution.py:39
  48.4 14.1 %collective-permute-start.13 = (f32[32,6912]{1,0:T(8,128)S(1)}, f32[32,6912]{1,0:T(8,128)S(1)}, u32[]{:S(2)}, u32[]{:S(2)}) collective-permute-start(f32[32,6912]{1,0:T(8,128)S(1)} %get-tuple-element.49), channel_id=1, source_target_pairs={{0,16},{8,56},{16,0},{24,40},{32,48},{40,24},{48,32},{56,8},{64,80... | collective-permute-start | bytes 2654216 | tf_op jit(solution)/shard_map/ppermute | solution.py:39
  48.7 3.6 %collective-permute-start.9 = (f32[8,128]{1,0:T(8,128)S(1)}, f32[8,128]{1,0:T(8,128)S(1)}, u32[]{:S(2)}, u32[]{:S(2)}) collective-permute-start(f32[8,128]{1,0:T(8,128)S(1)} %get-tuple-element.41), channel_id=1, source_target_pairs={{0,2},{1,3},{2,0},{3,1},{4,6},{5,7},{6,4},{7,5},{8,10},{9,11},{10,... | collective-permute-start | bytes 12296 | tf_op jit(solution)/shard_map/ppermute | solution.py:39
  52.3 4.8 %collective-permute-start.10 = (f32[8,128]{1,0:T(8,128)S(1)}, f32[8,128]{1,0:T(8,128)S(1)}, u32[]{:S(2)}, u32[]{:S(2)}) collective-permute-start(f32[8,128]{1,0:T(8,128)S(1)} %add.19), channel_id=1, source_target_pairs={{0,6},{1,7},{2,4},{3,5},{4,2},{5,3},{6,0},{7,1},{8,14},{9,15},{10,... | collective-permute-start | bytes 12296 | tf_op jit(solution)/shard_map/ppermute | solution.py:39
  57.1 5.4 %collective-permute-start.11 = (f32[8,128]{1,0:T(8,128)S(1)}, f32[8,128]{1,0:T(8,128)S(1)}, u32[]{:S(2)}, u32[]{:S(2)}) collective-permute-start(f32[8,128]{1,0:T(8,128)S(1)} %add.20), channel_id=1, source_target_pairs={{0,65},{1,64},{2,67},{3,66},{4,69},{5,68},{6,71},{7,70},{8,73},{9,... | collective-permute-start | bytes 12296 | tf_op jit(solution)/shard_map/ppermute | solution.py:39
  62.5 6.4 %collective-permute-start.16 = (f32[32,10240]{1,0:T(8,128)S(1)}, f32[32,10240]{1,0:T(8,128)S(1)}, u32[]{:S(2)}, u32[]{:S(2)}) collective-permute-start(f32[32,10240]{1,0:T(8,128)S(1)} %get-tuple-element.55.refs_1_), channel_id=1, source_target_pairs={{0,8},{8,0},{16,24},{24,16},{32,40},{40,32},{48,56},{56,48},{64,72... | collective-permute-start | bytes 3932168 | tf_op jit(solution)/shard_map/ppermute | solution.py:39
  62.6 6.3 %collective-permute-start.17 = (f32[32,10240]{1,0:T(8,128)S(1)}, f32[32,10240]{1,0:T(8,128)S(1)}, u32[]{:S(2)}, u32[]{:S(2)}) collective-permute-start(f32[32,10240]{1,0:T(8,128)S(1)} %constant_dynamic-update-slice_fusion.refs_3_), channel_id=1, source_target_pairs={{0,8},{8,0},{16,24},{24,16},{32,40},{40,32},{48,56},{56,48},{64,72... | collective-permute-start | bytes 3932168 | tf_op jit(solution)/shard_map/ppermute | solution.py:39
  63.2 4.5 %collective-permute-start.14 = (f32[8,128]{1,0:T(8,128)S(1)}, f32[8,128]{1,0:T(8,128)S(1)}, u32[]{:S(2)}, u32[]{:S(2)}) collective-permute-start(f32[8,128]{1,0:T(8,128)S(1)} %add.21), channel_id=1, source_target_pairs={{0,80},{8,120},{16,64},{24,104},{32,112},{40,88},{48,96},{56,72},{... | collective-permute-start | bytes 12296 | tf_op jit(solution)/shard_map/ppermute | solution.py:39
  67.7 1.2 %collective-permute-start.15 = (f32[8,128]{1,0:T(8,128)S(1)}, f32[8,128]{1,0:T(8,128)S(1)}, u32[]{:S(2)}, u32[]{:S(2)}) collective-permute-start(f32[8,128]{1,0:T(8,128)S(1)} %add.22), channel_id=1, source_target_pairs={{0,8},{8,0},{16,24},{24,16},{32,40},{40,32},{48,56},{56,48},{64,72... | collective-permute-start | bytes 12296 | tf_op jit(solution)/shard_map/ppermute | solution.py:39

commit v8 on v7

--- a/solution.py
+++ b/solution.py
@@ -293,7 +293,7 @@
     return tuple(update(sq, [near, near_peer, far, far_peer], anchor, momentum, entries, islands))
 
 
-STEPS = (*FSDP_STEPS, (ZX, "island"), (CORE, "island"))
+STEPS = (FSDP_STEPS[2], *FSDP_STEPS[:2], (ZX, "island"), (CORE, "island"))
 
 
 def solution(mesh):

time: 75.8 us -> 75.8 us (level)
  no operation moved by 1% of the time
where the time goes in v8:
time: 75.8 us; the launch traced here: 74.5 us
  waiting for transfers between devices  38 us (50%)
  starting transfers between devices  22.9 us (30%)
  Pallas kernels  12.4 us (16%)
  between operations  0.78 us (1%)
    ppermute x18, waiting for transfers between devices, hop(): return lax.ppermute(value, axis, pairs)  38 us
    ppermute x18, starting transfers between devices, hop(): return lax.ppermute(value, axis, pairs)  22.9 us
    pallas_call x3, Pallas kernels, fetch(): pl.pallas_call(kernel, out_shape=(shape,) * count, in_specs=[HBM] * len(a...  6.14 us
    pallas_call x1, Pallas kernels, update(): pl.pallas_call(lambda *refs: update_kernel(entries, islands, *refs), out_...  5.56 us
  transfers between devices with their start and end apart: 18, of which 11 were waited for; matrix products, arithmetic and copies ran while one was open for 1% of the time, Pallas kernels for 6%

profile of v8, /device:TPU:0, one launch (start us, length us, event | category | flops | bytes accessed | tf_op | source)
XLA Modules:
  0.0 74.5 jit_solution(4548478685443841613)
XLA Ops:
  0.6 1.6 %shard_map.51 = f32[32,10240]{1,0:T(8,128)S(1)} custom-call(f32[4,32,10240]{2,1,0:T(8,128)} %bitcast.3), custom_call_target="tpu_custom_call" | custom-call | bytes 1024 | tf_op jit(solution)/shard_map/pallas_call | solution.py:122
  2.3 2.4 %shard_map.50 = (f32[32,10240]{1,0:T(8,128)S(1)}, f32[32,10240]{1,0:T(8,128)S(1)}, f32[32,10240]{1,0:T(8,128)S(1)}) custom-call(f32[4,32,10240]{2,1,0:T(8,128)} %bitcast.4, f32[4,32,10240]{2,1,0:T(8,128)} %refs_5_.1), custom_call_target="tpu_custom_call" | custom-call | bytes 1024 | tf_op jit(solution)/shard_map/pallas_call | solution.py:122
  4.8 0.6 collective-permute-start.1
  5.4 0.2 subtract_add_fusion
  5.6 1.7 %collective-permute-start.3 = (f32[32,6912]{1,0:T(8,128)S(1)}, f32[32,6912]{1,0:T(8,128)S(1)}, u32[]{:S(2)}, u32[]{:S(2)}) collective-permute-start(f32[32,6912]{1,0:T(8,128)S(1)} %slice.13), channel_id=1, source_target_pairs={{0,16},{8,56},{16,0},{24,40},{32,48},{40,24},{48,32},{56,8},{64,80... | collective-permute-start | bytes 2654216 | tf_op jit(solution)/shard_map/ppermute | solution.py:39
  7.3 2.0 %collective-permute-start.2 = (f32[32,3328]{1,0:T(8,128)S(1)}, f32[32,3328]{1,0:T(8,128)S(1)}, u32[]{:S(2)}, u32[]{:S(2)}) collective-permute-start(f32[32,3328]{1,0:T(8,128)S(1)} %slice.12), channel_id=1, source_target_pairs={{0,64},{8,72},{16,80},{24,88},{32,96},{40,104},{48,112},{56,120},{... | collective-permute-start | bytes 1277960 | tf_op jit(solution)/shard_map/ppermute | solution.py:39
  9.3 2.1 %shard_map.52 = (f32[32,10240]{1,0:T(8,128)S(1)}, f32[32,10240]{1,0:T(8,128)S(1)}) custom-call(f32[4,32,10240]{2,1,0:T(8,128)} %bitcast.5, f32[4,32,10240]{2,1,0:T(8,128)} %refs_5_.1), custom_call_target="tpu_custom_call" | custom-call | bytes 1024 | tf_op jit(solution)/shard_map/pallas_call | solution.py:122
  11.4 8.3 %collective-permute-done.2.a_r = f32[32,3328]{1,0:T(8,128)S(1)} collective-permute-done((f32[32,3328]{1,0:T(8,128)S(1)}, f32[32,3328]{1,0:T(8,128)S(1)}, u32[]{:S(2)}, u32[]{:S(2)}) %collective-permute-start.2) | collective-permute-done | bytes 426016 | tf_op jit(solution)/shard_map/ppermute | solution.py:39
  19.8 0.2 shard_map.53
  20.0 1.9 %collective-permute-start.4 = (f32[32,7040]{1,0:T(8,128)S(1)}, f32[32,7040]{1,0:T(8,128)S(1)}, u32[]{:S(2)}, u32[]{:S(2)}) collective-permute-start(f32[32,7040]{1,0:T(8,128)S(1)} %get-tuple-element.35.ab), channel_id=1, source_target_pairs={{0,48},{8,24},{16,32},{24,8},{32,16},{40,56},{48,0},{56,40},{64,11... | collective-permute-start | bytes 2703368 | tf_op jit(solution)/shard_map/ppermute | solution.py:39
  21.9 1.9 %collective-permute-start.5 = (f32[32,3200]{1,0:T(8,128)S(1)}, f32[32,3200]{1,0:T(8,128)S(1)}, u32[]{:S(2)}, u32[]{:S(2)}) collective-permute-start(f32[32,3200]{1,0:T(8,128)S(1)} %get-tuple-element.36.c), channel_id=1, source_target_pairs={{0,64},{8,72},{16,80},{24,88},{32,96},{40,104},{48,112},{56,120},{... | collective-permute-start | bytes 1228808 | tf_op jit(solution)/shard_map/ppermute | solution.py:39
  23.8 8.2 %collective-permute-done.5.c_r = f32[32,3200]{1,0:T(8,128)S(1)} collective-permute-done((f32[32,3200]{1,0:T(8,128)S(1)}, f32[32,3200]{1,0:T(8,128)S(1)}, u32[]{:S(2)}, u32[]{:S(2)}) %collective-permute-start.5) | collective-permute-done | bytes 409632 | tf_op jit(solution)/shard_map/ppermute | solution.py:39
  32.0 2.5 %collective-permute-done.4.ab_r = f32[32,7040]{1,0:T(8,128)S(1)} collective-permute-done((f32[32,7040]{1,0:T(8,128)S(1)}, f32[32,7040]{1,0:T(8,128)S(1)}, u32[]{:S(2)}, u32[]{:S(2)}) %collective-permute-start.4) | collective-permute-done | bytes 901152 | tf_op jit(solution)/shard_map/ppermute | solution.py:39
  34.6 2.2 %collective-permute-start.7 = (f32[32,3712]{1,0:T(8,128)S(1)}, f32[32,3712]{1,0:T(8,128)S(1)}, u32[]{:S(2)}, u32[]{:S(2)}) collective-permute-start(f32[32,3712]{1,0:T(8,128)S(1)} %get-tuple-element.38.b), channel_id=1, source_target_pairs={{0,64},{8,72},{16,80},{24,88},{32,96},{40,104},{48,112},{56,120},{... | collective-permute-start | bytes 1425416 | tf_op jit(solution)/shard_map/ppermute | solution.py:39
  36.8 1.7 %collective-permute-start.8 = (f32[32,3200]{1,0:T(8,128)S(1)}, f32[32,3200]{1,0:T(8,128)S(1)}, u32[]{:S(2)}, u32[]{:S(2)}) collective-permute-start(f32[32,3200]{1,0:T(8,128)S(1)} %get-tuple-element.39.c), channel_id=1, source_target_pairs={{0,48},{8,24},{16,32},{24,8},{32,16},{40,56},{48,0},{56,40},{64,11... | collective-permute-start | bytes 1228808 | tf_op jit(solution)/shard_map/ppermute | solution.py:39
  38.5 8.9 %collective-permute-done.8.c_r = f32[32,3200]{1,0:T(8,128)S(1)} collective-permute-done((f32[32,3200]{1,0:T(8,128)S(1)}, f32[32,3200]{1,0:T(8,128)S(1)}, u32[]{:S(2)}, u32[]{:S(2)}) %collective-permute-start.8) | collective-permute-done | bytes 409632 | tf_op jit(solution)/shard_map/ppermute | solution.py:39
  47.3 0.3 collective-permute-done.6.a_r
  47.6 0.3 shard_map.55
  48.0 0.5 collective-permute-start.12
  48.4 0.3 collective-permute-start.13
  48.7 3.8 %collective-permute-start.9 = (f32[8,128]{1,0:T(8,128)S(1)}, f32[8,128]{1,0:T(8,128)S(1)}, u32[]{:S(2)}, u32[]{:S(2)}) collective-permute-start(f32[8,128]{1,0:T(8,128)S(1)} %get-tuple-element.41), channel_id=1, source_target_pairs={{0,65},{1,64},{2,67},{3,66},{4,69},{5,68},{6,71},{7,70},{8,73},{9,... | collective-permute-start | bytes 12296 | tf_op jit(solution)/shard_map/ppermute | solution.py:39
  52.5 1.6 %collective-permute-done.9 = f32[8,128]{1,0:T(8,128)S(1)} collective-permute-done((f32[8,128]{1,0:T(8,128)S(1)}, f32[8,128]{1,0:T(8,128)S(1)}, u32[]{:S(2)}, u32[]{:S(2)}) %collective-permute-start.9) | collective-permute-done | bytes 4128 | tf_op jit(solution)/shard_map/ppermute | solution.py:39
  54.1 1.6 %collective-permute-start.10 = (f32[8,128]{1,0:T(8,128)S(1)}, f32[8,128]{1,0:T(8,128)S(1)}, u32[]{:S(2)}, u32[]{:S(2)}) collective-permute-start(f32[8,128]{1,0:T(8,128)S(1)} %add.19), channel_id=1, source_target_pairs={{0,2},{1,3},{2,0},{3,1},{4,6},{5,7},{6,4},{7,5},{8,10},{9,11},{10,... | collective-permute-start | bytes 12296 | tf_op jit(solution)/shard_map/ppermute | solution.py:39
  55.6 2.0 %collective-permute-done.10 = f32[8,128]{1,0:T(8,128)S(1)} collective-permute-done((f32[8,128]{1,0:T(8,128)S(1)}, f32[8,128]{1,0:T(8,128)S(1)}, u32[]{:S(2)}, u32[]{:S(2)}) %collective-permute-start.10) | collective-permute-done | bytes 4128 | tf_op jit(solution)/shard_map/ppermute | solution.py:39
  57.7 3.0 %collective-permute-start.11 = (f32[8,128]{1,0:T(8,128)S(1)}, f32[8,128]{1,0:T(8,128)S(1)}, u32[]{:S(2)}, u32[]{:S(2)}) collective-permute-start(f32[8,128]{1,0:T(8,128)S(1)} %add.20), channel_id=1, source_target_pairs={{0,6},{1,7},{2,4},{3,5},{4,2},{5,3},{6,0},{7,1},{8,14},{9,15},{10,... | collective-permute-start | bytes 12296 | tf_op jit(solution)/shard_map/ppermute | solution.py:39
  60.7 1.8 %collective-permute-done.11 = f32[8,128]{1,0:T(8,128)S(1)} collective-permute-done((f32[8,128]{1,0:T(8,128)S(1)}, f32[8,128]{1,0:T(8,128)S(1)}, u32[]{:S(2)}, u32[]{:S(2)}) %collective-permute-start.11) | collective-permute-done | bytes 4128 | tf_op jit(solution)/shard_map/ppermute | solution.py:39
  62.6 0.6 collective-permute-start.17
  63.2 1.1 %collective-permute-start.14 = (f32[8,128]{1,0:T(8,128)S(1)}, f32[8,128]{1,0:T(8,128)S(1)}, u32[]{:S(2)}, u32[]{:S(2)}) collective-permute-start(f32[8,128]{1,0:T(8,128)S(1)} %add.21), channel_id=1, source_target_pairs={{0,80},{8,120},{16,64},{24,104},{32,112},{40,88},{48,96},{56,72},{... | collective-permute-start | bytes 12296 | tf_op jit(solution)/shard_map/ppermute | solution.py:39
  64.3 3.4 %collective-permute-done.14 = f32[8,128]{1,0:T(8,128)S(1)} collective-permute-done((f32[8,128]{1,0:T(8,128)S(1)}, f32[8,128]{1,0:T(8,128)S(1)}, u32[]{:S(2)}, u32[]{:S(2)}) %collective-permute-start.14) | collective-permute-done | bytes 4128 | tf_op jit(solution)/shard_map/ppermute | solution.py:39
  67.7 0.2 collective-permute-start.15
  67.9 1.0 %collective-permute-done.15 = f32[8,128]{1,0:T(8,128)S(1)} collective-permute-done((f32[8,128]{1,0:T(8,128)S(1)}, f32[8,128]{1,0:T(8,128)S(1)}, u32[]{:S(2)}, u32[]{:S(2)}) %collective-permute-start.15) | collective-permute-done | bytes 4128 | tf_op jit(solution)/shard_map/ppermute | solution.py:39
  68.9 5.6 %shard_map.56 = (f32[4,32,10240]{2,1,0:T(8,128)}, f32[4,32,10240]{2,1,0:T(8,128)}) custom-call(f32[8,128]{1,0:T(8,128)S(1)} %add.23.refs_0_, f32[32,10240]{1,0:T(8,128)S(1)} %get-tuple-element.55.refs_1_, f32[32,10240]{1,0:T(8,128)S(1)} %collective-permute-done.16.refs_2_, f32[32,10240]{1,0:T(8,128)S(1)} %constant_dynamic-update-slice_fusion.refs_3_, ...), custom_call_target="tpu_custom_call" | custom-call | flops 10485760 | bytes 26214400 | tf_op jit(solution)/shard_map/pallas_call | solution.py:247
  (27 shorter events, 0.5 us)
Async XLA Ops:
  2.2 3.1 %collective-permute-start = (f32[32,10240]{1,0:T(8,128)S(1)}, f32[32,10240]{1,0:T(8,128)S(1)}, u32[]{:S(2)}, u32[]{:S(2)}) collective-permute-start(f32[32,10240]{1,0:T(8,128)S(1)} %shard_map.51), channel_id=1, source_target_pairs={{0,8},{8,0},{16,24},{24,16},{32,40},{40,32},{48,56},{56,48},{64,72... | collective-permute-start | bytes 3932168 | tf_op jit(solution)/shard_map/ppermute | solution.py:39
  4.8 6.7 %collective-permute-start.1 = (f32[32,10240]{1,0:T(8,128)S(1)}, f32[32,10240]{1,0:T(8,128)S(1)}, u32[]{:S(2)}, u32[]{:S(2)}) collective-permute-start(f32[32,10240]{1,0:T(8,128)S(1)} %get-tuple-element.34), channel_id=1, source_target_pairs={{0,8},{8,0},{16,24},{24,16},{32,40},{40,32},{48,56},{56,48},{64,72... | collective-permute-start | bytes 3932168 | tf_op jit(solution)/shard_map/ppermute | solution.py:39
  5.6 14.1 %collective-permute-start.3 = (f32[32,6912]{1,0:T(8,128)S(1)}, f32[32,6912]{1,0:T(8,128)S(1)}, u32[]{:S(2)}, u32[]{:S(2)}) collective-permute-start(f32[32,6912]{1,0:T(8,128)S(1)} %slice.13), channel_id=1, source_target_pairs={{0,16},{8,56},{16,0},{24,40},{32,48},{40,24},{48,32},{56,8},{64,80... | collective-permute-start | bytes 2654216 | tf_op jit(solution)/shard_map/ppermute | solution.py:39
  7.3 12.4 %collective-permute-start.2 = (f32[32,3328]{1,0:T(8,128)S(1)}, f32[32,3328]{1,0:T(8,128)S(1)}, u32[]{:S(2)}, u32[]{:S(2)}) collective-permute-start(f32[32,3328]{1,0:T(8,128)S(1)} %slice.12), channel_id=1, source_target_pairs={{0,64},{8,72},{16,80},{24,88},{32,96},{40,104},{48,112},{56,120},{... | collective-permute-start | bytes 1277960 | tf_op jit(solution)/shard_map/ppermute | solution.py:39
  19.7 49.1 %slice-start = ((s8[5242880]{0:T(1024)(128)(4,1)}), s8[4194304]{0:T(1024)(128)(4,1)S(1)}, s32[]{:S(2)}) async-start(s8[5242880]{0:T(1024)(128)(4,1)} %bitcast.1), calls=%async_computation | async-start | bytes 8388608
  20.0 14.5 %collective-permute-start.4 = (f32[32,7040]{1,0:T(8,128)S(1)}, f32[32,7040]{1,0:T(8,128)S(1)}, u32[]{:S(2)}, u32[]{:S(2)}) collective-permute-start(f32[32,7040]{1,0:T(8,128)S(1)} %get-tuple-element.35.ab), channel_id=1, source_target_pairs={{0,48},{8,24},{16,32},{24,8},{32,16},{40,56},{48,0},{56,40},{64,11... | collective-permute-start | bytes 2703368 | tf_op jit(solution)/shard_map/ppermute | solution.py:39
  21.9 47.0 %slice-start.1 = ((s8[5242880]{0:T(1024)(128)(4,1)}), s8[1048576]{0:T(1024)(128)(4,1)S(1)}, s32[]{:S(2)}) async-start(s8[5242880]{0:T(1024)(128)(4,1)} %bitcast.1), calls=%async_computation.1 | async-start | bytes 2097152
  21.9 10.1 %collective-permute-start.5 = (f32[32,3200]{1,0:T(8,128)S(1)}, f32[32,3200]{1,0:T(8,128)S(1)}, u32[]{:S(2)}, u32[]{:S(2)}) collective-permute-start(f32[32,3200]{1,0:T(8,128)S(1)} %get-tuple-element.36.c), channel_id=1, source_target_pairs={{0,64},{8,72},{16,80},{24,88},{32,96},{40,104},{48,112},{56,120},{... | collective-permute-start | bytes 1228808 | tf_op jit(solution)/shard_map/ppermute | solution.py:39
  34.6 13.0 %collective-permute-start.7 = (f32[32,3712]{1,0:T(8,128)S(1)}, f32[32,3712]{1,0:T(8,128)S(1)}, u32[]{:S(2)}, u32[]{:S(2)}) collective-permute-start(f32[32,3712]{1,0:T(8,128)S(1)} %get-tuple-element.38.b), channel_id=1, source_target_pairs={{0,64},{8,72},{16,80},{24,88},{32,96},{40,104},{48,112},{56,120},{... | collective-permute-start | bytes 1425416 | tf_op jit(solution)/shard_map/ppermute | solution.py:39
  36.8 10.8 %collective-permute-start.6 = (f32[32,3328]{1,0:T(8,128)S(1)}, f32[32,3328]{1,0:T(8,128)S(1)}, u32[]{:S(2)}, u32[]{:S(2)}) collective-permute-start(f32[32,3328]{1,0:T(8,128)S(1)} %get-tuple-element.37.a), channel_id=1, source_target_pairs={{0,16},{8,56},{16,0},{24,40},{32,48},{40,24},{48,32},{56,8},{64,80... | collective-permute-start | bytes 1277960 | tf_op jit(solution)/shard_map/ppermute | solution.py:39
  36.8 10.5 %collective-permute-start.8 = (f32[32,3200]{1,0:T(8,128)S(1)}, f32[32,3200]{1,0:T(8,128)S(1)}, u32[]{:S(2)}, u32[]{:S(2)}) collective-permute-start(f32[32,3200]{1,0:T(8,128)S(1)} %get-tuple-element.39.c), channel_id=1, source_target_pairs={{0,48},{8,24},{16,32},{24,8},{32,16},{40,56},{48,0},{56,40},{64,11... | collective-permute-start | bytes 1228808 | tf_op jit(solution)/shard_map/ppermute | solution.py:39
  48.0 14.5 %collective-permute-start.12 = (f32[32,3328]{1,0:T(8,128)S(1)}, f32[32,3328]{1,0:T(8,128)S(1)}, u32[]{:S(2)}, u32[]{:S(2)}) collective-permute-start(f32[32,3328]{1,0:T(8,128)S(1)} %slice.11), channel_id=1, source_target_pairs={{0,64},{8,72},{16,80},{24,88},{32,96},{40,104},{48,112},{56,120},{... | collective-permute-start | bytes 1277960 | tf_op jit(solution)/shard_map/ppermute | solution.py:39
  48.4 14.1 %collective-permute-start.13 = (f32[32,6912]{1,0:T(8,128)S(1)}, f32[32,6912]{1,0:T(8,128)S(1)}, u32[]{:S(2)}, u32[]{:S(2)}) collective-permute-start(f32[32,6912]{1,0:T(8,128)S(1)} %get-tuple-element.49), channel_id=1, source_target_pairs={{0,16},{8,56},{16,0},{24,40},{32,48},{40,24},{48,32},{56,8},{64,80... | collective-permute-start | bytes 2654216 | tf_op jit(solution)/shard_map/ppermute | solution.py:39
  48.7 5.4 %collective-permute-start.9 = (f32[8,128]{1,0:T(8,128)S(1)}, f32[8,128]{1,0:T(8,128)S(1)}, u32[]{:S(2)}, u32[]{:S(2)}) collective-permute-start(f32[8,128]{1,0:T(8,128)S(1)} %get-tuple-element.41), channel_id=1, source_target_pairs={{0,65},{1,64},{2,67},{3,66},{4,69},{5,68},{6,71},{7,70},{8,73},{9,... | collective-permute-start | bytes 12296 | tf_op jit(solution)/shard_map/ppermute | solution.py:39
  54.1 3.6 %collective-permute-start.10 = (f32[8,128]{1,0:T(8,128)S(1)}, f32[8,128]{1,0:T(8,128)S(1)}, u32[]{:S(2)}, u32[]{:S(2)}) collective-permute-start(f32[8,128]{1,0:T(8,128)S(1)} %add.19), channel_id=1, source_target_pairs={{0,2},{1,3},{2,0},{3,1},{4,6},{5,7},{6,4},{7,5},{8,10},{9,11},{10,... | collective-permute-start | bytes 12296 | tf_op jit(solution)/shard_map/ppermute | solution.py:39
  57.7 4.8 %collective-permute-start.11 = (f32[8,128]{1,0:T(8,128)S(1)}, f32[8,128]{1,0:T(8,128)S(1)}, u32[]{:S(2)}, u32[]{:S(2)}) collective-permute-start(f32[8,128]{1,0:T(8,128)S(1)} %add.20), channel_id=1, source_target_pairs={{0,6},{1,7},{2,4},{3,5},{4,2},{5,3},{6,0},{7,1},{8,14},{9,15},{10,... | collective-permute-start | bytes 12296 | tf_op jit(solution)/shard_map/ppermute | solution.py:39
  62.5 6.4 %collective-permute-start.16 = (f32[32,10240]{1,0:T(8,128)S(1)}, f32[32,10240]{1,0:T(8,128)S(1)}, u32[]{:S(2)}, u32[]{:S(2)}) collective-permute-start(f32[32,10240]{1,0:T(8,128)S(1)} %get-tuple-element.55.refs_1_), channel_id=1, source_target_pairs={{0,8},{8,0},{16,24},{24,16},{32,40},{40,32},{48,56},{56,48},{64,72... | collective-permute-start | bytes 3932168 | tf_op jit(solution)/shard_map/ppermute | solution.py:39
  62.6 6.3 %collective-permute-start.17 = (f32[32,10240]{1,0:T(8,128)S(1)}, f32[32,10240]{1,0:T(8,128)S(1)}, u32[]{:S(2)}, u32[]{:S(2)}) collective-permute-start(f32[32,10240]{1,0:T(8,128)S(1)} %constant_dynamic-update-slice_fusion.refs_3_), channel_id=1, source_target_pairs={{0,8},{8,0},{16,24},{24,16},{32,40},{40,32},{48,56},{56,48},{64,72... | collective-permute-start | bytes 3932168 | tf_op jit(solution)/shard_map/ppermute | solution.py:39
  63.2 4.5 %collective-permute-start.14 = (f32[8,128]{1,0:T(8,128)S(1)}, f32[8,128]{1,0:T(8,128)S(1)}, u32[]{:S(2)}, u32[]{:S(2)}) collective-permute-start(f32[8,128]{1,0:T(8,128)S(1)} %add.21), channel_id=1, source_target_pairs={{0,80},{8,120},{16,64},{24,104},{32,112},{40,88},{48,96},{56,72},{... | collective-permute-start | bytes 12296 | tf_op jit(solution)/shard_map/ppermute | solution.py:39
  67.7 1.2 %collective-permute-start.15 = (f32[8,128]{1,0:T(8,128)S(1)}, f32[8,128]{1,0:T(8,128)S(1)}, u32[]{:S(2)}, u32[]{:S(2)}) collective-permute-start(f32[8,128]{1,0:T(8,128)S(1)} %add.22), channel_id=1, source_target_pairs={{0,8},{8,0},{16,24},{24,16},{32,40},{40,32},{48,56},{56,48},{64,72... | collective-permute-start | bytes 12296 | tf_op jit(solution)/shard_map/ppermute | solution.py:39
